TPU v7x, 32 devices: a whole 2x2x4 slice. The times are simulated.
32 devices in a mesh: len: 4 (over x, core), brick: 8 (over z, y).
Axes of the slice: x: 2, y: 2, z: 4, core: 2. Of those that a mesh axis runs over, the one named last changes fastest.
Arguments:
- forces: float32 [3, 32, 128, 128], P(None, 'len', 'brick'), may hold values from -6 to 6
- modulus: float32 [32, 128, 128], P('len', 'brick'), may hold values from 1 to 10
- occupancy: int32 [32, 128, 128], P('len', 'brick'), may hold values 0 or 1
- bonded: int32 [32, 128, 128], P('len', 'brick'), may hold values 0 or 1
Outputs:
- solution: float32 [3, 32, 128, 128], P(None, 'len', 'brick')
All inputs are finite; a program needn't handle non-finite values. No bound on the sum of `occupancy` or of `bonded` on one device may be relied on, other than what follows from the above.
Results may differ from a plain program's by a relative error of at most 0.0001.
Values sent between devices are 32-bit elements; how exact they have to be, the bound alone decides.
No kernel may reach another device: no remote copies, remote signals or barrier semaphores. Data moves between devices by JAX's collectives and lax.ppermute only.
A program may use at most 64 MiB of HBM per device.

v0:
```python
import jax
import jax.numpy as jnp
from jax import lax
from jax.sharding import PartitionSpec as P

LEVELS = 3
POST_SWEEPS = 2
COARSE_SWEEPS = 4


DAMPING = 0.6
COUPLING = 0.2
MASS_TERM = 0.1
PENALTY = 20.0
COARSE_SCALE = 0.25


def extended_2(block, sides, width):
    for axis, dim in sides:
        count = lax.axis_size(axis)
        forward = [(i, i + 1) for i in range(count - 1)]
        backward = [(target, source) for source, target in forward]
        low = lax.ppermute(
            lax.slice_in_dim(block, block.shape[dim] - width, None, axis=dim), axis, forward
        )
        high = lax.ppermute(lax.slice_in_dim(block, 0, width, axis=dim), axis, backward)
        block = jnp.concatenate([low, block, high], axis=dim)
    return block


def smooth(extended):
    ndims = extended.ndim
    padded = jnp.pad(extended, [(0, 0)] * (ndims - 1) + [(1, 1)])
    depth = padded.shape[-1]
    total = extended + 0.5 * (
        lax.slice_in_dim(padded, 0, depth - 2, axis=ndims - 1)
        + lax.slice_in_dim(padded, 2, depth, axis=ndims - 1)
    )
    for axis_now in (ndims - 2, ndims - 3):
        extent = total.shape[axis_now]
        total = lax.slice_in_dim(total, 1, extent - 1, axis=axis_now) + 0.5 * (
            lax.slice_in_dim(total, 0, extent - 2, axis=axis_now)
            + lax.slice_in_dim(total, 2, extent, axis=axis_now)
        )
    return total


def weights_only(coeff_ext):
    centre = coeff_ext[1:-1, 1:-1, :]
    weight_total = 6.0 * centre + smooth(coeff_ext)
    return (centre, weight_total)


def stencil(field_ext, coeff_ext):
    centre, weight_total = weights_only(coeff_ext)
    field_mid = field_ext[:, 1:-1, 1:-1, :]
    product_ext = coeff_ext[None] * field_ext
    product_mid = product_ext[:, 1:-1, 1:-1, :]
    gathered_sum = centre * (smooth(field_ext) - field_mid) + smooth(product_ext) - product_mid
    return (centre, weight_total, gathered_sum)


def apply_operator(field_ext, coeff_ext, shift_term):
    centre, weight_total, gathered_sum = stencil(field_ext, coeff_ext)
    field_mid = field_ext[:, 1:-1, 1:-1, :]
    return (
        (weight_total + shift_term) * field_mid
        - gathered_sum
        + COUPLING * centre * jnp.sum(field_mid, axis=0)
    )


def jacobi_step(field_ext, coeff_ext, shift_term, source, extra):
    centre, weight_total, gathered_sum = stencil(field_ext, coeff_ext)
    field_mid = field_ext[:, 1:-1, 1:-1, :]
    applied = (
        (weight_total + shift_term) * field_mid
        - gathered_sum
        + COUPLING * centre * jnp.sum(field_mid, axis=0)
    )
    return field_mid + DAMPING * (source - applied) / (
        weight_total + shift_term + COUPLING * centre + extra
    )


def first_step(coeff_ext, shift_term, source):
    centre, weight_total = weights_only(coeff_ext)
    return DAMPING * source / (weight_total + shift_term + COUPLING * centre)


def restrict_field(values):
    shaped = values.reshape(
        values.shape[0], values.shape[1] // 2, 2, values.shape[2] // 2, 2, values.shape[3] // 2, 2
    )
    return jnp.mean(shaped, axis=(2, 4, 6))


def restrict_cells(values):
    return restrict_field(values[None])[0]


def prolong(values):
    return jnp.repeat(jnp.repeat(jnp.repeat(values, 2, axis=1), 2, axis=2), 2, axis=3)


def grow_field(values):
    return extended_2(values, (("len", 1), ("brick", 2)), 1)


def grow_coeff(values):
    return extended_2(values, (("len", 0), ("brick", 1)), 1)


def body(forces, modulus, occupancy, bonded):
    coeffs = [modulus * occupancy.astype(jnp.float32)]
    shifts = [MASS_TERM + PENALTY * bonded.astype(jnp.float32)]
    for tier_index in range(LEVELS):
        coeffs.append(COARSE_SCALE * restrict_cells(coeffs[-1]))
        shifts.append(restrict_cells(shifts[-1]))
    first_coeff = grow_coeff(coeffs[0])
    last_tier = LEVELS
    coeff_exts = [first_coeff] + [
        grow_coeff(coeffs[tier_index]) for tier_index in range(1, last_tier)
    ]

    def coarsest_solve(source):
        coeff_ext = grow_coeff(coeffs[LEVELS])
        shift_term = shifts[LEVELS]
        iterate = first_step(coeff_ext, shift_term, source)
        for repeat_idx in range(COARSE_SWEEPS - 1):
            iterate = jacobi_step(grow_field(iterate), coeff_ext, shift_term, source, 0.0)
        return iterate

    def multigrid_pass(tier_index, source):
        coeff_ext = coeff_exts[tier_index]
        shift_term = shifts[tier_index]
        iterate = first_step(coeff_ext, shift_term, source)
        iterate = jacobi_step(grow_field(iterate), coeff_ext, shift_term, source, 0.0)
        residual = source - apply_operator(grow_field(iterate), coeff_ext, shift_term)
        coarse_source = restrict_field(residual)
        if tier_index + 1 == LEVELS:
            correction = coarsest_solve(coarse_source)
        else:
            correction = multigrid_pass(tier_index + 1, coarse_source)
        iterate = iterate + prolong(correction)
        for repeat_idx in range(POST_SWEEPS):
            iterate = jacobi_step(grow_field(iterate), coeff_ext, shift_term, source, 0.0)
        return iterate

    return multigrid_pass(0, forces)


def solution(mesh):
    in_specs = (
        P(None, "len", "brick", None),
        P("len", "brick", None),
        P("len", "brick", None),
        P("len", "brick", None),
    )
    out_specs = P(None, "len", "brick", None)
    return jax.shard_map(body, mesh=mesh, in_specs=in_specs, out_specs=out_specs, check_vma=False)
```

profile of v0, /device:TPU:26, one launch (start us, length us, event | category | flops | bytes accessed | tf_op | source)
XLA Modules:
  0.0 334.9 jit_solution(12039377355376766522)
XLA Ops:
  0.9 5.6 %reshape_broadcast_in_dim.8 = f32[4,2,8,2,64,2]{5,4,3,2,1,0:T(8,128)} reshape(f32[8,16,128]{2,1,0:T(8,128)S(1)} %convert_multiply_fusion) | data formatting | bytes 131072 | tf_op jit(solution)/shard_map/reshape;broadcast_in_dim | solution.py:92
  19.2 3.3 collective-permute-start.27
  33.1 4.2 %collective-permute-start.15 = (f32[6,1,64]{2,1,0:T(1,128)S(1)}, f32[6,1,64]{2,1,0:T(1,128)S(1)}, u32[]{:S(2)}, u32[]{:S(2)}) collective-permute-start(f32[6,1,64]{2,1,0:T(1,128)S(1)} %get-tuple-element.111), channel_id=1, source_target_pairs={{1,0},{2,1},{3,2},{4,3},{5,4},{6,5},{7,6},{9,8},{10,9},{11,10},{12... | collective-permute-start | bytes 4616 | tf_op jit(solution)/shard_map/ppermute | solution.py:26
  39.3 4.4 %collective-permute-done.14 = f32[6,1,64]{2,1,0:T(1,128)S(1)} collective-permute-done((f32[6,1,64]{2,1,0:T(1,128)S(1)}, f32[6,1,64]{2,1,0:T(1,128)S(1)}, u32[]{:S(2)}, u32[]{:S(2)}) %collective-permute-start.14) | collective-permute-done | bytes 1568 | tf_op jit(solution)/shard_map/ppermute | solution.py:23
  45.8 3.9 %collective-permute-start.2 = (f32[10,1,128]{2,1,0:T(1,128)S(1)}, f32[10,1,128]{2,1,0:T(1,128)S(1)}, u32[]{:S(2)}, u32[]{:S(2)}) collective-permute-start(f32[10,1,128]{2,1,0:T(1,128)S(1)} %get-tuple-element.71), channel_id=1, source_target_pairs={{0,1},{1,2},{2,3},{3,4},{4,5},{5,6},{6,7},{8,9},{9,10},{10,11},{11... | collective-permute-start | bytes 15368 | tf_op jit(solution)/shard_map/ppermute | solution.py:23
  52.5 5.6 %reshape_broadcast_in_dim.9 = f32[4,2,8,2,64,2]{5,4,3,2,1,0:T(8,128)} reshape(f32[8,16,128]{2,1,0:T(8,128)S(1)} %get-tuple-element.83) | data formatting | bytes 131072 | tf_op jit(solution)/shard_map/reshape;broadcast_in_dim | solution.py:92
  80.1 3.5 %collective-permute-done.6 = f32[3,10,1,128]{3,2,1,0:T(1,128)S(1)} collective-permute-done((f32[3,10,1,128]{3,2,1,0:T(1,128)S(1)}, f32[3,10,1,128]{3,2,1,0:T(1,128)S(1)}, u32[]{:S(2)}, u32[]{:S(2)}) %collective-permute-start.6) | collective-permute-done | bytes 15392 | tf_op jit(solution)/shard_map/ppermute | solution.py:23
  90.8 3.9 %collective-permute-start.38 = (f32[3,1,16]{2,1,0:T(1,128)S(1)}, f32[3,1,16]{2,1,0:T(1,128)S(1)}, u32[]{:S(2)}, u32[]{:S(2)}) collective-permute-start(f32[3,1,16]{2,1,0:T(1,128)S(1)} %get-tuple-element.141), channel_id=1, source_target_pairs={{0,1},{1,2},{2,3},{3,4},{4,5},{5,6},{6,7},{8,9},{9,10},{10,11},{11... | collective-permute-start | bytes 584 | tf_op jit(solution)/shard_map/ppermute | solution.py:23
  100.7 3.5 %collective-permute-done.10 = f32[3,10,1,128]{3,2,1,0:T(1,128)S(1)} collective-permute-done((f32[3,10,1,128]{3,2,1,0:T(1,128)S(1)}, f32[3,10,1,128]{3,2,1,0:T(1,128)S(1)}, u32[]{:S(2)}, u32[]{:S(2)}) %collective-permute-start.10) | collective-permute-done | bytes 15392 | tf_op jit(solution)/shard_map/ppermute | solution.py:23
  105.0 14.0 %reshape.274 = f32[3,4,2,8,2,64,2]{6,5,4,3,2,1,0:T(8,128)} reshape(f32[3,8,16,128]{3,2,1,0:T(8,128)S(1)} %fusion.68) | data formatting | bytes 393216 | tf_op jit(solution)/shard_map/reshape | solution.py:92
  119.0 5.5 %reduce_sum.239 = f32[3,4,8,64]{3,2,1,0:T(8,128)S(1)} reduce(f32[3,4,2,8,2,64,2]{6,5,4,3,2,1,0:T(8,128)} %reshape.274, f32[]{:T(128)} %constant.46.clone.1), dimensions={2,4,6}, to_apply=%region_2.0 | reduce | flops 43008 | bytes 221188 | tf_op jit(solution)/shard_map/reduce_sum | solution.py:95
  133.5 3.8 %collective-permute-start.18 = (f32[3,6,1,64]{3,2,1,0:T(1,128)S(1)}, f32[3,6,1,64]{3,2,1,0:T(1,128)S(1)}, u32[]{:S(2)}, u32[]{:S(2)}) collective-permute-start(f32[3,6,1,64]{3,2,1,0:T(1,128)S(1)} %get-tuple-element.79), channel_id=1, source_target_pairs={{0,1},{1,2},{2,3},{3,4},{4,5},{5,6},{6,7},{8,9},{9,10},{10,11},{11... | collective-permute-start | bytes 13832 | tf_op jit(solution)/shard_map/ppermute | solution.py:23
  153.5 3.2 collective-permute-done.22
  167.8 3.9 %collective-permute-start.30 = (f32[3,4,1,32]{3,2,1,0:T(1,128)S(1)}, f32[3,4,1,32]{3,2,1,0:T(1,128)S(1)}, u32[]{:S(2)}, u32[]{:S(2)}) collective-permute-start(f32[3,4,1,32]{3,2,1,0:T(1,128)S(1)} %get-tuple-element.108), channel_id=1, source_target_pairs={{0,1},{1,2},{2,3},{3,4},{4,5},{5,6},{6,7},{8,9},{9,10},{10,11},{11... | collective-permute-start | bytes 4616 | tf_op jit(solution)/shard_map/ppermute | solution.py:23
  183.4 3.9 %collective-permute-start.34 = (f32[3,4,1,32]{3,2,1,0:T(1,128)S(1)}, f32[3,4,1,32]{3,2,1,0:T(1,128)S(1)}, u32[]{:S(2)}, u32[]{:S(2)}) collective-permute-start(f32[3,4,1,32]{3,2,1,0:T(1,128)S(1)} %get-tuple-element.106), channel_id=1, source_target_pairs={{0,1},{1,2},{2,3},{3,4},{4,5},{5,6},{6,7},{8,9},{9,10},{10,11},{11... | collective-permute-start | bytes 4616 | tf_op jit(solution)/shard_map/ppermute | solution.py:23
  199.2 3.9 %collective-permute-start.42 = (f32[3,3,1,16]{3,2,0,1:T(1,128)S(1)}, f32[3,3,1,16]{3,2,0,1:T(1,128)S(1)}, u32[]{:S(2)}, u32[]{:S(2)}) collective-permute-start(f32[3,3,1,16]{3,2,0,1:T(1,128)S(1)} %get-tuple-element.133), channel_id=1, source_target_pairs={{0,1},{1,2},{2,3},{3,4},{4,5},{5,6},{6,7},{8,9},{9,10},{10,11},{11... | collective-permute-start | bytes 1736 | tf_op jit(solution)/shard_map/ppermute | solution.py:23
  214.6 3.9 %collective-permute-start.46 = (f32[3,3,1,16]{3,2,0,1:T(1,128)S(1)}, f32[3,3,1,16]{3,2,0,1:T(1,128)S(1)}, u32[]{:S(2)}, u32[]{:S(2)}) collective-permute-start(f32[3,3,1,16]{3,2,0,1:T(1,128)S(1)} %get-tuple-element.131), channel_id=1, source_target_pairs={{0,1},{1,2},{2,3},{3,4},{4,5},{5,6},{6,7},{8,9},{9,10},{10,11},{11... | collective-permute-start | bytes 1736 | tf_op jit(solution)/shard_map/ppermute | solution.py:23
  230.1 3.9 %collective-permute-start.50 = (f32[3,3,1,16]{3,2,0,1:T(1,128)S(1)}, f32[3,3,1,16]{3,2,0,1:T(1,128)S(1)}, u32[]{:S(2)}, u32[]{:S(2)}) collective-permute-start(f32[3,3,1,16]{3,2,0,1:T(1,128)S(1)} %get-tuple-element.129), channel_id=1, source_target_pairs={{0,1},{1,2},{2,3},{3,4},{4,5},{5,6},{6,7},{8,9},{9,10},{10,11},{11... | collective-permute-start | bytes 1736 | tf_op jit(solution)/shard_map/ppermute | solution.py:23
  245.9 3.9 %collective-permute-start.54 = (f32[3,4,1,32]{3,2,1,0:T(1,128)S(1)}, f32[3,4,1,32]{3,2,1,0:T(1,128)S(1)}, u32[]{:S(2)}, u32[]{:S(2)}) collective-permute-start(f32[3,4,1,32]{3,2,1,0:T(1,128)S(1)} %get-tuple-element.104), channel_id=1, source_target_pairs={{0,1},{1,2},{2,3},{3,4},{4,5},{5,6},{6,7},{8,9},{9,10},{10,11},{11... | collective-permute-start | bytes 4616 | tf_op jit(solution)/shard_map/ppermute | solution.py:23
  261.5 3.9 %collective-permute-start.58 = (f32[3,4,1,32]{3,2,1,0:T(1,128)S(1)}, f32[3,4,1,32]{3,2,1,0:T(1,128)S(1)}, u32[]{:S(2)}, u32[]{:S(2)}) collective-permute-start(f32[3,4,1,32]{3,2,1,0:T(1,128)S(1)} %get-tuple-element.102), channel_id=1, source_target_pairs={{0,1},{1,2},{2,3},{3,4},{4,5},{5,6},{6,7},{8,9},{9,10},{10,11},{11... | collective-permute-start | bytes 4616 | tf_op jit(solution)/shard_map/ppermute | solution.py:23
  277.6 3.9 %collective-permute-start.62 = (f32[3,6,1,64]{3,2,1,0:T(1,128)S(1)}, f32[3,6,1,64]{3,2,1,0:T(1,128)S(1)}, u32[]{:S(2)}, u32[]{:S(2)}) collective-permute-start(f32[3,6,1,64]{3,2,1,0:T(1,128)S(1)} %get-tuple-element.75), channel_id=1, source_target_pairs={{0,1},{1,2},{2,3},{3,4},{4,5},{5,6},{6,7},{8,9},{9,10},{10,11},{11... | collective-permute-start | bytes 13832 | tf_op jit(solution)/shard_map/ppermute | solution.py:23
  293.4 3.9 %collective-permute-start.66 = (f32[3,6,1,64]{3,2,1,0:T(1,128)S(1)}, f32[3,6,1,64]{3,2,1,0:T(1,128)S(1)}, u32[]{:S(2)}, u32[]{:S(2)}) collective-permute-start(f32[3,6,1,64]{3,2,1,0:T(1,128)S(1)} %get-tuple-element.73), channel_id=1, source_target_pairs={{0,1},{1,2},{2,3},{3,4},{4,5},{5,6},{6,7},{8,9},{9,10},{10,11},{11... | collective-permute-start | bytes 13832 | tf_op jit(solution)/shard_map/ppermute | solution.py:23
  310.4 3.9 %collective-permute-start.70 = (f32[3,10,1,128]{3,2,1,0:T(1,128)S(1)}, f32[3,10,1,128]{3,2,1,0:T(1,128)S(1)}, u32[]{:S(2)}, u32[]{:S(2)}) collective-permute-start(f32[3,10,1,128]{3,2,1,0:T(1,128)S(1)} %get-tuple-element.49), channel_id=1, source_target_pairs={{0,1},{1,2},{2,3},{3,4},{4,5},{5,6},{6,7},{8,9},{9,10},{10,11},{11... | collective-permute-start | bytes 46088 | tf_op jit(solution)/shard_map/ppermute | solution.py:23
  326.8 3.9 %collective-permute-start.74 = (f32[3,10,1,128]{3,2,1,0:T(1,128)S(1)}, f32[3,10,1,128]{3,2,1,0:T(1,128)S(1)}, u32[]{:S(2)}, u32[]{:S(2)}) collective-permute-start(f32[3,10,1,128]{3,2,1,0:T(1,128)S(1)} %get-tuple-element.47), channel_id=1, source_target_pairs={{0,1},{1,2},{2,3},{3,4},{4,5},{5,6},{6,7},{8,9},{9,10},{10,11},{11... | collective-permute-start | bytes 46088 | tf_op jit(solution)/shard_map/ppermute | solution.py:23
  (335 shorter events, 225.3 us)
Async XLA Ops:
  9.7 9.4 %collective-permute-start.25 = (f32[1,4,32]{2,1,0:T(4,128)S(1)}, f32[1,4,32]{2,1,0:T(4,128)S(1)}, u32[]{:S(2)}, u32[]{:S(2)}) collective-permute-start(f32[1,4,32]{2,1,0:T(4,128)S(1)} %get-tuple-element.140), channel_id=1, source_target_pairs={{8,0},{16,8},{24,16},{9,1},{17,9},{25,17},{10,2},{18,10},{26,18},{... | collective-permute-start | bytes 1544 | tf_op jit(solution)/shard_map/ppermute | solution.py:26
  11.7 7.5 %collective-permute-start.24 = (f32[1,4,32]{2,1,0:T(4,128)S(1)}, f32[1,4,32]{2,1,0:T(4,128)S(1)}, u32[]{:S(2)}, u32[]{:S(2)}) collective-permute-start(f32[1,4,32]{2,1,0:T(4,128)S(1)} %get-tuple-element.139), channel_id=1, source_target_pairs={{0,8},{8,16},{16,24},{1,9},{9,17},{17,25},{2,10},{10,18},{18,26},{... | collective-permute-start | bytes 1544 | tf_op jit(solution)/shard_map/ppermute | solution.py:23
  14.1 29.8 %collective-permute-start.1 = (f32[1,16,128]{2,1,0:T(8,128)S(1)}, f32[1,16,128]{2,1,0:T(8,128)S(1)}, u32[]{:S(2)}, u32[]{:S(2)}) collective-permute-start(f32[1,16,128]{2,1,0:T(8,128)S(1)} %get-tuple-element.85), channel_id=1, source_target_pairs={{8,0},{16,8},{24,16},{9,1},{17,9},{25,17},{10,2},{18,10},{26,18},{... | collective-permute-start | bytes 24584 | tf_op jit(solution)/shard_map/ppermute | solution.py:26
  17.3 26.6 %collective-permute-start = (f32[1,16,128]{2,1,0:T(8,128)S(1)}, f32[1,16,128]{2,1,0:T(8,128)S(1)}, u32[]{:S(2)}, u32[]{:S(2)}) collective-permute-start(f32[1,16,128]{2,1,0:T(8,128)S(1)} %get-tuple-element.84), channel_id=1, source_target_pairs={{0,8},{8,16},{16,24},{1,9},{9,17},{17,25},{2,10},{10,18},{18,26},{... | collective-permute-start | bytes 24584 | tf_op jit(solution)/shard_map/ppermute | solution.py:23
  19.2 9.0 %collective-permute-start.27 = (f32[4,1,32]{2,1,0:T(1,128)S(1)}, f32[4,1,32]{2,1,0:T(1,128)S(1)}, u32[]{:S(2)}, u32[]{:S(2)}) collective-permute-start(f32[4,1,32]{2,1,0:T(1,128)S(1)} %get-tuple-element.136), channel_id=1, source_target_pairs={{1,0},{2,1},{3,2},{4,3},{5,4},{6,5},{7,6},{9,8},{10,9},{11,10},{12... | collective-permute-start | bytes 1544 | tf_op jit(solution)/shard_map/ppermute | solution.py:26
  22.5 7.6 %collective-permute-start.26 = (f32[4,1,32]{2,1,0:T(1,128)S(1)}, f32[4,1,32]{2,1,0:T(1,128)S(1)}, u32[]{:S(2)}, u32[]{:S(2)}) collective-permute-start(f32[4,1,32]{2,1,0:T(1,128)S(1)} %get-tuple-element.135), channel_id=1, source_target_pairs={{0,1},{1,2},{2,3},{3,4},{4,5},{5,6},{6,7},{8,9},{9,10},{10,11},{11... | collective-permute-start | bytes 1544 | tf_op jit(solution)/shard_map/ppermute | solution.py:23
  61.5 18.6 %collective-permute-start.37 = (f32[1,2,16]{2,1,0:T(2,128)S(1)}, f32[1,2,16]{2,1,0:T(2,128)S(1)}, u32[]{:S(2)}, u32[]{:S(2)}) collective-permute-start(f32[1,2,16]{2,1,0:T(2,128)S(1)} %fusion.285), channel_id=1, source_target_pairs={{8,0},{16,8},{24,16},{9,1},{17,9},{25,17},{10,2},{18,10},{26,18},{... | collective-permute-start | bytes 392 | tf_op jit(solution)/shard_map/ppermute | solution.py:26
  63.4 16.7 %collective-permute-start.36 = (f32[1,2,16]{2,1,0:T(2,128)S(1)}, f32[1,2,16]{2,1,0:T(2,128)S(1)}, u32[]{:S(2)}, u32[]{:S(2)}) collective-permute-start(f32[1,2,16]{2,1,0:T(2,128)S(1)} %fusion.285), channel_id=1, source_target_pairs={{0,8},{8,16},{16,24},{1,9},{9,17},{17,25},{2,10},{10,18},{18,26},{... | collective-permute-start | bytes 392 | tf_op jit(solution)/shard_map/ppermute | solution.py:23
  77.1 6.5 %collective-permute-start.6 = (f32[3,10,1,128]{3,2,1,0:T(1,128)S(1)}, f32[3,10,1,128]{3,2,1,0:T(1,128)S(1)}, u32[]{:S(2)}, u32[]{:S(2)}) collective-permute-start(f32[3,10,1,128]{3,2,1,0:T(1,128)S(1)} %get-tuple-element.53), channel_id=1, source_target_pairs={{0,1},{1,2},{2,3},{3,4},{4,5},{5,6},{6,7},{8,9},{9,10},{10,11},{11... | collective-permute-start | bytes 46088 | tf_op jit(solution)/shard_map/ppermute | solution.py:23
  84.5 10.2 %collective-permute-start.9 = (f32[3,1,16,128]{3,2,1,0:T(8,128)S(1)}, f32[3,1,16,128]{3,2,1,0:T(8,128)S(1)}, u32[]{:S(2)}, u32[]{:S(2)}) collective-permute-start(f32[3,1,16,128]{3,2,1,0:T(8,128)S(1)} %get-tuple-element.60), channel_id=1, source_target_pairs={{8,0},{16,8},{24,16},{9,1},{17,9},{25,17},{10,2},{18,10},{26,18},{... | collective-permute-start | bytes 73736 | tf_op jit(solution)/shard_map/ppermute | solution.py:26
  86.4 8.3 %collective-permute-start.8 = (f32[3,1,16,128]{3,2,1,0:T(8,128)S(1)}, f32[3,1,16,128]{3,2,1,0:T(8,128)S(1)}, u32[]{:S(2)}, u32[]{:S(2)}) collective-permute-start(f32[3,1,16,128]{3,2,1,0:T(8,128)S(1)} %get-tuple-element.59), channel_id=1, source_target_pairs={{0,8},{8,16},{16,24},{1,9},{9,17},{17,25},{2,10},{10,18},{18,26},{... | collective-permute-start | bytes 73736 | tf_op jit(solution)/shard_map/ppermute | solution.py:23
  88.9 40.0 %collective-permute-start.39 = (f32[3,1,16]{2,1,0:T(1,128)S(1)}, f32[3,1,16]{2,1,0:T(1,128)S(1)}, u32[]{:S(2)}, u32[]{:S(2)}) collective-permute-start(f32[3,1,16]{2,1,0:T(1,128)S(1)} %get-tuple-element.142), channel_id=1, source_target_pairs={{1,0},{2,1},{3,2},{4,3},{5,4},{6,5},{7,6},{9,8},{10,9},{11,10},{12... | collective-permute-start | bytes 584 | tf_op jit(solution)/shard_map/ppermute | solution.py:26
  90.8 38.1 %collective-permute-start.38 = (f32[3,1,16]{2,1,0:T(1,128)S(1)}, f32[3,1,16]{2,1,0:T(1,128)S(1)}, u32[]{:S(2)}, u32[]{:S(2)}) collective-permute-start(f32[3,1,16]{2,1,0:T(1,128)S(1)} %get-tuple-element.141), channel_id=1, source_target_pairs={{0,1},{1,2},{2,3},{3,4},{4,5},{5,6},{6,7},{8,9},{9,10},{10,11},{11... | collective-permute-start | bytes 584 | tf_op jit(solution)/shard_map/ppermute | solution.py:23
  97.6 6.5 %collective-permute-start.10 = (f32[3,10,1,128]{3,2,1,0:T(1,128)S(1)}, f32[3,10,1,128]{3,2,1,0:T(1,128)S(1)}, u32[]{:S(2)}, u32[]{:S(2)}) collective-permute-start(f32[3,10,1,128]{3,2,1,0:T(1,128)S(1)} %get-tuple-element.51), channel_id=1, source_target_pairs={{0,1},{1,2},{2,3},{3,4},{4,5},{5,6},{6,7},{8,9},{9,10},{10,11},{11... | collective-permute-start | bytes 46088 | tf_op jit(solution)/shard_map/ppermute | solution.py:23
  133.5 6.5 %collective-permute-start.18 = (f32[3,6,1,64]{3,2,1,0:T(1,128)S(1)}, f32[3,6,1,64]{3,2,1,0:T(1,128)S(1)}, u32[]{:S(2)}, u32[]{:S(2)}) collective-permute-start(f32[3,6,1,64]{3,2,1,0:T(1,128)S(1)} %get-tuple-element.79), channel_id=1, source_target_pairs={{0,1},{1,2},{2,3},{3,4},{4,5},{5,6},{6,7},{8,9},{9,10},{10,11},{11... | collective-permute-start | bytes 13832 | tf_op jit(solution)/shard_map/ppermute | solution.py:23
  150.3 6.5 %collective-permute-start.22 = (f32[3,6,1,64]{3,2,1,0:T(1,128)S(1)}, f32[3,6,1,64]{3,2,1,0:T(1,128)S(1)}, u32[]{:S(2)}, u32[]{:S(2)}) collective-permute-start(f32[3,6,1,64]{3,2,1,0:T(1,128)S(1)} %get-tuple-element.77), channel_id=1, source_target_pairs={{0,1},{1,2},{2,3},{3,4},{4,5},{5,6},{6,7},{8,9},{9,10},{10,11},{11... | collective-permute-start | bytes 13832 | tf_op jit(solution)/shard_map/ppermute | solution.py:23
  167.8 6.4 %collective-permute-start.30 = (f32[3,4,1,32]{3,2,1,0:T(1,128)S(1)}, f32[3,4,1,32]{3,2,1,0:T(1,128)S(1)}, u32[]{:S(2)}, u32[]{:S(2)}) collective-permute-start(f32[3,4,1,32]{3,2,1,0:T(1,128)S(1)} %get-tuple-element.108), channel_id=1, source_target_pairs={{0,1},{1,2},{2,3},{3,4},{4,5},{5,6},{6,7},{8,9},{9,10},{10,11},{11... | collective-permute-start | bytes 4616 | tf_op jit(solution)/shard_map/ppermute | solution.py:23
  183.4 6.4 %collective-permute-start.34 = (f32[3,4,1,32]{3,2,1,0:T(1,128)S(1)}, f32[3,4,1,32]{3,2,1,0:T(1,128)S(1)}, u32[]{:S(2)}, u32[]{:S(2)}) collective-permute-start(f32[3,4,1,32]{3,2,1,0:T(1,128)S(1)} %get-tuple-element.106), channel_id=1, source_target_pairs={{0,1},{1,2},{2,3},{3,4},{4,5},{5,6},{6,7},{8,9},{9,10},{10,11},{11... | collective-permute-start | bytes 4616 | tf_op jit(solution)/shard_map/ppermute | solution.py:23
  245.9 6.4 %collective-permute-start.54 = (f32[3,4,1,32]{3,2,1,0:T(1,128)S(1)}, f32[3,4,1,32]{3,2,1,0:T(1,128)S(1)}, u32[]{:S(2)}, u32[]{:S(2)}) collective-permute-start(f32[3,4,1,32]{3,2,1,0:T(1,128)S(1)} %get-tuple-element.104), channel_id=1, source_target_pairs={{0,1},{1,2},{2,3},{3,4},{4,5},{5,6},{6,7},{8,9},{9,10},{10,11},{11... | collective-permute-start | bytes 4616 | tf_op jit(solution)/shard_map/ppermute | solution.py:23
  261.5 6.4 %collective-permute-start.58 = (f32[3,4,1,32]{3,2,1,0:T(1,128)S(1)}, f32[3,4,1,32]{3,2,1,0:T(1,128)S(1)}, u32[]{:S(2)}, u32[]{:S(2)}) collective-permute-start(f32[3,4,1,32]{3,2,1,0:T(1,128)S(1)} %get-tuple-element.102), channel_id=1, source_target_pairs={{0,1},{1,2},{2,3},{3,4},{4,5},{5,6},{6,7},{8,9},{9,10},{10,11},{11... | collective-permute-start | bytes 4616 | tf_op jit(solution)/shard_map/ppermute | solution.py:23
  277.6 6.5 %collective-permute-start.62 = (f32[3,6,1,64]{3,2,1,0:T(1,128)S(1)}, f32[3,6,1,64]{3,2,1,0:T(1,128)S(1)}, u32[]{:S(2)}, u32[]{:S(2)}) collective-permute-start(f32[3,6,1,64]{3,2,1,0:T(1,128)S(1)} %get-tuple-element.75), channel_id=1, source_target_pairs={{0,1},{1,2},{2,3},{3,4},{4,5},{5,6},{6,7},{8,9},{9,10},{10,11},{11... | collective-permute-start | bytes 13832 | tf_op jit(solution)/shard_map/ppermute | solution.py:23
  293.4 6.5 %collective-permute-start.66 = (f32[3,6,1,64]{3,2,1,0:T(1,128)S(1)}, f32[3,6,1,64]{3,2,1,0:T(1,128)S(1)}, u32[]{:S(2)}, u32[]{:S(2)}) collective-permute-start(f32[3,6,1,64]{3,2,1,0:T(1,128)S(1)} %get-tuple-element.73), channel_id=1, source_target_pairs={{0,1},{1,2},{2,3},{3,4},{4,5},{5,6},{6,7},{8,9},{9,10},{10,11},{11... | collective-permute-start | bytes 13832 | tf_op jit(solution)/shard_map/ppermute | solution.py:23
  310.4 6.5 %collective-permute-start.70 = (f32[3,10,1,128]{3,2,1,0:T(1,128)S(1)}, f32[3,10,1,128]{3,2,1,0:T(1,128)S(1)}, u32[]{:S(2)}, u32[]{:S(2)}) collective-permute-start(f32[3,10,1,128]{3,2,1,0:T(1,128)S(1)} %get-tuple-element.49), channel_id=1, source_target_pairs={{0,1},{1,2},{2,3},{3,4},{4,5},{5,6},{6,7},{8,9},{9,10},{10,11},{11... | collective-permute-start | bytes 46088 | tf_op jit(solution)/shard_map/ppermute | solution.py:23
  326.8 6.5 %collective-permute-start.74 = (f32[3,10,1,128]{3,2,1,0:T(1,128)S(1)}, f32[3,10,1,128]{3,2,1,0:T(1,128)S(1)}, u32[]{:S(2)}, u32[]{:S(2)}) collective-permute-start(f32[3,10,1,128]{3,2,1,0:T(1,128)S(1)} %get-tuple-element.47), channel_id=1, source_target_pairs={{0,1},{1,2},{2,3},{3,4},{4,5},{5,6},{6,7},{8,9},{9,10},{10,11},{11... | collective-permute-start | bytes 46088 | tf_op jit(solution)/shard_map/ppermute | solution.py:23
  (54 other events, 333.7 us)
where the time goes:
time: 337 us; the launch traced here: 335 us
  starting transfers between devices  196 us (58%)
  waiting for transfers between devices  86.4 us (26%)
  local copies, waits for them, and re-layouts  29.7 us (9%)
  other arithmetic  21 us (6%)
    ppermute x38, starting transfers between devices, extended_2(): lax.ppermute(lax.slice_in_dim(block, block.shape[dim] - width, None, axis...  113 us
    ppermute x38, waiting for transfers between devices, extended_2(): lax.ppermute(lax.slice_in_dim(block, block.shape[dim] - width, None, axis...  86.3 us
    ppermute x38, starting transfers between devices, extended_2(): lax.ppermute(lax.slice_in_dim(block, 0, width, axis=dim), axis, backward)  83.2 us
    reshape x2, local copies, waits for them, and re-layouts, restrict_field(): values.reshape(values.shape[0], values.shape[1] // 2, 2, values.shape[2]...  15.6 us
    reduce_sum x10, other arithmetic, restrict_field(): return jnp.mean(shaped, axis=(2, 4, 6))  11.4 us
    another operation x2, local copies, waits for them, and re-layouts, restrict_field(): values.reshape(values.shape[0], values.shape[1] // 2, 2, values.shape[2]...  11.1 us
  transfers between devices with their start and end apart: 76, of which 32 were waited for; matrix products, arithmetic and copies ran while one was open for 6% of the time, Pallas kernels for 0%

commit v1 on v0

v1 whole, which is shorter than its diff:
```python
import functools

import jax
import jax.numpy as jnp
from jax import lax
from jax.experimental import pallas as pl
from jax.experimental.pallas import tpu as pltpu
from jax.sharding import PartitionSpec as P

DAMPING = 0.6
COUPLING = 0.2
MASS_TERM = 0.1
PENALTY = 20.0

HALO = 4
LANES = 128
F32 = jnp.float32
BOTH = ("len", "brick")


def lane_ids(shape):
    return lax.broadcasted_iota(jnp.int32, shape, len(shape) - 1)


def turn(x, by, axis):
    return pltpu.roll(x, by % x.shape[axis], axis)


class Lane:
    def __init__(self, rows, wide):
        ids = lane_ids((rows, LANES))
        self.wide = wide
        self.low = jnp.where(ids >= wide, 0.5, 0.0).astype(F32)
        self.high = jnp.where(ids < LANES - wide, 0.5, 0.0).astype(F32)
        self.first = (ids & wide) == 0

    def smooth(self, x):
        return x + self.low * turn(x, self.wide, 1) + self.high * turn(x, -self.wide, 1)

    def pair(self, x):
        return x + jnp.where(self.first, turn(x, -self.wide, 1), turn(x, self.wide, 1))


def smooth_rows(x):
    pair = x + turn(x, 1, 0)
    return pair + turn(pair, -1, 0)


def smooth_planes(get, p):
    below, here, above = get(p - 1), get(p), get(p + 1)
    total = here + here
    if below is not None:
        total = total + below
    if above is not None:
        total = total + above
    return total


def remember(get):
    seen = {}

    def cached(p):
        if p not in seen:
            seen[p] = get(p)
        return seen[p]

    return cached


def within(get, low, high):
    return lambda p: get(p) if low <= p < high else None


def gathered(field, quarter, planes, bounds, lane):
    low, high = bounds
    q_at = remember(within(lambda p: quarter[p], low, high))
    v_at = [remember(within(lambda p, k=k: field(k, p), low, high)) for k in range(3)]
    w_at = [
        remember(within(lambda p, k=k: q_at(p) * v_at[k](p), low, high)) for k in range(3)
    ]
    for p in planes:
        q = q_at(p)
        sums = []
        for k in range(3):
            x = smooth_rows(smooth_planes(v_at[k], p))
            y = smooth_rows(smooth_planes(w_at[k], p))
            sums.append(q * lane.smooth(x) + lane.smooth(y))
        yield p, [v_at[k](p) for k in range(3)], q, sums


def defects(field, quarter, weight, source, planes, bounds, lane):
    for p, v, q, sums in gathered(field, quarter, planes, bounds, lane):
        coupled = (4.0 * COUPLING) * q * (v[0] + v[1] + v[2])
        e = weight[p]
        yield p, v, [source[k, p] - e * v[k] + sums[k] - coupled for k in range(3)]


def sweep(field, quarter, weight, step, source, planes, bounds, lane, put):
    for p, v, r in defects(field, quarter, weight, source, planes, bounds, lane):
        s = step[p]
        for k in range(3):
            put(k, p, v[k] + s * r[k])


def stiffness_sum(quarter, planes, bounds, lane):
    q_at = remember(within(lambda p: quarter[p], *bounds))
    for p in planes:
        yield p, 24.0 * q_at(p) + lane.smooth(smooth_rows(smooth_planes(q_at, p)))


def step_of(inside, diagonal):
    return jnp.where(inside > 0.0, DAMPING / diagonal, 0.0)


def odd(axis):
    return lax.rem(lax.axis_index(axis), 2) == 1


def vmem(shape):
    return pltpu.VMEM(shape, F32)


def raw_field(forces, modulus, occupancy, bonded, k, p, rows):
    if k < 3:
        return forces[k, p, rows, :]
    if k == 3:
        return modulus[p, rows, :] * occupancy[p, rows, :].astype(F32)
    return MASS_TERM + PENALTY * bonded[p, rows, :].astype(F32)


def pack_planes(forces, modulus, occupancy, bonded, to_a, to_b):
    planes, rows = modulus.shape[0], modulus.shape[1]
    last = planes - HALO
    is_odd = lax.rem(lax.axis_index("len"), 2)
    start_a, start_b = (1 - is_odd) * last, is_odd * last
    for i in range(HALO):
        for k in range(5):
            to_a[k, i] = raw_field(
                forces, modulus, occupancy, bonded, k, start_a + i, slice(0, rows)
            )
            to_b[k, i] = raw_field(
                forces, modulus, occupancy, bonded, k, start_b + i, slice(0, rows)
            )


def extended_rows(own, from_a, from_b, planes, is_odd):
    def get(k, p, rows):
        if p < HALO:
            return jnp.where(is_odd, from_a[k, p, rows, :], from_b[k, p, rows, :])
        if p >= HALO + planes:
            i = p - HALO - planes
            return jnp.where(is_odd, from_b[k, i, rows, :], from_a[k, i, rows, :])
        return own(k, p - HALO, rows)

    return get


def pack_rows_from(get, planes, rows, to_c, to_d):
    is_odd = odd("brick")
    for k in range(5):
        for p in range(planes + 2 * HALO):
            first = get(k, p, slice(0, HALO))
            last = get(k, p, slice(rows - HALO, rows))
            to_c[k, p] = jnp.where(is_odd, first, last)
            to_d[k, p] = jnp.where(is_odd, last, first)


def pack_rows_fine(forces, modulus, occupancy, bonded, from_a, from_b, to_c, to_d):
    planes, rows = modulus.shape[0], modulus.shape[1]
    own = functools.partial(raw_field, forces, modulus, occupancy, bonded)
    pack_rows_from(
        extended_rows(own, from_a, from_b, planes, odd("len")), planes, rows, to_c, to_d
    )


def pack_rows_coarse(own, from_a, from_b, to_c, to_d):
    planes, rows = own.shape[1], own.shape[2]
    get = extended_rows(lambda k, p, r: own[k, p, r, :], from_a, from_b, planes, odd("len"))
    pack_rows_from(get, planes, rows, to_c, to_d)


def spread_rows(get, from_c, from_d, planes, rows, put):
    is_odd = odd("brick")
    for p in range(planes + 2 * HALO):
        for k in range(5):
            low = jnp.where(is_odd, from_c[k, p], from_d[k, p])
            high = jnp.where(is_odd, from_d[k, p], from_c[k, p])
            put(k, p, slice(0, HALO), low)
            put(k, p, slice(HALO, HALO + rows), get(k, p, slice(0, rows)))
            put(k, p, slice(HALO + rows, 2 * HALO + rows), high)


def fine_before(
    forces, modulus, occupancy, bonded, from_a, from_b, from_c, from_d,
    own_coarse, cells, v2, source, quarter, weight, step,
    shift, v1, work, coarse_q,
):
    planes, rows = modulus.shape[0], modulus.shape[1]
    ext_planes, ext_rows = planes + 2 * HALO, rows + 2 * HALO
    lane = Lane(ext_rows, 1)
    own = functools.partial(raw_field, forces, modulus, occupancy, bonded)

    def put(k, p, r, value):
        if k < 3:
            source[k, p, r, :] = value
        elif k == 3:
            quarter[p, r, :] = 0.25 * value
        else:
            shift[p, r, :] = value

    get = extended_rows(own, from_a, from_b, planes, odd("len"))
    spread_rows(get, from_c, from_d, planes, rows, put)

    bounds = (0, ext_planes)
    for p, w in stiffness_sum(quarter, range(1, ext_planes - 1), bounds, lane):
        q, s = quarter[p], shift[p]
        total = w + s
        weight[p] = total + 8.0 * q
        st = step_of(s, total + (4.0 * COUPLING) * q)
        step[p] = st
        for k in range(3):
            v1[k, p] = st * source[k, p]

    def put_v2(k, p, value):
        v2[k, p] = value

    sweep(
        lambda k, p: v1[k, p], quarter, weight, step, source,
        range(2, ext_planes - 2), bounds, lane, put_v2,
    )

    held = {}
    half = rows // 2
    for p, _, r in defects(
        lambda k, p: v2[k, p], quarter, weight, source,
        range(HALO, HALO + planes), bounds, lane,
    ):
        if p % 2 == 0:
            held = r
            continue
        i = (p - HALO) // 2
        for k in range(3):
            work[k, i] = lane.pair(held[k] + r[k])
    for i in range(planes // 2):
        for k in range(3):
            own_coarse[k, i] = 0.125 * (
                work[k, i, pl.ds(HALO, half, stride=2), :]
                + work[k, i, pl.ds(HALO + 1, half, stride=2), :]
            )

    reach = planes // 2 + 2
    for j in range(reach):
        p = 2 * j + 2
        work[0, j] = lane.pair(quarter[p] + quarter[p + 1])
        coarse_q[j, pl.ds(6, ext_rows // 2), :] = (0.25 * 0.125) * (
            work[0, j, pl.ds(0, ext_rows // 2, stride=2), :]
            + work[0, j, pl.ds(1, ext_rows // 2, stride=2), :]
        )
    for i in range(planes // 2):
        p = HALO + 2 * i
        work[1, i] = lane.pair(shift[p] + shift[p + 1])
    lane1 = Lane(half, 2)
    shift1, q1 = [], []
    for i in range(planes // 2):
        s = 0.125 * (
            work[1, i, pl.ds(HALO, half, stride=2), :]
            + work[1, i, pl.ds(HALO + 1, half, stride=2), :]
        )
        sides = smooth_planes(lambda j: coarse_q[j, pl.ds(7, half), :], i + 1)
        here = smooth_planes(lambda j: coarse_q[j, pl.ds(8, half), :], i + 1)
        others = smooth_planes(lambda j: coarse_q[j, pl.ds(9, half), :], i + 1)
        q = coarse_q[i + 1, pl.ds(8, half), :]
        w = 24.0 * q + lane1.smooth(sides + 2.0 * here + others)
        own_coarse[3, i] = q
        own_coarse[4, i] = w + s
        shift1.append(s)
        q1.append(q)

    quarter_rows = half // 2
    for i in range(planes // 4):
        work[2, 0, pl.ds(0, half), :] = lane1.pair(q1[2 * i] + q1[2 * i + 1])
        work[2, 1, pl.ds(0, half), :] = lane1.pair(shift1[2 * i] + shift1[2 * i + 1])
        cells[0, i] = (0.25 * 0.125) * (
            work[2, 0, pl.ds(0, quarter_rows, stride=2), :]
            + work[2, 0, pl.ds(1, quarter_rows, stride=2), :]
        )
        cells[1, i] = 0.125 * (
            work[2, 1, pl.ds(0, quarter_rows, stride=2), :]
            + work[2, 1, pl.ds(1, quarter_rows, stride=2), :]
        )


def middle_before(
    own, cells, from_a, from_b, from_c, from_d,
    to_all, v2, source, quarter, weight, step,
    v1, work,
):
    planes, rows = own.shape[1], own.shape[2]
    ext_planes, ext_rows = planes + 2 * HALO, rows + 2 * HALO
    lane = Lane(ext_rows, 2)

    def put(k, p, r, value):
        if k < 3:
            source[k, p, r, :] = value
        elif k == 3:
            quarter[p, r, :] = value
        else:
            weight[p, r, :] = value

    get = extended_rows(lambda k, p, r: own[k, p, r, :], from_a, from_b, planes, odd("len"))
    spread_rows(get, from_c, from_d, planes, rows, put)

    for p in range(ext_planes):
        q, total = quarter[p], weight[p]
        st = step_of(total, total + (4.0 * COUPLING) * q)
        step[p] = st
        weight[p] = total + 8.0 * q
        for k in range(3):
            v1[k, p] = st * source[k, p]

    def put_v2(k, p, value):
        v2[k, p] = value

    bounds = (0, ext_planes)
    sweep(
        lambda k, p: v1[k, p], quarter, weight, step, source,
        range(1, ext_planes - 1), bounds, lane, put_v2,
    )
    held = {}
    half = rows // 2
    ids = lane_ids((half, LANES))
    mine = (ids & 3) == lax.broadcasted_iota(jnp.int32, (half, LANES), 0)
    slots = 2 * to_all.shape[0] // (5 * (planes // 2))

    def send(row, value):
        packed = jnp.sum(jnp.where(mine, value, 0.0), axis=0, keepdims=True)
        for s in range(slots):
            at = s * (5 * (planes // 2)) + row
            to_all[at // 2, at % 2 : at % 2 + 1, :] = packed

    for p, _, r in defects(
        lambda k, p: v2[k, p], quarter, weight, source,
        range(HALO, HALO + planes), bounds, lane,
    ):
        if p % 2 == 0:
            held = r
            continue
        i = (p - HALO) // 2
        for k in range(3):
            work[k, i] = lane.pair(held[k] + r[k])
    for i in range(planes // 2):
        for k in range(3):
            send(
                k * (planes // 2) + i,
                0.125
                * (
                    work[k, i, pl.ds(HALO, half, stride=2), :]
                    + work[k, i, pl.ds(HALO + 1, half, stride=2), :]
                ),
            )
        for k in range(2):
            send((3 + k) * (planes // 2) + i, cells[k, i])


def prolong_rows(coarse, put):
    rows = coarse.shape[0]
    put(pl.ds(0, rows, stride=2), coarse)
    put(pl.ds(1, rows, stride=2), coarse)


def coarse_and_after(
    bricks_before,
    table, v2_mid, source_mid, quarter_mid, weight_mid, step_mid,
    v2_fine, source_fine, quarter_fine, weight_fine, step_fine,
    out,
    b2, q2, s2, e2, x2, u2, t2, b3, q3, s3, e3, x3, u3, grown, u_mid, x_mid, u_fine, x_fine,
):
    brick = lax.axis_index("brick")
    slab = lax.axis_index("len")
    slabs, bricks, lines = table.shape[0], table.shape[1], table.shape[2]
    depth = lines // 5
    rows_each = 4
    planes2 = slabs * depth
    all_rows = b2.shape[2]
    used = rows_each * bricks + 2 * HALO
    pad = HALO

    ids = lane_ids((bricks, LANES))
    first1, first2 = (ids & 1) == 0, (ids & 2) == 0
    zero_rows = jnp.zeros((pad, LANES), F32)
    zero_tail = jnp.zeros((all_rows - pad - rows_each * bricks, LANES), F32)
    for f in range(5):
        for i in range(planes2):
            target = b2.at[f, i] if f < 3 else (q2.at[i] if f == 3 else s2.at[i])
            target[pl.ds(0, pad), :] = zero_rows
            target[pl.ds(pad + rows_each * bricks, zero_tail.shape[0]), :] = zero_tail
            line = table[i // depth, :, f * depth + i % depth, :]
            for row in range(rows_each):
                x = jnp.where((ids & 3) == row, line, 0.0)
                x = x + jnp.where(first1, turn(x, -1, 1), turn(x, 1, 1))
                x = x + jnp.where(first2, turn(x, -2, 1), turn(x, 2, 1))
                target[pl.ds(pad + row, bricks, stride=rows_each), :] = x

    lane2 = Lane(all_rows, 4)
    bounds = (0, planes2)
    everything = range(planes2)
    for p, w in stiffness_sum(q2, everything, bounds, lane2):
        q, s = q2[p], s2[p]
        total = w + s
        e2[p] = total + 8.0 * q
        st = step_of(s, total + (4.0 * COUPLING) * q)
        x2[p] = st
        for k in range(3):
            u2[k, p] = st * b2[k, p]

    def put_t2(k, p, value):
        t2[k, p] = value

    sweep(lambda k, p: u2[k, p], q2, e2, x2, b2, everything, bounds, lane2, put_t2)

    rows3 = all_rows // 2
    planes3 = planes2 // 2
    held = {}
    for p, _, r in defects(lambda k, p: t2[k, p], q2, e2, b2, everything, bounds, lane2):
        if p % 2 == 0:
            held = r
            continue
        for k in range(3):
            u2[k, p] = lane2.pair(held[k] + r[k])
    for i in range(planes3):
        grown[0] = lane2.pair(q2[2 * i] + q2[2 * i + 1])
        grown[1] = lane2.pair(s2[2 * i] + s2[2 * i + 1])
        q3[i] = (0.25 * 0.125) * (
            grown[0, pl.ds(0, rows3, stride=2), :] + grown[0, pl.ds(1, rows3, stride=2), :]
        )
        s3[i] = 0.125 * (
            grown[1, pl.ds(0, rows3, stride=2), :] + grown[1, pl.ds(1, rows3, stride=2), :]
        )
        for k in range(3):
            b3[k, i] = 0.125 * (
                u2[k, 2 * i + 1, pl.ds(0, rows3, stride=2), :]
                + u2[k, 2 * i + 1, pl.ds(1, rows3, stride=2), :]
            )

    lane3 = Lane(rows3, 8)
    bounds3 = (0, planes3)
    for p, w in stiffness_sum(q3, range(planes3), bounds3, lane3):
        q, s = q3[p], s3[p]
        total = w + s
        e3[p] = total + 8.0 * q
        st = step_of(s, total + (4.0 * COUPLING) * q)
        x3[p] = st
        for k in range(3):
            u3[0, k, p] = st * b3[k, p]
    for turn_at in range(3):

        def put_u3(k, p, value, turn_at=turn_at):
            u3[(turn_at + 1) % 2, k, p] = value

        sweep(
            lambda k, p: u3[turn_at % 2, k, p], q3, e3, x3, b3,
            range(planes3), bounds3, lane3, put_u3,
        )

    for k in range(3):
        for i in range(planes3):
            coarse = u3[1, k, i]
            for half in range(2):
                u2[k, 2 * i, pl.ds(half, rows3, stride=2), :] = coarse
            both = u2[k, 2 * i]
            t2[k, 2 * i] = t2[k, 2 * i] + both
            t2[k, 2 * i + 1] = t2[k, 2 * i + 1] + both

    def put_u2(k, p, value):
        u2[k, p] = value

    zero_plane = jnp.zeros((all_rows, LANES), F32)
    sweep(lambda k, p: t2[k, p], q2, e2, x2, b2, everything, bounds, lane2, put_u2)

    def put_wide(k, p, value):
        t2[k, p + 2] = value

    for k in range(3):
        for p in (0, 1, planes2 + 2, planes2 + 3):
            t2[k, p] = zero_plane
    sweep(lambda k, p: u2[k, p], q2, e2, x2, b2, everything, bounds, lane2, put_wide)

    planes1 = v2_mid.shape[1]
    rows1 = v2_mid.shape[2]
    lane1 = Lane(rows1, 2)
    bounds1 = (0, planes1)
    row_at = rows_each * (brick - bricks_before(brick)) + pad - 2
    for k in range(3):
        for i in range(planes1 // 2):
            piece = t2[k, depth * slab + i, pl.ds(row_at, rows1 // 2), :]
            for half in range(2):
                x_mid[k, i, pl.ds(half, rows1 // 2, stride=2), :] = piece
            both = x_mid[k, i]
            for p in (2 * i, 2 * i + 1):
                if 1 <= p < planes1 - 1:
                    u_mid[k, p] = v2_mid[k, p] + both

    def put_mid(k, p, value):
        x_mid[k, p] = value

    sweep(
        lambda k, p: u_mid[k, p], quarter_mid, weight_mid, step_mid, source_mid,
        range(2, planes1 - 2), bounds1, lane1, put_mid,
    )

    def put_mid_last(k, p, value):
        u_mid[k, p] = value

    sweep(
        lambda k, p: x_mid[k, p], quarter_mid, weight_mid, step_mid, source_mid,
        range(3, planes1 - 3), bounds1, lane1, put_mid_last,
    )

    planes0, rows0 = v2_fine.shape[1], v2_fine.shape[2]
    lane0 = Lane(rows0, 1)
    bounds0 = (0, planes0)
    half_rows = rows0 // 2
    for k in range(3):
        for i in range(3, planes1 - 3):
            piece = u_mid[k, i, pl.ds(2, half_rows), :]
            p = 2 * i - HALO
            for half in range(2):
                x_fine[k, p, pl.ds(half, half_rows, stride=2), :] = piece
            both = x_fine[k, p]
            for at in (p, p + 1):
                u_fine[k, at] = v2_fine[k, at] + both

    def put_fine(k, p, value):
        x_fine[k, p] = value

    sweep(
        lambda k, p: u_fine[k, p], quarter_fine, weight_fine, step_fine, source_fine,
        range(3, planes0 - 3), bounds0, lane0, put_fine,
    )

    def put_out(k, p, value):
        out[k, p - HALO] = value[HALO : rows0 - HALO]

    sweep(
        lambda k, p: x_fine[k, p], quarter_fine, weight_fine, step_fine, source_fine,
        range(HALO, planes0 - HALO), bounds0, lane0, put_out,
    )


def call(kernel, outs, scratch=(), name=None):
    return pl.pallas_call(
        kernel,
        out_shape=[jax.ShapeDtypeStruct(shape, F32) for shape in outs],
        scratch_shapes=[vmem(shape) for shape in scratch],
        compiler_params=pltpu.CompilerParams(vmem_limit_bytes=48 * 1024 * 1024),
        name=name,
    )


def swap(x, axis, first):
    count = lax.axis_size(axis)
    pairs = []
    for i in range(first, count - 1, 2):
        pairs += [(i, i + 1), (i + 1, i)]
    return lax.ppermute(x, axis, pairs)


def body(forces, modulus, occupancy, bonded):
    planes, rows = modulus.shape[0], modulus.shape[1]
    slabs, bricks = lax.axis_size("len"), lax.axis_size("brick")
    raw = (forces, modulus, occupancy, bonded)
    ext, ext_rows = planes + 2 * HALO, rows + 2 * HALO
    half, half_rows = planes // 2, rows // 2
    mid, mid_rows = half + 2 * HALO, half_rows + 2 * HALO

    side = (5, HALO, rows, LANES)
    to_a, to_b = call(pack_planes, [side, side], name="pack_planes")(*raw)
    from_a, from_b = swap(to_a, "len", 0), swap(to_b, "len", 1)
    side = (5, ext, HALO, LANES)
    to_c, to_d = call(pack_rows_fine, [side, side], name="pack_rows_fine")(*raw, from_a, from_b)
    from_c, from_d = swap(to_c, "brick", 0), swap(to_d, "brick", 1)

    field, cell = (3, ext, ext_rows, LANES), (ext, ext_rows, LANES)
    own, cells, *fine = call(
        fine_before,
        [(5, half, half_rows, LANES), (2, half // 2, half_rows // 2, LANES)]
        + [field, field, cell, cell, cell],
        [cell, field, (3, half + 2, ext_rows, LANES), (half + 2, ext_rows, LANES)],
        name="fine_before",
    )(*raw, from_a, from_b, from_c, from_d)

    from_a, from_b = swap(own, "len", 0), swap(own, "len", 1)
    side = (5, mid, HALO, LANES)
    to_c, to_d = call(pack_rows_coarse, [side, side], name="pack_rows_coarse")(
        own, from_a, from_b
    )
    from_c, from_d = swap(to_c, "brick", 0), swap(to_d, "brick", 1)

    field1, cell1 = (3, mid, mid_rows, LANES), (mid, mid_rows, LANES)
    depth = half // 2
    lines = 5 * depth
    to_all, *middle = call(
        middle_before,
        [(slabs * bricks * lines // 2, 2, LANES)] + [field1, field1, cell1, cell1, cell1],
        [field1, (3, depth, mid_rows, LANES)],
        name="middle_before",
    )(own, cells, from_a, from_b, from_c, from_d)

    table = lax.all_to_all(to_all, BOTH, 0, 0, tiled=True)
    table = table.reshape(slabs, bricks, lines, LANES)
    window = bricks if bricks <= 8 else 16

    def first_brick(brick):
        return jnp.clip(brick - 4, 0, bricks - window)

    if window < bricks:
        table = lax.dynamic_slice_in_dim(
            table, first_brick(lax.axis_index("brick")), window, axis=1
        )
    planes2 = slabs * depth
    rows2 = -(-(4 * window + 2 * HALO) // 16) * 16
    f2, c2 = (3, planes2, rows2, LANES), (planes2, rows2, LANES)
    f3, c3 = (3, planes2 // 2, rows2 // 2, LANES), (planes2 // 2, rows2 // 2, LANES)
    (out,) = call(
        functools.partial(coarse_and_after, first_brick),
        [forces.shape],
        [f2, c2, c2, c2, c2, f2, (3, planes2 + 4, rows2, LANES)]
        + [f3, c3, c3, c3, c3, (2,) + f3]
        + [(2, rows2, LANES), field1, field1, field, field],
        name="coarse_and_after",
    )(table, *middle, *fine)
    return out


def solution(mesh):
    cells = P("len", "brick", None)
    forces = P(None, "len", "brick", None)
    return jax.shard_map(
        body, mesh=mesh, in_specs=(forces, cells, cells, cells), out_specs=forces, check_vma=False
    )
```

time: 337 us -> 67.3 us (0.20)
  the two profiles are of different devices: /device:TPU:26 before, /device:TPU:0 now
where the time goes in v1:
time: 67.3 us; the launch traced here: 67 us
  starting transfers between devices  19.6 us (29%)
  Pallas kernels  18.9 us (28%)
  blocking collectives  17.7 us (26%)
  waiting for transfers between devices  7.07 us (11%)
  local copies, waits for them, and re-layouts  3.56 us (5%)
    ppermute x8, starting transfers between devices, swap(): return lax.ppermute(x, axis, pairs)  19.6 us
    all_to_all x1, blocking collectives, body(): table = lax.all_to_all(to_all, BOTH, 0, 0, tiled=True)  17.7 us
    pallas_call x1, Pallas kernels, body(): call(functools.partial(coarse_and_after, first_brick), [forces.shape], [f...  16.4 us
    ppermute x8, waiting for transfers between devices, swap(): return lax.ppermute(x, axis, pairs)  7.07 us
    unnamed x8, local copies, waits for them, and re-layouts  3.44 us
    pallas_call x1, Pallas kernels, body(): call(fine_before, [(5, half, half_rows, LANES), (2, half // 2, half_rows...  1.64 us
  transfers between devices with their start and end apart: 8, of which 4 were waited for; matrix products, arithmetic and copies ran while one was open for 0% of the time, Pallas kernels for 0%

profile of v1, /device:TPU:0, one launch (start us, length us, event | category | flops | bytes accessed | tf_op | source)
XLA Modules:
  0.0 67.0 jit_solution(16854934261660766154)
XLA Ops:
  0.0 0.9 %copy-done = f32[3,8,16,128]{3,2,1,0:T(8,128)S(1)} copy-done((f32[3,8,16,128]{3,2,1,0:T(8,128)S(1)}, f32[3,8,16,128]{3,2,1,0:T(8,128)}, u32[]{:S(2)}) %copy-start) | copy-done | bytes 196632
  0.9 0.8 %copy-done.1 = f32[8,16,128]{2,1,0:T(8,128)S(1)} copy-done((f32[8,16,128]{2,1,0:T(8,128)S(1)}, f32[8,16,128]{2,1,0:T(8,128)}, u32[]{:S(2)}) %copy-start.1) | copy-done | bytes 65560
  1.8 0.8 %copy-done.2 = s32[8,16,128]{2,1,0:T(8,128)S(1)} copy-done((s32[8,16,128]{2,1,0:T(8,128)S(1)}, s32[8,16,128]{2,1,0:T(8,128)}, u32[]{:S(2)}) %copy-start.2) | copy-done | bytes 65560
  2.6 0.8 %copy-done.3 = s32[8,16,128]{2,1,0:T(8,128)S(1)} copy-done((s32[8,16,128]{2,1,0:T(8,128)S(1)}, s32[8,16,128]{2,1,0:T(8,128)}, u32[]{:S(2)}) %copy-start.3) | copy-done | bytes 65560
  3.5 0.5 collective-permute-start
  4.0 0.7 collective-permute-start.1
  4.7 0.4 collective-permute-done.from_a
  5.0 0.0 collective-permute-done.1.from_b
  5.0 0.1 pack_rows_fine.1
  5.1 2.9 %collective-permute-start.2 = (f32[5,16,4,128]{3,2,1,0:T(4,128)S(1)}, f32[5,16,4,128]{3,2,1,0:T(4,128)S(1)}, u32[]{:S(2)}, u32[]{:S(2)}) collective-permute-start(f32[5,16,4,128]{3,2,1,0:T(4,128)S(1)} %get-tuple-element.26), channel_id=1, source_target_pairs={{0,1},{1,0},{2,3},{3,2},{4,5},{5,4},{6,7},{7,6},{8,9},{9,8},{10,11... | collective-permute-start | bytes 491528 | tf_op jit(solution)/shard_map/ppermute | solution.py:565
  8.1 0.7 collective-permute-start.3
  8.7 2.6 %collective-permute-done.2.from_c = f32[5,16,4,128]{3,2,1,0:T(4,128)S(1)} collective-permute-done((f32[5,16,4,128]{3,2,1,0:T(4,128)S(1)}, f32[5,16,4,128]{3,2,1,0:T(4,128)S(1)}, u32[]{:S(2)}, u32[]{:S(2)}) %collective-permute-start.2) | collective-permute-done | bytes 163872 | tf_op jit(solution)/shard_map/ppermute | solution.py:565
  11.4 0.0 collective-permute-done.3.from_d
  11.4 1.6 %fine_before.1 = (f32[5,4,8,128]{3,2,1,0:T(8,128)S(1)}, f32[2,2,4,128]{3,2,1,0:T(4,128)S(1)}, f32[3,16,24,128]{3,2,1,0:T(8,128)S(1)}, f32[3,16,24,128]{3,2,1,0:T...) custom-call(f32[3,8,16,128]{3,2,1,0:T(8,128)S(1)} %copy-done, ...), custom_call_target="tpu_custom_call" | custom-call | tf_op jit(solution)/shard_map/fine_before/pallas_call | solution.py:584
  13.0 0.7 collective-permute-start.5
  13.7 8.7 %collective-permute-start.4 = (f32[5,4,8,128]{3,2,1,0:T(8,128)S(1)}, f32[5,4,8,128]{3,2,1,0:T(8,128)S(1)}, u32[]{:S(2)}, u32[]{:S(2)}) collective-permute-start(f32[5,4,8,128]{3,2,1,0:T(8,128)S(1)} %get-tuple-element.28.own), channel_id=1, source_target_pairs={{0,8},{8,0},{16,24},{24,16},{1,9},{9,1},{17,25},{25,17},{2,10},{10... | collective-permute-start | bytes 245768 | tf_op jit(solution)/shard_map/ppermute | solution.py:565
  22.3 0.9 %collective-permute-done.4.from_a = f32[5,4,8,128]{3,2,1,0:T(8,128)S(1)} collective-permute-done((f32[5,4,8,128]{3,2,1,0:T(8,128)S(1)}, f32[5,4,8,128]{3,2,1,0:T(8,128)S(1)}, u32[]{:S(2)}, u32[]{:S(2)}) %collective-permute-start.4) | collective-permute-done | bytes 81952 | tf_op jit(solution)/shard_map/ppermute | solution.py:565
  23.3 4.9 %collective-permute-start.6 = (f32[5,12,4,128]{3,2,1,0:T(4,128)S(1)}, f32[5,12,4,128]{3,2,1,0:T(4,128)S(1)}, u32[]{:S(2)}, u32[]{:S(2)}) collective-permute-start(f32[5,12,4,128]{3,2,1,0:T(4,128)S(1)} %get-tuple-element.30), channel_id=1, source_target_pairs={{0,1},{1,0},{2,3},{3,2},{4,5},{5,4},{6,7},{7,6},{8,9},{9,8},{10,11... | collective-permute-start | bytes 368648 | tf_op jit(solution)/shard_map/ppermute | solution.py:565
  28.2 0.7 collective-permute-start.7
  28.8 3.1 %collective-permute-done.6.from_c = f32[5,12,4,128]{3,2,1,0:T(4,128)S(1)} collective-permute-done((f32[5,12,4,128]{3,2,1,0:T(4,128)S(1)}, f32[5,12,4,128]{3,2,1,0:T(4,128)S(1)}, u32[]{:S(2)}, u32[]{:S(2)}) %collective-permute-start.6) | collective-permute-done | bytes 122912 | tf_op jit(solution)/shard_map/ppermute | solution.py:565
  32.0 0.7 %middle_before.1 = (f32[160,2,128]{2,1,0:T(2,128)S(1)}, f32[3,12,16,128]{3,2,1,0:T(8,128)S(1)}, f32[3,12,16,128]{3,2,1,0:T(8,128)S(1)}, f32[12,16,128]{2,1,0:T(8...) custom-call(f32[5,4,8,128]{3,2,1,0:T(8,128)S(1)} %get-tuple-element.28.own, ...), custom_call_target="tpu_custom_call" | custom-call | tf_op jit(solution)/shard_map/middle_before/pallas_call | solution.py:602
  32.7 17.7 %all_to_all.5 = f32[160,2,128]{2,1,0:T(2,128)S(1)} all-to-all(f32[160,2,128]{2,1,0:T(2,128)S(1)} %get-tuple-element.32), channel_id=1, replica_groups=mesh['len'=4,'brick'=8] {'len','brick'}, dimensions={0} | all-to-all | bytes 327680 | tf_op jit(solution)/shard_map/all_to_all | solution.py:609
  50.4 0.1 reshape.3.table
  50.5 16.4 %coarse_and_after.1 = f32[3,8,16,128]{3,2,1,0:T(8,128)} custom-call(f32[4,8,10,128]{3,2,1,0:T(8,128)S(1)} %reshape.3.table, f32[3,12,16,128]{3,2,1,0:T(8,128)S(1)} %get-tuple-element.33.v2_mid, f32[3,12,16,128]{3,2,1,0:T(8,128)S(1)} %get-tuple-element.34.source_mid, f32[12,16,128]{2,1,0:T(8,128)S(1)} %get-tuple-element.35.quarter_mid, ...), custom_call_target="tpu_custom_call" | custom-call | tf_op jit(solution)/shard_map/coarse_and_after/pallas_call | solution.py:624
  (8 shorter events, 0.1 us)
Async XLA Ops:
  0.0 0.9 %copy-start = (f32[3,8,16,128]{3,2,1,0:T(8,128)S(1)}, f32[3,8,16,128]{3,2,1,0:T(8,128)}, u32[]{:S(2)}) copy-start(f32[3,8,16,128]{3,2,1,0:T(8,128)} %forces.5) | copy-start | bytes 589828
  0.9 0.8 %copy-start.1 = (f32[8,16,128]{2,1,0:T(8,128)S(1)}, f32[8,16,128]{2,1,0:T(8,128)}, u32[]{:S(2)}) copy-start(f32[8,16,128]{2,1,0:T(8,128)} %modulus.5) | copy-start | bytes 196612
  1.8 0.8 %copy-start.2 = (s32[8,16,128]{2,1,0:T(8,128)S(1)}, s32[8,16,128]{2,1,0:T(8,128)}, u32[]{:S(2)}) copy-start(s32[8,16,128]{2,1,0:T(8,128)} %occupancy.5) | copy-start | bytes 196612
  2.6 0.8 %copy-start.3 = (s32[8,16,128]{2,1,0:T(8,128)S(1)}, s32[8,16,128]{2,1,0:T(8,128)}, u32[]{:S(2)}) copy-start(s32[8,16,128]{2,1,0:T(8,128)} %bonded.5) | copy-start | bytes 196612
  3.5 1.5 %collective-permute-start = (f32[5,4,16,128]{3,2,1,0:T(8,128)S(1)}, f32[5,4,16,128]{3,2,1,0:T(8,128)S(1)}, u32[]{:S(2)}, u32[]{:S(2)}) collective-permute-start(f32[5,4,16,128]{3,2,1,0:T(8,128)S(1)} %get-tuple-element.24), channel_id=1, source_target_pairs={{0,8},{8,0},{16,24},{24,16},{1,9},{9,1},{17,25},{25,17},{2,10},{10... | collective-permute-start | bytes 491528 | tf_op jit(solution)/shard_map/ppermute | solution.py:565
  4.0 1.0 %collective-permute-start.1 = (f32[5,4,16,128]{3,2,1,0:T(8,128)S(1)}, f32[5,4,16,128]{3,2,1,0:T(8,128)S(1)}, u32[]{:S(2)}, u32[]{:S(2)}) collective-permute-start(f32[5,4,16,128]{3,2,1,0:T(8,128)S(1)} %get-tuple-element.25), channel_id=1, source_target_pairs={{8,16},{16,8},{9,17},{17,9},{10,18},{18,10},{11,19},{19,11},{12,20... | collective-permute-start | bytes 491528 | tf_op jit(solution)/shard_map/ppermute | solution.py:565
  5.1 6.2 %collective-permute-start.2 = (f32[5,16,4,128]{3,2,1,0:T(4,128)S(1)}, f32[5,16,4,128]{3,2,1,0:T(4,128)S(1)}, u32[]{:S(2)}, u32[]{:S(2)}) collective-permute-start(f32[5,16,4,128]{3,2,1,0:T(4,128)S(1)} %get-tuple-element.26), channel_id=1, source_target_pairs={{0,1},{1,0},{2,3},{3,2},{4,5},{5,4},{6,7},{7,6},{8,9},{9,8},{10,11... | collective-permute-start | bytes 491528 | tf_op jit(solution)/shard_map/ppermute | solution.py:565
  8.1 3.3 %collective-permute-start.3 = (f32[5,16,4,128]{3,2,1,0:T(4,128)S(1)}, f32[5,16,4,128]{3,2,1,0:T(4,128)S(1)}, u32[]{:S(2)}, u32[]{:S(2)}) collective-permute-start(f32[5,16,4,128]{3,2,1,0:T(4,128)S(1)} %get-tuple-element.27), channel_id=1, source_target_pairs={{1,2},{2,1},{3,4},{4,3},{5,6},{6,5},{9,10},{10,9},{11,12},{12,11},... | collective-permute-start | bytes 491528 | tf_op jit(solution)/shard_map/ppermute | solution.py:565
  13.0 9.3 %collective-permute-start.5 = (f32[5,4,8,128]{3,2,1,0:T(8,128)S(1)}, f32[5,4,8,128]{3,2,1,0:T(8,128)S(1)}, u32[]{:S(2)}, u32[]{:S(2)}) collective-permute-start(f32[5,4,8,128]{3,2,1,0:T(8,128)S(1)} %get-tuple-element.28.own), channel_id=1, source_target_pairs={{8,16},{16,8},{9,17},{17,9},{10,18},{18,10},{11,19},{19,11},{12,20... | collective-permute-start | bytes 245768 | tf_op jit(solution)/shard_map/ppermute | solution.py:565
  13.7 9.6 %collective-permute-start.4 = (f32[5,4,8,128]{3,2,1,0:T(8,128)S(1)}, f32[5,4,8,128]{3,2,1,0:T(8,128)S(1)}, u32[]{:S(2)}, u32[]{:S(2)}) collective-permute-start(f32[5,4,8,128]{3,2,1,0:T(8,128)S(1)} %get-tuple-element.28.own), channel_id=1, source_target_pairs={{0,8},{8,0},{16,24},{24,16},{1,9},{9,1},{17,25},{25,17},{2,10},{10... | collective-permute-start | bytes 245768 | tf_op jit(solution)/shard_map/ppermute | solution.py:565
  23.3 8.7 %collective-permute-start.6 = (f32[5,12,4,128]{3,2,1,0:T(4,128)S(1)}, f32[5,12,4,128]{3,2,1,0:T(4,128)S(1)}, u32[]{:S(2)}, u32[]{:S(2)}) collective-permute-start(f32[5,12,4,128]{3,2,1,0:T(4,128)S(1)} %get-tuple-element.30), channel_id=1, source_target_pairs={{0,1},{1,0},{2,3},{3,2},{4,5},{5,4},{6,7},{7,6},{8,9},{9,8},{10,11... | collective-permute-start | bytes 368648 | tf_op jit(solution)/shard_map/ppermute | solution.py:565
  28.2 3.8 %collective-permute-start.7 = (f32[5,12,4,128]{3,2,1,0:T(4,128)S(1)}, f32[5,12,4,128]{3,2,1,0:T(4,128)S(1)}, u32[]{:S(2)}, u32[]{:S(2)}) collective-permute-start(f32[5,12,4,128]{3,2,1,0:T(4,128)S(1)} %get-tuple-element.31), channel_id=1, source_target_pairs={{1,2},{2,1},{3,4},{4,3},{5,6},{6,5},{9,10},{10,9},{11,12},{12,11},... | collective-permute-start | bytes 368648 | tf_op jit(solution)/shard_map/ppermute | solution.py:565

commit v2 on v1

--- a/solution.py
+++ b/solution.py
@@ -38,12 +38,88 @@
         return x + self.low * turn(x, self.wide, 1) + self.high * turn(x, -self.wide, 1)
 
     def pair(self, x):
-        return x + jnp.where(self.first, turn(x, -self.wide, 1), turn(x, self.wide, 1))
-
-
-def smooth_rows(x):
-    pair = x + turn(x, 1, 0)
-    return pair + turn(pair, -1, 0)
+        return x + swap_lanes(x, self.wide, self.first)
+
+    def rows(self, x):
+        pair = x + turn(x, 1, 0)
+        return pair + turn(pair, -1, 0)
+
+
+def swap_lanes(x, by, first):
+    return jnp.where(first, turn(x, -by, 1), turn(x, by, 1))
+
+
+class Packed:
+    def __init__(self, bricks, wide):
+        shape = (1, bricks, LANES)
+        ids = lane_ids(shape)
+        line = lax.broadcasted_iota(jnp.int32, shape, 1)
+        self.wide, self.across = wide, 4 * wide
+        row = ids & (4 - wide)
+        top, bottom = row == 0, row == 4 - wide
+
+        def number(mask, value):
+            return jnp.where(mask, value, 0.0).astype(F32)
+
+        self.low = number(ids >= self.across, 0.5)
+        self.high = number(ids < LANES - self.across, 0.5)
+        self.not_top, self.not_bottom = number(~top, 1.0), number(~bottom, 1.0)
+        self.top = number(top & (line > 0), 1.0)
+        self.bottom = number(bottom & (line < bricks - 1), 1.0)
+        self.odd_row, self.odd_lane = number((ids & 1) > 0, 1.0), number((ids & 4) > 0, 1.0)
+
+    def smooth(self, x):
+        return x + (self.low * turn(x, self.across, 2) + self.high * turn(x, -self.across, 2))
+
+    def rows(self, x):
+        back, ahead = turn(x, self.wide, 2), turn(x, -self.wide, 2)
+        if self.wide == 2:
+            far_back, far_ahead = ahead, back
+        else:
+            far_back, far_ahead = turn(x, -3, 2), turn(x, 3, 2)
+        before = self.not_top * back + self.top * turn(far_back, 1, 1)
+        after = self.not_bottom * ahead + self.bottom * turn(far_ahead, -1, 1)
+        return (x + x) + (before + after)
+
+    def pair(self, x):
+        for by, is_odd in ((1, self.odd_row), (4, self.odd_lane)):
+            x = x + (is_odd * turn(x, by, 2) + (1.0 - is_odd) * turn(x, -by, 2))
+        return x
+
+    def planes(self, x):
+        none = jnp.zeros_like(x[:1])
+        above = jnp.concatenate([x[1:], none], axis=0)
+        below = jnp.concatenate([none, x[:-1]], axis=0)
+        return (x + x) + (above + below)
+
+    def full(self, x):
+        return self.smooth(self.rows(self.planes(x)))
+
+    def terms(self, q, s):
+        total = 24.0 * q + self.full(q) + s
+        return total + 8.0 * q, DAMPING / (total + (4.0 * COUPLING) * q)
+
+    def defects(self, v, q, weight, source):
+        count = q.shape[0]
+        stack = [self.planes(x) for x in v] + [self.planes(q * x) for x in v]
+        both = self.smooth(self.rows(jnp.concatenate(stack, axis=0)))
+        part = [both[i * count : (i + 1) * count] for i in range(6)]
+        coupled = (4.0 * COUPLING) * q * (v[0] + v[1] + v[2])
+        return [
+            source[k] - weight * v[k] + (q * part[k] + part[3 + k]) - coupled for k in range(3)
+        ]
+
+    def sweep(self, v, q, weight, step, source):
+        r = self.defects(v, q, weight, source)
+        return [v[k] + step * r[k] for k in range(3)]
+
+    def restrict(self, x):
+        x = x.reshape((x.shape[0] // 2, 2) + x.shape[1:])
+        return 0.125 * self.pair(x[:, 0] + x[:, 1])
+
+
+def twice_planes(x):
+    return jnp.concatenate([x[i // 2 : i // 2 + 1] for i in range(2 * x.shape[0])], axis=0)
 
 
 def smooth_planes(get, p):
@@ -82,8 +158,8 @@
         q = q_at(p)
         sums = []
         for k in range(3):
-            x = smooth_rows(smooth_planes(v_at[k], p))
-            y = smooth_rows(smooth_planes(w_at[k], p))
+            x = lane.rows(smooth_planes(v_at[k], p))
+            y = lane.rows(smooth_planes(w_at[k], p))
             sums.append(q * lane.smooth(x) + lane.smooth(y))
         yield p, [v_at[k](p) for k in range(3)], q, sums
 
@@ -105,7 +181,7 @@
 def stiffness_sum(quarter, planes, bounds, lane):
     q_at = remember(within(lambda p: quarter[p], *bounds))
     for p in planes:
-        yield p, 24.0 * q_at(p) + lane.smooth(smooth_rows(smooth_planes(q_at, p)))
+        yield p, 24.0 * q_at(p) + lane.smooth(lane.rows(smooth_planes(q_at, p)))
 
 
 def step_of(inside, diagonal):
@@ -240,7 +316,10 @@
             continue
         i = (p - HALO) // 2
         for k in range(3):
-            work[k, i] = lane.pair(held[k] + r[k])
+            work[k, i] = held[k] + r[k]
+    for i in range(planes // 2):
+        for k in range(3):
+            work[k, i] = lane.pair(work[k, i])
     for i in range(planes // 2):
         for k in range(3):
             own_coarse[k, i] = 0.125 * (
@@ -347,7 +426,10 @@
             continue
         i = (p - HALO) // 2
         for k in range(3):
-            work[k, i] = lane.pair(held[k] + r[k])
+            work[k, i] = held[k] + r[k]
+    for i in range(planes // 2):
+        for k in range(3):
+            work[k, i] = lane.pair(work[k, i])
     for i in range(planes // 2):
         for k in range(3):
             send(
@@ -362,137 +444,70 @@
             send((3 + k) * (planes // 2) + i, cells[k, i])
 
 
-def prolong_rows(coarse, put):
-    rows = coarse.shape[0]
-    put(pl.ds(0, rows, stride=2), coarse)
-    put(pl.ds(1, rows, stride=2), coarse)
-
-
 def coarse_and_after(
     bricks_before,
     table, v2_mid, source_mid, quarter_mid, weight_mid, step_mid,
     v2_fine, source_fine, quarter_fine, weight_fine, step_fine,
     out,
-    b2, q2, s2, e2, x2, u2, t2, b3, q3, s3, e3, x3, u3, grown, u_mid, x_mid, u_fine, x_fine,
+    wide2, u_mid, x_mid, u_fine, x_fine,
 ):
     brick = lax.axis_index("brick")
     slab = lax.axis_index("len")
     slabs, bricks, lines = table.shape[0], table.shape[1], table.shape[2]
     depth = lines // 5
-    rows_each = 4
     planes2 = slabs * depth
-    all_rows = b2.shape[2]
-    used = rows_each * bricks + 2 * HALO
-    pad = HALO
-
-    ids = lane_ids((bricks, LANES))
-    first1, first2 = (ids & 1) == 0, (ids & 2) == 0
-    zero_rows = jnp.zeros((pad, LANES), F32)
-    zero_tail = jnp.zeros((all_rows - pad - rows_each * bricks, LANES), F32)
-    for f in range(5):
-        for i in range(planes2):
-            target = b2.at[f, i] if f < 3 else (q2.at[i] if f == 3 else s2.at[i])
-            target[pl.ds(0, pad), :] = zero_rows
-            target[pl.ds(pad + rows_each * bricks, zero_tail.shape[0]), :] = zero_tail
-            line = table[i // depth, :, f * depth + i % depth, :]
-            for row in range(rows_each):
-                x = jnp.where((ids & 3) == row, line, 0.0)
-                x = x + jnp.where(first1, turn(x, -1, 1), turn(x, 1, 1))
-                x = x + jnp.where(first2, turn(x, -2, 1), turn(x, 2, 1))
-                target[pl.ds(pad + row, bricks, stride=rows_each), :] = x
-
-    lane2 = Lane(all_rows, 4)
-    bounds = (0, planes2)
-    everything = range(planes2)
-    for p, w in stiffness_sum(q2, everything, bounds, lane2):
-        q, s = q2[p], s2[p]
-        total = w + s
-        e2[p] = total + 8.0 * q
-        st = step_of(s, total + (4.0 * COUPLING) * q)
-        x2[p] = st
-        for k in range(3):
-            u2[k, p] = st * b2[k, p]
-
-    def put_t2(k, p, value):
-        t2[k, p] = value
-
-    sweep(lambda k, p: u2[k, p], q2, e2, x2, b2, everything, bounds, lane2, put_t2)
-
-    rows3 = all_rows // 2
-    planes3 = planes2 // 2
-    held = {}
-    for p, _, r in defects(lambda k, p: t2[k, p], q2, e2, b2, everything, bounds, lane2):
-        if p % 2 == 0:
-            held = r
-            continue
-        for k in range(3):
-            u2[k, p] = lane2.pair(held[k] + r[k])
-    for i in range(planes3):
-        grown[0] = lane2.pair(q2[2 * i] + q2[2 * i + 1])
-        grown[1] = lane2.pair(s2[2 * i] + s2[2 * i + 1])
-        q3[i] = (0.25 * 0.125) * (
-            grown[0, pl.ds(0, rows3, stride=2), :] + grown[0, pl.ds(1, rows3, stride=2), :]
+
+    def field(f):
+        return jnp.stack(
+            [table[i // depth, :, f * depth + i % depth, :] for i in range(planes2)], axis=0
         )
-        s3[i] = 0.125 * (
-            grown[1, pl.ds(0, rows3, stride=2), :] + grown[1, pl.ds(1, rows3, stride=2), :]
-        )
-        for k in range(3):
-            b3[k, i] = 0.125 * (
-                u2[k, 2 * i + 1, pl.ds(0, rows3, stride=2), :]
-                + u2[k, 2 * i + 1, pl.ds(1, rows3, stride=2), :]
-            )
-
-    lane3 = Lane(rows3, 8)
-    bounds3 = (0, planes3)
-    for p, w in stiffness_sum(q3, range(planes3), bounds3, lane3):
-        q, s = q3[p], s3[p]
-        total = w + s
-        e3[p] = total + 8.0 * q
-        st = step_of(s, total + (4.0 * COUPLING) * q)
-        x3[p] = st
-        for k in range(3):
-            u3[0, k, p] = st * b3[k, p]
-    for turn_at in range(3):
-
-        def put_u3(k, p, value, turn_at=turn_at):
-            u3[(turn_at + 1) % 2, k, p] = value
-
-        sweep(
-            lambda k, p: u3[turn_at % 2, k, p], q3, e3, x3, b3,
-            range(planes3), bounds3, lane3, put_u3,
-        )
-
+
+    lane2, lane3 = Packed(bricks, 1), Packed(bricks, 2)
+    b2, q2, s2 = [field(k) for k in range(3)], field(3), field(4)
+    e2, x2 = lane2.terms(q2, s2)
+    u2 = lane2.sweep([x2 * b for b in b2], q2, e2, x2, b2)
+
+    rest = lane2.defects(u2, q2, e2, b2)
+    joint = lane2.restrict(jnp.concatenate(rest + [0.25 * q2, s2], axis=0))
+    count = planes2 // 2
+    *b3, q3, s3 = [joint[i * count : (i + 1) * count] for i in range(5)]
+    e3, x3 = lane3.terms(q3, s3)
+    u3 = [x3 * b for b in b3]
+    for _ in range(3):
+        u3 = lane3.sweep(u3, q3, e3, x3, b3)
+
+    u2 = [u2[k] + twice_planes(u3[k]) for k in range(3)]
+    for _ in range(2):
+        u2 = lane2.sweep(u2, q2, e2, x2, b2)
+    wide2[...] = jnp.zeros_like(wide2)
     for k in range(3):
-        for i in range(planes3):
-            coarse = u3[1, k, i]
-            for half in range(2):
-                u2[k, 2 * i, pl.ds(half, rows3, stride=2), :] = coarse
-            both = u2[k, 2 * i]
-            t2[k, 2 * i] = t2[k, 2 * i] + both
-            t2[k, 2 * i + 1] = t2[k, 2 * i + 1] + both
-
-    def put_u2(k, p, value):
-        u2[k, p] = value
-
-    zero_plane = jnp.zeros((all_rows, LANES), F32)
-    sweep(lambda k, p: t2[k, p], q2, e2, x2, b2, everything, bounds, lane2, put_u2)
-
-    def put_wide(k, p, value):
-        t2[k, p + 2] = value
-
-    for k in range(3):
-        for p in (0, 1, planes2 + 2, planes2 + 3):
-            t2[k, p] = zero_plane
-    sweep(lambda k, p: u2[k, p], q2, e2, x2, b2, everything, bounds, lane2, put_wide)
+        wide2[k, pl.ds(2, planes2), pl.ds(8, bricks), :] = u2[k]
 
     planes1 = v2_mid.shape[1]
     rows1 = v2_mid.shape[2]
     lane1 = Lane(rows1, 2)
     bounds1 = (0, planes1)
-    row_at = rows_each * (brick - bricks_before(brick)) + pad - 2
+    line_at = brick - bricks_before(brick) + 8
+    half_shape = (rows1 // 2, LANES)
+    ids, row = lane_ids(half_shape), lax.broadcasted_iota(jnp.int32, half_shape, 0)
+    mine = (ids & 3) == ((row + 2) & 3)
+    pieces = []
     for k in range(3):
         for i in range(planes1 // 2):
-            piece = t2[k, depth * slab + i, pl.ds(row_at, rows1 // 2), :]
+            low, own, high = [
+                jnp.broadcast_to(
+                    wide2[k, depth * slab + i, pl.ds(line_at + at, 1), :], half_shape
+                )
+                for at in (-1, 0, 1)
+            ]
+            piece = jnp.where(row < 2, low, jnp.where(row < 6, own, high))
+            pieces.append(jnp.where(mine, piece, 0.0))
+    for by in (1, 2):
+        first = (ids & by) == 0
+        pieces = [x + swap_lanes(x, by, first) for x in pieces]
+    for k in range(3):
+        for i in range(planes1 // 2):
+            piece = pieces[k * (planes1 // 2) + i]
             for half in range(2):
                 x_mid[k, i, pl.ds(half, rows1 // 2, stride=2), :] = piece
             both = x_mid[k, i]
@@ -618,15 +633,10 @@
             table, first_brick(lax.axis_index("brick")), window, axis=1
         )
     planes2 = slabs * depth
-    rows2 = -(-(4 * window + 2 * HALO) // 16) * 16
-    f2, c2 = (3, planes2, rows2, LANES), (planes2, rows2, LANES)
-    f3, c3 = (3, planes2 // 2, rows2 // 2, LANES), (planes2 // 2, rows2 // 2, LANES)
     (out,) = call(
         functools.partial(coarse_and_after, first_brick),
         [forces.shape],
-        [f2, c2, c2, c2, c2, f2, (3, planes2 + 4, rows2, LANES)]
-        + [f3, c3, c3, c3, c3, (2,) + f3]
-        + [(2, rows2, LANES), field1, field1, field, field],
+        [(3, planes2 + 4, window + 16, LANES), field1, field1, field, field],
         name="coarse_and_after",
     )(table, *middle, *fine)
     return out

time: 67.3 us -> 55.8 us (0.83)
  Pallas kernels: 18.9 us -> 7.49 us
    pallas_call x1, Pallas kernels: 16.4 us -> 5.15 us  [body(): call(functools.partial(coarse_and_after, first_brick), [forces.shape], [(...]
where the time goes in v2:
time: 55.8 us; the launch traced here: 55.5 us
  starting transfers between devices  19.6 us (35%)
  blocking collectives  17.7 us (32%)
  Pallas kernels  7.49 us (13%)
  waiting for transfers between devices  7.07 us (13%)
  local copies, waits for them, and re-layouts  3.56 us (6%)
    ppermute x8, starting transfers between devices, swap(): return lax.ppermute(x, axis, pairs)  19.6 us
    all_to_all x1, blocking collectives, body(): table = lax.all_to_all(to_all, BOTH, 0, 0, tiled=True)  17.7 us
    ppermute x8, waiting for transfers between devices, swap(): return lax.ppermute(x, axis, pairs)  7.07 us
    pallas_call x1, Pallas kernels, body(): call(functools.partial(coarse_and_after, first_brick), [forces.shape], [(...  5.15 us
    unnamed x8, local copies, waits for them, and re-layouts  3.44 us
    pallas_call x1, Pallas kernels, body(): call(fine_before, [(5, half, half_rows, LANES), (2, half // 2, half_rows...  1.46 us
  transfers between devices with their start and end apart: 8, of which 4 were waited for; matrix products, arithmetic and copies ran while one was open for 0% of the time, Pallas kernels for 0%

profile of v2, /device:TPU:0, one launch (start us, length us, event | category | flops | bytes accessed | tf_op | source)
XLA Modules:
  0.0 55.5 jit_solution(12330310460291194771)
XLA Ops:
  0.0 0.9 %copy-done = f32[3,8,16,128]{3,2,1,0:T(8,128)S(1)} copy-done((f32[3,8,16,128]{3,2,1,0:T(8,128)S(1)}, f32[3,8,16,128]{3,2,1,0:T(8,128)}, u32[]{:S(2)}) %copy-start) | copy-done | bytes 196632
  0.9 0.8 %copy-done.1 = f32[8,16,128]{2,1,0:T(8,128)S(1)} copy-done((f32[8,16,128]{2,1,0:T(8,128)S(1)}, f32[8,16,128]{2,1,0:T(8,128)}, u32[]{:S(2)}) %copy-start.1) | copy-done | bytes 65560
  1.8 0.8 %copy-done.2 = s32[8,16,128]{2,1,0:T(8,128)S(1)} copy-done((s32[8,16,128]{2,1,0:T(8,128)S(1)}, s32[8,16,128]{2,1,0:T(8,128)}, u32[]{:S(2)}) %copy-start.2) | copy-done | bytes 65560
  2.6 0.8 %copy-done.3 = s32[8,16,128]{2,1,0:T(8,128)S(1)} copy-done((s32[8,16,128]{2,1,0:T(8,128)S(1)}, s32[8,16,128]{2,1,0:T(8,128)}, u32[]{:S(2)}) %copy-start.3) | copy-done | bytes 65560
  3.5 0.5 collective-permute-start
  4.0 0.7 %collective-permute-start.1 = (f32[5,4,16,128]{3,2,1,0:T(8,128)S(1)}, f32[5,4,16,128]{3,2,1,0:T(8,128)S(1)}, u32[]{:S(2)}, u32[]{:S(2)}) collective-permute-start(f32[5,4,16,128]{3,2,1,0:T(8,128)S(1)} %get-tuple-element.25), channel_id=1, source_target_pairs={{8,16},{16,8},{9,17},{17,9},{10,18},{18,10},{11,19},{19,11},{12,20... | collective-permute-start | bytes 491528 | tf_op jit(solution)/shard_map/ppermute | solution.py:580
  4.7 0.4 collective-permute-done.from_a
  5.0 0.0 collective-permute-done.1.from_b
  5.0 0.1 pack_rows_fine.1
  5.1 2.9 %collective-permute-start.2 = (f32[5,16,4,128]{3,2,1,0:T(4,128)S(1)}, f32[5,16,4,128]{3,2,1,0:T(4,128)S(1)}, u32[]{:S(2)}, u32[]{:S(2)}) collective-permute-start(f32[5,16,4,128]{3,2,1,0:T(4,128)S(1)} %get-tuple-element.26), channel_id=1, source_target_pairs={{0,1},{1,0},{2,3},{3,2},{4,5},{5,4},{6,7},{7,6},{8,9},{9,8},{10,11... | collective-permute-start | bytes 491528 | tf_op jit(solution)/shard_map/ppermute | solution.py:580
  8.1 0.7 %collective-permute-start.3 = (f32[5,16,4,128]{3,2,1,0:T(4,128)S(1)}, f32[5,16,4,128]{3,2,1,0:T(4,128)S(1)}, u32[]{:S(2)}, u32[]{:S(2)}) collective-permute-start(f32[5,16,4,128]{3,2,1,0:T(4,128)S(1)} %get-tuple-element.27), channel_id=1, source_target_pairs={{1,2},{2,1},{3,4},{4,3},{5,6},{6,5},{9,10},{10,9},{11,12},{12,11},... | collective-permute-start | bytes 491528 | tf_op jit(solution)/shard_map/ppermute | solution.py:580
  8.7 2.6 %collective-permute-done.2.from_c = f32[5,16,4,128]{3,2,1,0:T(4,128)S(1)} collective-permute-done((f32[5,16,4,128]{3,2,1,0:T(4,128)S(1)}, f32[5,16,4,128]{3,2,1,0:T(4,128)S(1)}, u32[]{:S(2)}, u32[]{:S(2)}) %collective-permute-start.2) | collective-permute-done | bytes 163872 | tf_op jit(solution)/shard_map/ppermute | solution.py:580
  11.4 0.0 collective-permute-done.3.from_d
  11.4 1.5 %fine_before.1 = (f32[5,4,8,128]{3,2,1,0:T(8,128)S(1)}, f32[2,2,4,128]{3,2,1,0:T(4,128)S(1)}, f32[3,16,24,128]{3,2,1,0:T(8,128)S(1)}, f32[3,16,24,128]{3,2,1,0:T...) custom-call(f32[3,8,16,128]{3,2,1,0:T(8,128)S(1)} %copy-done, ...), custom_call_target="tpu_custom_call" | custom-call | tf_op jit(solution)/shard_map/fine_before/pallas_call | solution.py:599
  12.8 0.7 %collective-permute-start.5 = (f32[5,4,8,128]{3,2,1,0:T(8,128)S(1)}, f32[5,4,8,128]{3,2,1,0:T(8,128)S(1)}, u32[]{:S(2)}, u32[]{:S(2)}) collective-permute-start(f32[5,4,8,128]{3,2,1,0:T(8,128)S(1)} %get-tuple-element.28.own), channel_id=1, source_target_pairs={{8,16},{16,8},{9,17},{17,9},{10,18},{18,10},{11,19},{19,11},{12,20... | collective-permute-start | bytes 245768 | tf_op jit(solution)/shard_map/ppermute | solution.py:580
  13.5 8.7 %collective-permute-start.4 = (f32[5,4,8,128]{3,2,1,0:T(8,128)S(1)}, f32[5,4,8,128]{3,2,1,0:T(8,128)S(1)}, u32[]{:S(2)}, u32[]{:S(2)}) collective-permute-start(f32[5,4,8,128]{3,2,1,0:T(8,128)S(1)} %get-tuple-element.28.own), channel_id=1, source_target_pairs={{0,8},{8,0},{16,24},{24,16},{1,9},{9,1},{17,25},{25,17},{2,10},{10... | collective-permute-start | bytes 245768 | tf_op jit(solution)/shard_map/ppermute | solution.py:580
  22.2 0.9 %collective-permute-done.4.from_a = f32[5,4,8,128]{3,2,1,0:T(8,128)S(1)} collective-permute-done((f32[5,4,8,128]{3,2,1,0:T(8,128)S(1)}, f32[5,4,8,128]{3,2,1,0:T(8,128)S(1)}, u32[]{:S(2)}, u32[]{:S(2)}) %collective-permute-start.4) | collective-permute-done | bytes 81952 | tf_op jit(solution)/shard_map/ppermute | solution.py:580
  23.1 4.9 %collective-permute-start.6 = (f32[5,12,4,128]{3,2,1,0:T(4,128)S(1)}, f32[5,12,4,128]{3,2,1,0:T(4,128)S(1)}, u32[]{:S(2)}, u32[]{:S(2)}) collective-permute-start(f32[5,12,4,128]{3,2,1,0:T(4,128)S(1)} %get-tuple-element.30), channel_id=1, source_target_pairs={{0,1},{1,0},{2,3},{3,2},{4,5},{5,4},{6,7},{7,6},{8,9},{9,8},{10,11... | collective-permute-start | bytes 368648 | tf_op jit(solution)/shard_map/ppermute | solution.py:580
  28.0 0.7 %collective-permute-start.7 = (f32[5,12,4,128]{3,2,1,0:T(4,128)S(1)}, f32[5,12,4,128]{3,2,1,0:T(4,128)S(1)}, u32[]{:S(2)}, u32[]{:S(2)}) collective-permute-start(f32[5,12,4,128]{3,2,1,0:T(4,128)S(1)} %get-tuple-element.31), channel_id=1, source_target_pairs={{1,2},{2,1},{3,4},{4,3},{5,6},{6,5},{9,10},{10,9},{11,12},{12,11},... | collective-permute-start | bytes 368648 | tf_op jit(solution)/shard_map/ppermute | solution.py:580
  28.7 3.1 %collective-permute-done.6.from_c = f32[5,12,4,128]{3,2,1,0:T(4,128)S(1)} collective-permute-done((f32[5,12,4,128]{3,2,1,0:T(4,128)S(1)}, f32[5,12,4,128]{3,2,1,0:T(4,128)S(1)}, u32[]{:S(2)}, u32[]{:S(2)}) %collective-permute-start.6) | collective-permute-done | bytes 122912 | tf_op jit(solution)/shard_map/ppermute | solution.py:580
  31.8 0.7 %middle_before.1 = (f32[160,2,128]{2,1,0:T(2,128)S(1)}, f32[3,12,16,128]{3,2,1,0:T(8,128)S(1)}, f32[3,12,16,128]{3,2,1,0:T(8,128)S(1)}, f32[12,16,128]{2,1,0:T(8...) custom-call(f32[5,4,8,128]{3,2,1,0:T(8,128)S(1)} %get-tuple-element.28.own, ...), custom_call_target="tpu_custom_call" | custom-call | tf_op jit(solution)/shard_map/middle_before/pallas_call | solution.py:617
  32.6 17.7 %all_to_all.5 = f32[160,2,128]{2,1,0:T(2,128)S(1)} all-to-all(f32[160,2,128]{2,1,0:T(2,128)S(1)} %get-tuple-element.32), channel_id=1, replica_groups=mesh['len'=4,'brick'=8] {'len','brick'}, dimensions={0} | all-to-all | bytes 327680 | tf_op jit(solution)/shard_map/all_to_all | solution.py:624
  50.2 0.1 reshape.3.table
  50.3 5.1 %coarse_and_after.1 = f32[3,8,16,128]{3,2,1,0:T(8,128)} custom-call(f32[4,8,10,128]{3,2,1,0:T(8,128)S(1)} %reshape.3.table, f32[3,12,16,128]{3,2,1,0:T(8,128)S(1)} %get-tuple-element.33.v2_mid, f32[3,12,16,128]{3,2,1,0:T(8,128)S(1)} %get-tuple-element.34.source_mid, f32[12,16,128]{2,1,0:T(8,128)S(1)} %get-tuple-element.35.quarter_mid, ...), custom_call_target="tpu_custom_call" | custom-call | tf_op jit(solution)/shard_map/coarse_and_after/pallas_call | solution.py:636
  (8 shorter events, 0.1 us)
Async XLA Ops:
  0.0 0.9 %copy-start = (f32[3,8,16,128]{3,2,1,0:T(8,128)S(1)}, f32[3,8,16,128]{3,2,1,0:T(8,128)}, u32[]{:S(2)}) copy-start(f32[3,8,16,128]{3,2,1,0:T(8,128)} %forces.5) | copy-start | bytes 589828
  0.9 0.8 %copy-start.1 = (f32[8,16,128]{2,1,0:T(8,128)S(1)}, f32[8,16,128]{2,1,0:T(8,128)}, u32[]{:S(2)}) copy-start(f32[8,16,128]{2,1,0:T(8,128)} %modulus.5) | copy-start | bytes 196612
  1.8 0.8 %copy-start.2 = (s32[8,16,128]{2,1,0:T(8,128)S(1)}, s32[8,16,128]{2,1,0:T(8,128)}, u32[]{:S(2)}) copy-start(s32[8,16,128]{2,1,0:T(8,128)} %occupancy.5) | copy-start | bytes 196612
  2.6 0.8 %copy-start.3 = (s32[8,16,128]{2,1,0:T(8,128)S(1)}, s32[8,16,128]{2,1,0:T(8,128)}, u32[]{:S(2)}) copy-start(s32[8,16,128]{2,1,0:T(8,128)} %bonded.5) | copy-start | bytes 196612
  3.5 1.5 %collective-permute-start = (f32[5,4,16,128]{3,2,1,0:T(8,128)S(1)}, f32[5,4,16,128]{3,2,1,0:T(8,128)S(1)}, u32[]{:S(2)}, u32[]{:S(2)}) collective-permute-start(f32[5,4,16,128]{3,2,1,0:T(8,128)S(1)} %get-tuple-element.24), channel_id=1, source_target_pairs={{0,8},{8,0},{16,24},{24,16},{1,9},{9,1},{17,25},{25,17},{2,10},{10... | collective-permute-start | bytes 491528 | tf_op jit(solution)/shard_map/ppermute | solution.py:580
  4.0 1.0 %collective-permute-start.1 = (f32[5,4,16,128]{3,2,1,0:T(8,128)S(1)}, f32[5,4,16,128]{3,2,1,0:T(8,128)S(1)}, u32[]{:S(2)}, u32[]{:S(2)}) collective-permute-start(f32[5,4,16,128]{3,2,1,0:T(8,128)S(1)} %get-tuple-element.25), channel_id=1, source_target_pairs={{8,16},{16,8},{9,17},{17,9},{10,18},{18,10},{11,19},{19,11},{12,20... | collective-permute-start | bytes 491528 | tf_op jit(solution)/shard_map/ppermute | solution.py:580
  5.1 6.2 %collective-permute-start.2 = (f32[5,16,4,128]{3,2,1,0:T(4,128)S(1)}, f32[5,16,4,128]{3,2,1,0:T(4,128)S(1)}, u32[]{:S(2)}, u32[]{:S(2)}) collective-permute-start(f32[5,16,4,128]{3,2,1,0:T(4,128)S(1)} %get-tuple-element.26), channel_id=1, source_target_pairs={{0,1},{1,0},{2,3},{3,2},{4,5},{5,4},{6,7},{7,6},{8,9},{9,8},{10,11... | collective-permute-start | bytes 491528 | tf_op jit(solution)/shard_map/ppermute | solution.py:580
  8.1 3.3 %collective-permute-start.3 = (f32[5,16,4,128]{3,2,1,0:T(4,128)S(1)}, f32[5,16,4,128]{3,2,1,0:T(4,128)S(1)}, u32[]{:S(2)}, u32[]{:S(2)}) collective-permute-start(f32[5,16,4,128]{3,2,1,0:T(4,128)S(1)} %get-tuple-element.27), channel_id=1, source_target_pairs={{1,2},{2,1},{3,4},{4,3},{5,6},{6,5},{9,10},{10,9},{11,12},{12,11},... | collective-permute-start | bytes 491528 | tf_op jit(solution)/shard_map/ppermute | solution.py:580
  12.8 9.3 %collective-permute-start.5 = (f32[5,4,8,128]{3,2,1,0:T(8,128)S(1)}, f32[5,4,8,128]{3,2,1,0:T(8,128)S(1)}, u32[]{:S(2)}, u32[]{:S(2)}) collective-permute-start(f32[5,4,8,128]{3,2,1,0:T(8,128)S(1)} %get-tuple-element.28.own), channel_id=1, source_target_pairs={{8,16},{16,8},{9,17},{17,9},{10,18},{18,10},{11,19},{19,11},{12,20... | collective-permute-start | bytes 245768 | tf_op jit(solution)/shard_map/ppermute | solution.py:580
  13.5 9.6 %collective-permute-start.4 = (f32[5,4,8,128]{3,2,1,0:T(8,128)S(1)}, f32[5,4,8,128]{3,2,1,0:T(8,128)S(1)}, u32[]{:S(2)}, u32[]{:S(2)}) collective-permute-start(f32[5,4,8,128]{3,2,1,0:T(8,128)S(1)} %get-tuple-element.28.own), channel_id=1, source_target_pairs={{0,8},{8,0},{16,24},{24,16},{1,9},{9,1},{17,25},{25,17},{2,10},{10... | collective-permute-start | bytes 245768 | tf_op jit(solution)/shard_map/ppermute | solution.py:580
  23.1 8.7 %collective-permute-start.6 = (f32[5,12,4,128]{3,2,1,0:T(4,128)S(1)}, f32[5,12,4,128]{3,2,1,0:T(4,128)S(1)}, u32[]{:S(2)}, u32[]{:S(2)}) collective-permute-start(f32[5,12,4,128]{3,2,1,0:T(4,128)S(1)} %get-tuple-element.30), channel_id=1, source_target_pairs={{0,1},{1,0},{2,3},{3,2},{4,5},{5,4},{6,7},{7,6},{8,9},{9,8},{10,11... | collective-permute-start | bytes 368648 | tf_op jit(solution)/shard_map/ppermute | solution.py:580
  28.0 3.8 %collective-permute-start.7 = (f32[5,12,4,128]{3,2,1,0:T(4,128)S(1)}, f32[5,12,4,128]{3,2,1,0:T(4,128)S(1)}, u32[]{:S(2)}, u32[]{:S(2)}) collective-permute-start(f32[5,12,4,128]{3,2,1,0:T(4,128)S(1)} %get-tuple-element.31), channel_id=1, source_target_pairs={{1,2},{2,1},{3,4},{4,3},{5,6},{6,5},{9,10},{10,9},{11,12},{12,11},... | collective-permute-start | bytes 368648 | tf_op jit(solution)/shard_map/ppermute | solution.py:580

commit v3 on v2

--- a/solution.py
+++ b/solution.py
@@ -13,6 +13,9 @@
 PENALTY = 20.0
 
 HALO = 4
+WIDE = 12
+ROWS = (10, 10, 10, 11, 10)
+PLANES = (3, 3, 3, 4, 3)
 LANES = 128
 F32 = jnp.float32
 BOTH = ("len", "brick")
@@ -192,89 +195,116 @@
     return lax.rem(lax.axis_index(axis), 2) == 1
 
 
+class From:
+    def __init__(self, ref, first):
+        self.ref, self.first = ref, first
+
+    def __getitem__(self, at):
+        if isinstance(at, tuple):
+            return self.ref[at[0], at[1] - self.first]
+        return self.ref[at - self.first]
+
+
 def vmem(shape):
     return pltpu.VMEM(shape, F32)
 
 
-def raw_field(forces, modulus, occupancy, bonded, k, p, rows):
-    if k < 3:
-        return forces[k, p, rows, :]
-    if k == 3:
-        return modulus[p, rows, :] * occupancy[p, rows, :].astype(F32)
-    return MASS_TERM + PENALTY * bonded[p, rows, :].astype(F32)
-
-
-def pack_planes(forces, modulus, occupancy, bonded, to_a, to_b):
-    planes, rows = modulus.shape[0], modulus.shape[1]
-    last = planes - HALO
-    is_odd = lax.rem(lax.axis_index("len"), 2)
-    start_a, start_b = (1 - is_odd) * last, is_odd * last
-    for i in range(HALO):
-        for k in range(5):
-            to_a[k, i] = raw_field(
-                forces, modulus, occupancy, bonded, k, start_a + i, slice(0, rows)
-            )
-            to_b[k, i] = raw_field(
-                forces, modulus, occupancy, bonded, k, start_b + i, slice(0, rows)
-            )
-
-
-def extended_rows(own, from_a, from_b, planes, is_odd):
-    def get(k, p, rows):
-        if p < HALO:
-            return jnp.where(is_odd, from_a[k, p, rows, :], from_b[k, p, rows, :])
-        if p >= HALO + planes:
-            i = p - HALO - planes
-            return jnp.where(is_odd, from_b[k, i, rows, :], from_a[k, i, rows, :])
-        return own(k, p - HALO, rows)
+def row_spots(planes):
+    spots, at = {}, 0
+    for k, reach in enumerate(ROWS):
+        for p in range(planes):
+            spots[k, p] = slice(at, at + reach)
+            at += reach
+    return spots, at
+
+
+def plane_spots(heights):
+    spots, at = {}, 0
+    for k, count in enumerate(PLANES):
+        for i in range(count):
+            spots[k, i] = slice(at, at + heights[k])
+            at += heights[k]
+    return spots, at
+
+
+def middle_spots(rows):
+    return plane_spots([rows] * 5)
+
+
+def corner_spots():
+    return plane_spots([2 * reach for reach in ROWS])
+
+
+def pack_rows(
+    forces, modulus, occupancy, bonded, own, to_c, to_d, to_a, to_b,
+    modulus_here, occupancy_here, bonded_here, arrived,
+):
+    copies = [
+        pltpu.make_async_copy(source, target, arrived.at[i])
+        for i, (source, target) in enumerate(
+            [
+                (modulus, modulus_here),
+                (occupancy, occupancy_here),
+                (bonded, bonded_here),
+                (forces, own.at[pl.ds(0, 3)]),
+            ]
+        )
+    ]
+    for copy in copies:
+        copy.start()
+    for copy in copies:
+        copy.wait()
+    planes, rows = own.shape[1], own.shape[2]
+    for p in range(planes):
+        own[3, p] = modulus_here[p] * occupancy_here[p].astype(F32)
+        own[4, p] = MASS_TERM + PENALTY * bonded_here[p].astype(F32)
+    is_odd = odd("brick")
+    spots, _ = row_spots(planes)
+    for (k, p), spot in spots.items():
+        first = own[k, p, 0 : ROWS[k], :]
+        last = own[k, p, rows - ROWS[k] : rows, :]
+        to_c[spot, :] = jnp.where(is_odd, first, last)
+        to_d[spot, :] = jnp.where(is_odd, last, first)
+    is_odd = odd("len")
+    for (k, i), spot in middle_spots(rows)[0].items():
+        first, last = own[k, i], own[k, planes - PLANES[k] + i]
+        to_a[spot, :] = jnp.where(is_odd, first, last)
+        to_b[spot, :] = jnp.where(is_odd, last, first)
+
+
+def rows_beside(from_c, from_d):
+    is_odd = odd("brick")
+
+    def get(spot):
+        c, d = from_c[spot, :], from_d[spot, :]
+        return jnp.where(is_odd, c, d), jnp.where(is_odd, d, c)
 
     return get
 
 
-def pack_rows_from(get, planes, rows, to_c, to_d):
-    is_odd = odd("brick")
-    for k in range(5):
-        for p in range(planes + 2 * HALO):
-            first = get(k, p, slice(0, HALO))
-            last = get(k, p, slice(rows - HALO, rows))
-            to_c[k, p] = jnp.where(is_odd, first, last)
-            to_d[k, p] = jnp.where(is_odd, last, first)
-
-
-def pack_rows_fine(forces, modulus, occupancy, bonded, from_a, from_b, to_c, to_d):
-    planes, rows = modulus.shape[0], modulus.shape[1]
-    own = functools.partial(raw_field, forces, modulus, occupancy, bonded)
-    pack_rows_from(
-        extended_rows(own, from_a, from_b, planes, odd("len")), planes, rows, to_c, to_d
-    )
-
-
-def pack_rows_coarse(own, from_a, from_b, to_c, to_d):
+def pack_corners(planes, from_c, from_d, middle_a, middle_b, to_a, to_b):
+    del middle_a, middle_b
+    is_odd = odd("len")
+    from_rows, _ = row_spots(planes)
+    beside = rows_beside(from_c, from_d)
+    for (k, i), spot in corner_spots()[0].items():
+        firsts = beside(from_rows[k, i])
+        lasts = beside(from_rows[k, planes - PLANES[k] + i])
+        for half, (first, last) in enumerate(zip(firsts, lasts)):
+            start = spot.start + half * ROWS[k]
+            span = slice(start, start + ROWS[k])
+            to_a[span, :] = jnp.where(is_odd, first, last)
+            to_b[span, :] = jnp.where(is_odd, last, first)
+
+
+def fine_before(
+    own, from_c, from_d, middle_a, middle_b, corner_a, corner_b,
+    own_coarse, to_len, cells, v2_kept, source_kept, quarter_kept, weight_kept, step_kept,
+    v2, source, quarter, weight, step, shift, v1, work, coarse_q,
+):
     planes, rows = own.shape[1], own.shape[2]
-    get = extended_rows(lambda k, p, r: own[k, p, r, :], from_a, from_b, planes, odd("len"))
-    pack_rows_from(get, planes, rows, to_c, to_d)
-
-
-def spread_rows(get, from_c, from_d, planes, rows, put):
-    is_odd = odd("brick")
-    for p in range(planes + 2 * HALO):
-        for k in range(5):
-            low = jnp.where(is_odd, from_c[k, p], from_d[k, p])
-            high = jnp.where(is_odd, from_d[k, p], from_c[k, p])
-            put(k, p, slice(0, HALO), low)
-            put(k, p, slice(HALO, HALO + rows), get(k, p, slice(0, rows)))
-            put(k, p, slice(HALO + rows, 2 * HALO + rows), high)
-
-
-def fine_before(
-    forces, modulus, occupancy, bonded, from_a, from_b, from_c, from_d,
-    own_coarse, cells, v2, source, quarter, weight, step,
-    shift, v1, work, coarse_q,
-):
-    planes, rows = modulus.shape[0], modulus.shape[1]
-    ext_planes, ext_rows = planes + 2 * HALO, rows + 2 * HALO
+    ext_planes, ext_rows = planes + 2 * HALO, rows + 2 * WIDE
     lane = Lane(ext_rows, 1)
-    own = functools.partial(raw_field, forces, modulus, occupancy, bonded)
 
     def put(k, p, r, value):
         if k < 3:
@@ -284,8 +314,29 @@
         else:
             shift[p, r, :] = value
 
-    get = extended_rows(own, from_a, from_b, planes, odd("len"))
-    spread_rows(get, from_c, from_d, planes, rows, put)
+    beside = rows_beside(from_c, from_d)
+    for (k, p), spot in row_spots(planes)[0].items():
+        low, high = beside(spot)
+        put(k, HALO + p, slice(WIDE - ROWS[k], WIDE), low)
+        put(k, HALO + p, slice(WIDE, WIDE + rows), own[k, p])
+        put(k, HALO + p, slice(WIDE + rows, WIDE + rows + ROWS[k]), high)
+    is_odd = odd("len")
+    kept = slice(WIDE - HALO, WIDE + rows + HALO)
+    corners = corner_spots()[0]
+    for (k, i), spot in middle_spots(rows)[0].items():
+        reach, corner = ROWS[k], corners[k, i].start
+        for start, a, b in (
+            (WIDE - reach, corner_a[corner : corner + reach, :], corner_b[corner : corner + reach, :]),
+            (WIDE, middle_a[spot, :], middle_b[spot, :]),
+            (
+                WIDE + rows,
+                corner_a[corner + reach : corner + 2 * reach, :],
+                corner_b[corner + reach : corner + 2 * reach, :],
+            ),
+        ):
+            r = slice(start, start + a.shape[0])
+            put(k, HALO - PLANES[k] + i, r, jnp.where(is_odd, a, b))
+            put(k, HALO + planes + i, r, jnp.where(is_odd, b, a))
 
     bounds = (0, ext_planes)
     for p, w in stiffness_sum(quarter, range(1, ext_planes - 1), bounds, lane):
@@ -296,9 +347,17 @@
         step[p] = st
         for k in range(3):
             v1[k, p] = st * source[k, p]
+        if 2 <= p < ext_planes - 2:
+            quarter_kept[p - 2] = q[kept]
+        if 3 <= p < ext_planes - 3:
+            weight_kept[p - 3] = weight[p, kept, :]
+            step_kept[p - 3] = st[kept]
+            for k in range(3):
+                source_kept[k, p - 3] = source[k, p, kept, :]
 
     def put_v2(k, p, value):
         v2[k, p] = value
+        v2_kept[k, p - 2] = value[kept]
 
     sweep(
         lambda k, p: v1[k, p], quarter, weight, step, source,
@@ -306,7 +365,9 @@
     )
 
     held = {}
-    half = rows // 2
+    half = rows // 2 + 2 * HALO
+    first_row = WIDE - 2 * HALO
+    coarse_planes = planes // 2
     for p, _, r in defects(
         lambda k, p: v2[k, p], quarter, weight, source,
         range(HALO, HALO + planes), bounds, lane,
@@ -317,77 +378,86 @@
         i = (p - HALO) // 2
         for k in range(3):
             work[k, i] = held[k] + r[k]
-    for i in range(planes // 2):
-        for k in range(3):
+    for i in range(coarse_planes):
+        work[4, i] = shift[HALO + 2 * i] + shift[HALO + 2 * i + 1]
+    reach = coarse_planes + 2
+    for j in range(reach):
+        work[3, j] = quarter[2 * j + 2] + quarter[2 * j + 3]
+    for k in range(5):
+        for i in range(reach if k == 3 else coarse_planes):
             work[k, i] = lane.pair(work[k, i])
-    for i in range(planes // 2):
-        for k in range(3):
-            own_coarse[k, i] = 0.125 * (
-                work[k, i, pl.ds(HALO, half, stride=2), :]
-                + work[k, i, pl.ds(HALO + 1, half, stride=2), :]
-            )
-
-    reach = planes // 2 + 2
+
+    def halved(k, i, start, count):
+        return (
+            work[k, i, pl.ds(start, count, stride=2), :]
+            + work[k, i, pl.ds(start + 1, count, stride=2), :]
+        )
+
+    for i in range(coarse_planes):
+        for k in range(3):
+            own_coarse[k, i] = 0.125 * halved(k, i, first_row, half)
+
     for j in range(reach):
-        p = 2 * j + 2
-        work[0, j] = lane.pair(quarter[p] + quarter[p + 1])
-        coarse_q[j, pl.ds(6, ext_rows // 2), :] = (0.25 * 0.125) * (
-            work[0, j, pl.ds(0, ext_rows // 2, stride=2), :]
-            + work[0, j, pl.ds(1, ext_rows // 2, stride=2), :]
-        )
-    for i in range(planes // 2):
-        p = HALO + 2 * i
-        work[1, i] = lane.pair(shift[p] + shift[p + 1])
+        coarse_q[j, pl.ds(7, half + 2), :] = (0.25 * 0.125) * halved(3, j, first_row - 2, half + 2)
     lane1 = Lane(half, 2)
     shift1, q1 = [], []
-    for i in range(planes // 2):
-        s = 0.125 * (
-            work[1, i, pl.ds(HALO, half, stride=2), :]
-            + work[1, i, pl.ds(HALO + 1, half, stride=2), :]
-        )
+    for i in range(coarse_planes):
+        s = 0.125 * halved(4, i, first_row, half)
         sides = smooth_planes(lambda j: coarse_q[j, pl.ds(7, half), :], i + 1)
         here = smooth_planes(lambda j: coarse_q[j, pl.ds(8, half), :], i + 1)
         others = smooth_planes(lambda j: coarse_q[j, pl.ds(9, half), :], i + 1)
         q = coarse_q[i + 1, pl.ds(8, half), :]
         w = 24.0 * q + lane1.smooth(sides + 2.0 * here + others)
         own_coarse[3, i] = q
-        own_coarse[4, i] = w + s
+        own_coarse[4, i] = jnp.where(s > 0.0, w + s, 0.0)
         shift1.append(s)
         q1.append(q)
 
-    quarter_rows = half // 2
-    for i in range(planes // 4):
-        work[2, 0, pl.ds(0, half), :] = lane1.pair(q1[2 * i] + q1[2 * i + 1])
-        work[2, 1, pl.ds(0, half), :] = lane1.pair(shift1[2 * i] + shift1[2 * i + 1])
-        cells[0, i] = (0.25 * 0.125) * (
-            work[2, 0, pl.ds(0, quarter_rows, stride=2), :]
-            + work[2, 0, pl.ds(1, quarter_rows, stride=2), :]
-        )
-        cells[1, i] = 0.125 * (
-            work[2, 1, pl.ds(0, quarter_rows, stride=2), :]
-            + work[2, 1, pl.ds(1, quarter_rows, stride=2), :]
-        )
+    even = (lane_ids((half, LANES)) & 1) == 0
+    for k in range(5):
+        for i in range(coarse_planes // 2):
+            to_len[k, i] = jnp.where(even, own_coarse[k, 2 * i], own_coarse[k, 2 * i + 1])
+
+    for i in range(coarse_planes // 2):
+        for f, (values, scale) in enumerate(((q1, 0.25 * 0.125), (shift1, 0.125))):
+            work[f, i, pl.ds(0, half), :] = lane1.pair(values[2 * i] + values[2 * i + 1])
+            cells[f, i] = scale * (
+                work[f, i, pl.ds(HALO, rows // 4, stride=2), :]
+                + work[f, i, pl.ds(HALO + 1, rows // 4, stride=2), :]
+            )
 
 
 def middle_before(
-    own, cells, from_a, from_b, from_c, from_d,
+    own, cells, from_a, from_b,
     to_all, v2, source, quarter, weight, step,
     v1, work,
 ):
-    planes, rows = own.shape[1], own.shape[2]
-    ext_planes, ext_rows = planes + 2 * HALO, rows + 2 * HALO
+    planes, ext_rows = own.shape[1], own.shape[2]
+    rows = ext_rows - 2 * HALO
+    ext_planes = planes + 2 * HALO
     lane = Lane(ext_rows, 2)
 
-    def put(k, p, r, value):
+    def put(k, p, value):
         if k < 3:
-            source[k, p, r, :] = value
+            source[k, p] = value
         elif k == 3:
-            quarter[p, r, :] = value
+            quarter[p] = value
         else:
-            weight[p, r, :] = value
-
-    get = extended_rows(lambda k, p, r: own[k, p, r, :], from_a, from_b, planes, odd("len"))
-    spread_rows(get, from_c, from_d, planes, rows, put)
+            weight[p] = value
+
+    is_odd = odd("len")
+    even = (lane_ids((ext_rows, LANES)) & 1) == 0
+    for k in range(5):
+        for p in range(planes):
+            put(k, HALO + p, own[k, p])
+        for i in range(HALO // 2):
+            a, b = from_a[k, i], from_b[k, i]
+            for start, x in (
+                (0, jnp.where(is_odd, a, b)),
+                (HALO + planes, jnp.where(is_odd, b, a)),
+            ):
+                put(k, start + 2 * i, jnp.where(even, x, turn(x, 1, 1)))
+                put(k, start + 2 * i + 1, jnp.where(even, turn(x, -1, 1), x))
 
     for p in range(ext_planes):
         q, total = quarter[p], weight[p]
@@ -409,13 +479,13 @@
     half = rows // 2
     ids = lane_ids((half, LANES))
     mine = (ids & 3) == lax.broadcasted_iota(jnp.int32, (half, LANES), 0)
-    slots = 2 * to_all.shape[0] // (5 * (planes // 2))
+    lines = 5 * (planes // 2)
+    slots = to_all.shape[0] // lines
 
     def send(row, value):
         packed = jnp.sum(jnp.where(mine, value, 0.0), axis=0, keepdims=True)
         for s in range(slots):
-            at = s * (5 * (planes // 2)) + row
-            to_all[at // 2, at % 2 : at % 2 + 1, :] = packed
+            to_all[s * lines + row : s * lines + row + 1, :] = packed
 
     for p, _, r in defects(
         lambda k, p: v2[k, p], quarter, weight, source,
@@ -453,13 +523,17 @@
 ):
     brick = lax.axis_index("brick")
     slab = lax.axis_index("len")
-    slabs, bricks, lines = table.shape[0], table.shape[1], table.shape[2]
-    depth = lines // 5
-    planes2 = slabs * depth
+    bricks, planes2 = wide2.shape[2] - 16, wide2.shape[1] - 4
+    depth = (v2_mid.shape[1] - 2 * HALO) // 2
+    lines = 5 * depth
 
     def field(f):
         return jnp.stack(
-            [table[i // depth, :, f * depth + i % depth, :] for i in range(planes2)], axis=0
+            [
+                table[pl.ds((i // depth) * bricks * lines + f * depth + i % depth, bricks, stride=lines), :]
+                for i in range(planes2)
+            ],
+            axis=0,
         )
 
     lane2, lane3 = Packed(bricks, 1), Packed(bricks, 2)
@@ -483,6 +557,10 @@
     for k in range(3):
         wide2[k, pl.ds(2, planes2), pl.ds(8, bricks), :] = u2[k]
 
+    v2_fine, quarter_fine = From(v2_fine, 2), From(quarter_fine, 2)
+    source_fine, weight_fine, step_fine = [
+        From(x, 3) for x in (source_fine, weight_fine, step_fine)
+    ]
     planes1 = v2_mid.shape[1]
     rows1 = v2_mid.shape[2]
     lane1 = Lane(rows1, 2)
@@ -531,7 +609,7 @@
         range(3, planes1 - 3), bounds1, lane1, put_mid_last,
     )
 
-    planes0, rows0 = v2_fine.shape[1], v2_fine.shape[2]
+    planes0, rows0 = x_fine.shape[1], x_fine.shape[2]
     lane0 = Lane(rows0, 1)
     bounds0 = (0, planes0)
     half_rows = rows0 // 2
@@ -562,13 +640,14 @@
     )
 
 
-def call(kernel, outs, scratch=(), name=None):
+def call(kernel, outs, scratch=(), name=None, **more):
     return pl.pallas_call(
         kernel,
         out_shape=[jax.ShapeDtypeStruct(shape, F32) for shape in outs],
-        scratch_shapes=[vmem(shape) for shape in scratch],
-        compiler_params=pltpu.CompilerParams(vmem_limit_bytes=48 * 1024 * 1024),
+        scratch_shapes=[vmem(x) if isinstance(x, tuple) else x for x in scratch],
+        compiler_params=pltpu.CompilerParams(vmem_limit_bytes=40 * 1024 * 1024),
         name=name,
+        **more,
     )
 
 
@@ -583,46 +662,60 @@
 def body(forces, modulus, occupancy, bonded):
     planes, rows = modulus.shape[0], modulus.shape[1]
     slabs, bricks = lax.axis_size("len"), lax.axis_size("brick")
-    raw = (forces, modulus, occupancy, bonded)
-    ext, ext_rows = planes + 2 * HALO, rows + 2 * HALO
+    ext, ext_rows = planes + 2 * HALO, rows + 2 * WIDE
     half, half_rows = planes // 2, rows // 2
     mid, mid_rows = half + 2 * HALO, half_rows + 2 * HALO
 
-    side = (5, HALO, rows, LANES)
-    to_a, to_b = call(pack_planes, [side, side], name="pack_planes")(*raw)
-    from_a, from_b = swap(to_a, "len", 0), swap(to_b, "len", 1)
-    side = (5, ext, HALO, LANES)
-    to_c, to_d = call(pack_rows_fine, [side, side], name="pack_rows_fine")(*raw, from_a, from_b)
+    side, block = (row_spots(planes)[1], LANES), (planes, rows, LANES)
+    middle_side, corner = (middle_spots(rows)[1], LANES), (corner_spots()[1], LANES)
+    here = [
+        pltpu.with_memory_space_constraint(x, pltpu.HBM)
+        for x in (forces, modulus, occupancy, bonded)
+    ]
+    own, to_c, to_d, to_a, to_b = call(
+        pack_rows,
+        [(5,) + block, side, side, middle_side, middle_side],
+        [block, pltpu.VMEM(block, jnp.int32), pltpu.VMEM(block, jnp.int32)]
+        + [pltpu.SemaphoreType.DMA((4,))],
+        name="pack_rows",
+        in_specs=[pl.BlockSpec(memory_space=pltpu.HBM)] * 4,
+    )(*here)
     from_c, from_d = swap(to_c, "brick", 0), swap(to_d, "brick", 1)
+    middle_a, middle_b = swap(to_a, "len", 0), swap(to_b, "len", 1)
+    to_a, to_b = call(
+        functools.partial(pack_corners, planes),
+        [corner, corner],
+        name="pack_corners",
+        in_specs=[pl.BlockSpec(memory_space=pltpu.VMEM)] * 2
+        + [pl.BlockSpec(memory_space=pl.ANY)] * 2,
+    )(from_c, from_d, middle_a, middle_b)
+    corner_a, corner_b = swap(to_a, "len", 0), swap(to_b, "len", 1)
 
     field, cell = (3, ext, ext_rows, LANES), (ext, ext_rows, LANES)
-    own, cells, *fine = call(
+    line = (rows + 2 * HALO, LANES)
+    own, to_len, cells, *fine = call(
         fine_before,
-        [(5, half, half_rows, LANES), (2, half // 2, half_rows // 2, LANES)]
-        + [field, field, cell, cell, cell],
-        [cell, field, (3, half + 2, ext_rows, LANES), (half + 2, ext_rows, LANES)],
+        [(5, half, mid_rows, LANES), (5, half // 2, mid_rows, LANES)]
+        + [(2, half // 2, half_rows // 2, LANES)]
+        + [(3, ext - 4) + line, (3, ext - 6) + line, (ext - 4,) + line]
+        + [(ext - 6,) + line] * 2,
+        [field, field, cell, cell, cell, cell, field, (5, half + 2, ext_rows, LANES), (half + 2, mid_rows + 16, LANES)],
         name="fine_before",
-    )(*raw, from_a, from_b, from_c, from_d)
-
-    from_a, from_b = swap(own, "len", 0), swap(own, "len", 1)
-    side = (5, mid, HALO, LANES)
-    to_c, to_d = call(pack_rows_coarse, [side, side], name="pack_rows_coarse")(
-        own, from_a, from_b
-    )
-    from_c, from_d = swap(to_c, "brick", 0), swap(to_d, "brick", 1)
+    )(own, from_c, from_d, middle_a, middle_b, corner_a, corner_b)
+    from_a, from_b = swap(to_len, "len", 0), swap(to_len, "len", 1)
 
     field1, cell1 = (3, mid, mid_rows, LANES), (mid, mid_rows, LANES)
     depth = half // 2
     lines = 5 * depth
     to_all, *middle = call(
         middle_before,
-        [(slabs * bricks * lines // 2, 2, LANES)] + [field1, field1, cell1, cell1, cell1],
+        [(slabs * bricks * lines, LANES)] + [field1, field1, cell1, cell1, cell1],
         [field1, (3, depth, mid_rows, LANES)],
         name="middle_before",
-    )(own, cells, from_a, from_b, from_c, from_d)
-
-    table = lax.all_to_all(to_all, BOTH, 0, 0, tiled=True)
-    table = table.reshape(slabs, bricks, lines, LANES)
+    )(own, cells, from_a, from_b)
+
+    to_all = to_all.reshape(-1, 2, LANES)
+    table = lax.all_to_all(to_all, BOTH, 0, 0, tiled=True).reshape(-1, LANES)
     window = bricks if bricks <= 8 else 16
 
     def first_brick(brick):
@@ -630,13 +723,15 @@
 
     if window < bricks:
         table = lax.dynamic_slice_in_dim(
-            table, first_brick(lax.axis_index("brick")), window, axis=1
-        )
+            table.reshape(slabs, bricks * lines, LANES),
+            first_brick(lax.axis_index("brick")) * lines, window * lines, axis=1,
+        ).reshape(slabs * window * lines, LANES)
     planes2 = slabs * depth
     (out,) = call(
         functools.partial(coarse_and_after, first_brick),
         [forces.shape],
-        [(3, planes2 + 4, window + 16, LANES), field1, field1, field, field],
+        [(3, planes2 + 4, window + 16, LANES), field1, field1]
+        + [(3, ext, rows + 2 * HALO, LANES)] * 2,
         name="coarse_and_after",
     )(table, *middle, *fine)
     return out

time: 55.8 us -> 47.8 us (0.86)
  starting transfers between devices: 19.6 us -> 14 us
  local copies, waits for them, and re-layouts: 3.56 us -> 0 us
  blocking collectives: 17.7 us -> 14.8 us
  waiting for transfers between devices: 7.07 us -> 9.11 us
  Pallas kernels: 7.49 us -> 9.49 us
    ppermute x8, starting transfers between devices: 19.6 us -> 14 us  [swap(): return lax.ppermute(x, axis, pairs)]
    unnamed x8 -> x0, local copies, waits for them, and re-layouts: 3.44 us -> none
    all_to_all x1, blocking collectives: 17.7 us -> 14.8 us  [body(): table = lax.all_to_all(to_all, BOTH, 0, 0, tiled=True).reshape(-1, LANES)]
    ppermute x8, waiting for transfers between devices: 7.07 us -> 9.11 us  [swap(): return lax.ppermute(x, axis, pairs)]
    pallas_call x5 -> x4, Pallas kernels: 2.34 us -> 4.37 us  [the longest x1 2.4 us: body(): call(fine_before, [(5, half, mid_rows, LANES), (5, half // 2, mid_rows, L...]
where the time goes in v3:
time: 47.8 us; the launch traced here: 47.6 us
  blocking collectives  14.8 us (31%)
  starting transfers between devices  14 us (29%)
  Pallas kernels  9.49 us (20%)
  waiting for transfers between devices  9.11 us (19%)
    all_to_all x1, blocking collectives, body(): table = lax.all_to_all(to_all, BOTH, 0, 0, tiled=True).reshape(-1, LANES)  14.8 us
    ppermute x8, starting transfers between devices, swap(): return lax.ppermute(x, axis, pairs)  14 us
    ppermute x8, waiting for transfers between devices, swap(): return lax.ppermute(x, axis, pairs)  9.11 us
    pallas_call x1, Pallas kernels, body(): call(functools.partial(coarse_and_after, first_brick), [forces.shape], [(...  5.12 us
    pallas_call x1, Pallas kernels, body(): call(fine_before, [(5, half, mid_rows, LANES), (5, half // 2, mid_rows, L...  2.4 us
    pallas_call x1, Pallas kernels, body(): call(pack_rows, [(5,) + block, side, side, middle_side, middle_side], [bl...  1.14 us
  transfers between devices with their start and end apart: 8, of which 4 were waited for; matrix products, arithmetic and copies ran while one was open for 0% of the time, Pallas kernels for 0%

profile of v3, /device:TPU:0, one launch (start us, length us, event | category | flops | bytes accessed | tf_op | source)
XLA Modules:
  0.0 47.6 jit_solution(5285725790313667434)
XLA Ops:
  0.0 1.1 %pack_rows.1 = (f32[5,8,16,128]{3,2,1,0:T(8,128)S(1)}, f32[408,128]{1,0:T(8,128)S(1)}, f32[408,128]{1,0:T(8,128)S(1)}, f32[256,128]{1,0:T(8,128)S(1)}, f32[256,128]{1,0:T(8,128)S(1)}) custom-call(f32[3,8,16,128]{3,2,1,0:T(8,128)} %forces.1, f32[8,16,128]{2,1,0:T(8,128)} %modulus.1, s32[8,16,128]{2,1,0:T(8,128)} %occupancy.1, s32[8,16,128]{2,1,0:T(8,128)} %bonded.1), custom_call_target="tpu_custom_call" | custom-call | tf_op jit(solution)/shard_map/pack_rows/pallas_call | solution.py:675
  1.1 3.0 %collective-permute-start = (f32[408,128]{1,0:T(8,128)S(1)}, f32[408,128]{1,0:T(8,128)S(1)}, u32[]{:S(2)}, u32[]{:S(2)}) collective-permute-start(f32[408,128]{1,0:T(8,128)S(1)} %get-tuple-element.27), channel_id=1, source_target_pairs={{0,1},{1,0},{2,3},{3,2},{4,5},{5,4},{6,7},{7,6},{8,9},{9,8},{10,11... | collective-permute-start | bytes 626696 | tf_op jit(solution)/shard_map/ppermute | solution.py:659
  4.2 0.7 %collective-permute-start.1 = (f32[408,128]{1,0:T(8,128)S(1)}, f32[408,128]{1,0:T(8,128)S(1)}, u32[]{:S(2)}, u32[]{:S(2)}) collective-permute-start(f32[408,128]{1,0:T(8,128)S(1)} %get-tuple-element.28), channel_id=1, source_target_pairs={{1,2},{2,1},{3,4},{4,3},{5,6},{6,5},{9,10},{10,9},{11,12},{12,11},... | collective-permute-start | bytes 626696 | tf_op jit(solution)/shard_map/ppermute | solution.py:659
  4.8 0.1 collective-permute-start.2
  4.9 0.7 %collective-permute-start.3 = (f32[256,128]{1,0:T(8,128)S(1)}, f32[256,128]{1,0:T(8,128)S(1)}, u32[]{:S(2)}, u32[]{:S(2)}) collective-permute-start(f32[256,128]{1,0:T(8,128)S(1)} %get-tuple-element.30), channel_id=1, source_target_pairs={{8,16},{16,8},{9,17},{17,9},{10,18},{18,10},{11,19},{19,11},{12,20... | collective-permute-start | bytes 393224 | tf_op jit(solution)/shard_map/ppermute | solution.py:659
  5.6 0.7 %collective-permute-done.2.middle_a = f32[256,128]{1,0:T(8,128)S(1)} collective-permute-done((f32[256,128]{1,0:T(8,128)S(1)}, f32[256,128]{1,0:T(8,128)S(1)}, u32[]{:S(2)}, u32[]{:S(2)}) %collective-permute-start.2) | collective-permute-done | bytes 131104 | tf_op jit(solution)/shard_map/ppermute | solution.py:659
  6.3 0.0 collective-permute-done.3.middle_b
  6.3 6.8 %collective-permute-done.from_c = f32[408,128]{1,0:T(8,128)S(1)} collective-permute-done((f32[408,128]{1,0:T(8,128)S(1)}, f32[408,128]{1,0:T(8,128)S(1)}, u32[]{:S(2)}, u32[]{:S(2)}) %collective-permute-start) | collective-permute-done | bytes 208928 | tf_op jit(solution)/shard_map/ppermute | solution.py:659
  13.1 0.0 collective-permute-done.1.from_d
  13.1 0.1 pack_corners.1
  13.1 0.1 collective-permute-start.4
  13.2 0.7 %collective-permute-start.5 = (f32[328,128]{1,0:T(8,128)S(1)}, f32[328,128]{1,0:T(8,128)S(1)}, u32[]{:S(2)}, u32[]{:S(2)}) collective-permute-start(f32[328,128]{1,0:T(8,128)S(1)} %get-tuple-element.32), channel_id=1, source_target_pairs={{8,16},{16,8},{9,17},{17,9},{10,18},{18,10},{11,19},{19,11},{12,20... | collective-permute-start | bytes 503816 | tf_op jit(solution)/shard_map/ppermute | solution.py:659
  13.9 0.7 %collective-permute-done.4.corner_a = f32[328,128]{1,0:T(8,128)S(1)} collective-permute-done((f32[328,128]{1,0:T(8,128)S(1)}, f32[328,128]{1,0:T(8,128)S(1)}, u32[]{:S(2)}, u32[]{:S(2)}) %collective-permute-start.4) | collective-permute-done | bytes 167968 | tf_op jit(solution)/shard_map/ppermute | solution.py:659
  14.6 0.0 collective-permute-done.5.corner_b
  14.6 2.4 %fine_before.1 = (f32[5,4,16,128]{3,2,1,0:T(8,128)S(1)}, f32[5,2,16,128]{3,2,1,0:T(8,128)S(1)}, f32[2,2,4,128]{3,2,1,0:T(4,128)S(1)}, f32[3,12,24,128]{3,2,1,0:T...) custom-call(f32[5,8,16,128]{3,2,1,0:T(8,128)S(1)} %get-tuple-element, ...), custom_call_target="tpu_custom_call" | custom-call | tf_op jit(solution)/shard_map/fine_before/pallas_call | solution.py:696
  17.0 0.7 %collective-permute-start.7 = (f32[5,2,16,128]{3,2,1,0:T(8,128)S(1)}, f32[5,2,16,128]{3,2,1,0:T(8,128)S(1)}, u32[]{:S(2)}, u32[]{:S(2)}) collective-permute-start(f32[5,2,16,128]{3,2,1,0:T(8,128)S(1)} %get-tuple-element.35), channel_id=1, source_target_pairs={{8,16},{16,8},{9,17},{17,9},{10,18},{18,10},{11,19},{19,11},{12,20... | collective-permute-start | bytes 245768 | tf_op jit(solution)/shard_map/ppermute | solution.py:659
  17.7 8.2 %collective-permute-start.6 = (f32[5,2,16,128]{3,2,1,0:T(8,128)S(1)}, f32[5,2,16,128]{3,2,1,0:T(8,128)S(1)}, u32[]{:S(2)}, u32[]{:S(2)}) collective-permute-start(f32[5,2,16,128]{3,2,1,0:T(8,128)S(1)} %get-tuple-element.35), channel_id=1, source_target_pairs={{0,8},{8,0},{16,24},{24,16},{1,9},{9,1},{17,25},{25,17},{2,10},{10... | collective-permute-start | bytes 245768 | tf_op jit(solution)/shard_map/ppermute | solution.py:659
  25.9 0.0 collective-permute-done.7.from_b
  25.9 0.9 %collective-permute-done.6.from_a = f32[5,2,16,128]{3,2,1,0:T(8,128)S(1)} collective-permute-done((f32[5,2,16,128]{3,2,1,0:T(8,128)S(1)}, f32[5,2,16,128]{3,2,1,0:T(8,128)S(1)}, u32[]{:S(2)}, u32[]{:S(2)}) %collective-permute-start.6) | collective-permute-done | bytes 81952 | tf_op jit(solution)/shard_map/ppermute | solution.py:659
  26.8 0.8 %middle_before.1 = (f32[320,128]{1,0:T(8,128)S(1)}, f32[3,12,16,128]{3,2,1,0:T(8,128)S(1)}, f32[3,12,16,128]{3,2,1,0:T(8,128)S(1)}, f32[12,16,128]{2,1,0:T(8,128...) custom-call(f32[5,4,16,128]{3,2,1,0:T(8,128)S(1)} %get-tuple-element.33.own, ...), custom_call_target="tpu_custom_call" | custom-call | tf_op jit(solution)/shard_map/middle_before/pallas_call | solution.py:710
  27.6 14.8 %all_to_all.5 = f32[160,2,128]{2,1,0:T(2,128)S(1)} all-to-all(f32[160,2,128]{2,1,0:T(2,128)S(1)} %bitcast.3), channel_id=1, replica_groups=mesh['len'=4,'brick'=8] {'len','brick'}, dimensions={0} | all-to-all | bytes 327680 | tf_op jit(solution)/shard_map/all_to_all | solution.py:718
  42.4 5.1 %coarse_and_after.1 = f32[3,8,16,128]{3,2,1,0:T(8,128)} custom-call(f32[320,128]{1,0:T(8,128)S(1)} %bitcast.2, f32[3,12,16,128]{3,2,1,0:T(8,128)S(1)} %get-tuple-element.37.v2_mid, f32[3,12,16,128]{3,2,1,0:T(8,128)S(1)} %get-tuple-element.38.source_mid, f32[12,16,128]{2,1,0:T(8,128)S(1)} %get-tuple-element.39.quarter_mid, ...), custom_call_target="tpu_custom_call" | custom-call | tf_op jit(solution)/shard_map/coarse_and_after/pallas_call | solution.py:730
Async XLA Ops:
  1.1 11.9 %collective-permute-start = (f32[408,128]{1,0:T(8,128)S(1)}, f32[408,128]{1,0:T(8,128)S(1)}, u32[]{:S(2)}, u32[]{:S(2)}) collective-permute-start(f32[408,128]{1,0:T(8,128)S(1)} %get-tuple-element.27), channel_id=1, source_target_pairs={{0,1},{1,0},{2,3},{3,2},{4,5},{5,4},{6,7},{7,6},{8,9},{9,8},{10,11... | collective-permute-start | bytes 626696 | tf_op jit(solution)/shard_map/ppermute | solution.py:659
  4.2 8.9 %collective-permute-start.1 = (f32[408,128]{1,0:T(8,128)S(1)}, f32[408,128]{1,0:T(8,128)S(1)}, u32[]{:S(2)}, u32[]{:S(2)}) collective-permute-start(f32[408,128]{1,0:T(8,128)S(1)} %get-tuple-element.28), channel_id=1, source_target_pairs={{1,2},{2,1},{3,4},{4,3},{5,6},{6,5},{9,10},{10,9},{11,12},{12,11},... | collective-permute-start | bytes 626696 | tf_op jit(solution)/shard_map/ppermute | solution.py:659
  4.8 1.4 %collective-permute-start.2 = (f32[256,128]{1,0:T(8,128)S(1)}, f32[256,128]{1,0:T(8,128)S(1)}, u32[]{:S(2)}, u32[]{:S(2)}) collective-permute-start(f32[256,128]{1,0:T(8,128)S(1)} %get-tuple-element.29), channel_id=1, source_target_pairs={{0,8},{8,0},{16,24},{24,16},{1,9},{9,1},{17,25},{25,17},{2,10},{10... | collective-permute-start | bytes 393224 | tf_op jit(solution)/shard_map/ppermute | solution.py:659
  4.9 1.3 %collective-permute-start.3 = (f32[256,128]{1,0:T(8,128)S(1)}, f32[256,128]{1,0:T(8,128)S(1)}, u32[]{:S(2)}, u32[]{:S(2)}) collective-permute-start(f32[256,128]{1,0:T(8,128)S(1)} %get-tuple-element.30), channel_id=1, source_target_pairs={{8,16},{16,8},{9,17},{17,9},{10,18},{18,10},{11,19},{19,11},{12,20... | collective-permute-start | bytes 393224 | tf_op jit(solution)/shard_map/ppermute | solution.py:659
  13.1 1.5 %collective-permute-start.4 = (f32[328,128]{1,0:T(8,128)S(1)}, f32[328,128]{1,0:T(8,128)S(1)}, u32[]{:S(2)}, u32[]{:S(2)}) collective-permute-start(f32[328,128]{1,0:T(8,128)S(1)} %get-tuple-element.31), channel_id=1, source_target_pairs={{0,8},{8,0},{16,24},{24,16},{1,9},{9,1},{17,25},{25,17},{2,10},{10... | collective-permute-start | bytes 503816 | tf_op jit(solution)/shard_map/ppermute | solution.py:659
  13.2 1.4 %collective-permute-start.5 = (f32[328,128]{1,0:T(8,128)S(1)}, f32[328,128]{1,0:T(8,128)S(1)}, u32[]{:S(2)}, u32[]{:S(2)}) collective-permute-start(f32[328,128]{1,0:T(8,128)S(1)} %get-tuple-element.32), channel_id=1, source_target_pairs={{8,16},{16,8},{9,17},{17,9},{10,18},{18,10},{11,19},{19,11},{12,20... | collective-permute-start | bytes 503816 | tf_op jit(solution)/shard_map/ppermute | solution.py:659
  17.0 8.9 %collective-permute-start.7 = (f32[5,2,16,128]{3,2,1,0:T(8,128)S(1)}, f32[5,2,16,128]{3,2,1,0:T(8,128)S(1)}, u32[]{:S(2)}, u32[]{:S(2)}) collective-permute-start(f32[5,2,16,128]{3,2,1,0:T(8,128)S(1)} %get-tuple-element.35), channel_id=1, source_target_pairs={{8,16},{16,8},{9,17},{17,9},{10,18},{18,10},{11,19},{19,11},{12,20... | collective-permute-start | bytes 245768 | tf_op jit(solution)/shard_map/ppermute | solution.py:659
  17.7 9.1 %collective-permute-start.6 = (f32[5,2,16,128]{3,2,1,0:T(8,128)S(1)}, f32[5,2,16,128]{3,2,1,0:T(8,128)S(1)}, u32[]{:S(2)}, u32[]{:S(2)}) collective-permute-start(f32[5,2,16,128]{3,2,1,0:T(8,128)S(1)} %get-tuple-element.35), channel_id=1, source_target_pairs={{0,8},{8,0},{16,24},{24,16},{1,9},{9,1},{17,25},{25,17},{2,10},{10... | collective-permute-start | bytes 245768 | tf_op jit(solution)/shard_map/ppermute | solution.py:659

commit v4 on v3

--- a/solution.py
+++ b/solution.py
@@ -17,6 +17,7 @@
 ROWS = (10, 10, 10, 11, 10)
 PLANES = (3, 3, 3, 4, 3)
 LANES = 128
+ROW = 32
 F32 = jnp.float32
 BOTH = ("len", "brick")
 
@@ -27,6 +28,10 @@
 
 def turn(x, by, axis):
     return pltpu.roll(x, by % x.shape[axis], axis)
+
+
+def pick(x, lanes):
+    return jnp.take_along_axis(x, lanes, axis=1, mode="promise_in_bounds")
 
 
 class Lane:
@@ -57,35 +62,31 @@
         shape = (1, bricks, LANES)
         ids = lane_ids(shape)
         line = lax.broadcasted_iota(jnp.int32, shape, 1)
-        self.wide, self.across = wide, 4 * wide
-        row = ids & (4 - wide)
-        top, bottom = row == 0, row == 4 - wide
+        self.wide = wide
+        top, bottom = ids < ROW * wide, ids >= LANES - ROW * wide
 
         def number(mask, value):
             return jnp.where(mask, value, 0.0).astype(F32)
 
-        self.low = number(ids >= self.across, 0.5)
-        self.high = number(ids < LANES - self.across, 0.5)
+        self.low = number((ids & (ROW - 1)) >= wide, 0.5)
+        self.high = number((ids & (ROW - 1)) < ROW - wide, 0.5)
         self.not_top, self.not_bottom = number(~top, 1.0), number(~bottom, 1.0)
         self.top = number(top & (line > 0), 1.0)
         self.bottom = number(bottom & (line < bricks - 1), 1.0)
-        self.odd_row, self.odd_lane = number((ids & 1) > 0, 1.0), number((ids & 4) > 0, 1.0)
+        self.odd_row, self.odd_lane = number((ids & ROW) > 0, 1.0), number((ids & 1) > 0, 1.0)
 
     def smooth(self, x):
-        return x + (self.low * turn(x, self.across, 2) + self.high * turn(x, -self.across, 2))
+        return x + (self.low * turn(x, self.wide, 2) + self.high * turn(x, -self.wide, 2))
 
     def rows(self, x):
-        back, ahead = turn(x, self.wide, 2), turn(x, -self.wide, 2)
-        if self.wide == 2:
-            far_back, far_ahead = ahead, back
-        else:
-            far_back, far_ahead = turn(x, -3, 2), turn(x, 3, 2)
-        before = self.not_top * back + self.top * turn(far_back, 1, 1)
-        after = self.not_bottom * ahead + self.bottom * turn(far_ahead, -1, 1)
+        back = turn(x, ROW * self.wide, 2)
+        ahead = back if self.wide == 2 else turn(x, -ROW, 2)
+        before = self.not_top * back + self.top * turn(back, 1, 1)
+        after = self.not_bottom * ahead + self.bottom * turn(ahead, -1, 1)
         return (x + x) + (before + after)
 
     def pair(self, x):
-        for by, is_odd in ((1, self.odd_row), (4, self.odd_lane)):
+        for by, is_odd in ((ROW, self.odd_row), (1, self.odd_lane)):
             x = x + (is_odd * turn(x, by, 2) + (1.0 - is_odd) * turn(x, -by, 2))
         return x
 
@@ -205,6 +206,15 @@
         return self.ref[at - self.first]
 
 
+class Either:
+    def __init__(self, inner, span, outer):
+        self.inner, self.span, self.outer = From(inner, span[0]), span, outer
+
+    def __getitem__(self, at):
+        p = at[1] if isinstance(at, tuple) else at
+        return self.inner[at] if p in self.span else self.outer[at]
+
+
 def vmem(shape):
     return pltpu.VMEM(shape, F32)
 
@@ -232,7 +242,13 @@
 
 
 def corner_spots():
-    return plane_spots([2 * reach for reach in ROWS])
+    spots, at = {}, 0
+    for k, count in enumerate(PLANES):
+        for distance in range(1, count + 1):
+            reach = ROWS[k] if distance < count else count
+            spots[k, distance] = at, reach
+            at += 2 * reach
+    return spots, at
 
 
 def pack_rows(
@@ -275,36 +291,42 @@
 def rows_beside(from_c, from_d):
     is_odd = odd("brick")
 
-    def get(spot):
-        c, d = from_c[spot, :], from_d[spot, :]
-        return jnp.where(is_odd, c, d), jnp.where(is_odd, d, c)
+    def get(spot, reach):
+        low, high = slice(spot.stop - reach, spot.stop), slice(spot.start, spot.start + reach)
+        return (
+            jnp.where(is_odd, from_c[low, :], from_d[low, :]),
+            jnp.where(is_odd, from_d[high, :], from_c[high, :]),
+        )
 
     return get
 
 
-def pack_corners(planes, from_c, from_d, middle_a, middle_b, to_a, to_b):
+def pack_corners(planes, from_c, middle_b, from_d, middle_a, to_a, to_b):
     del middle_a, middle_b
     is_odd = odd("len")
     from_rows, _ = row_spots(planes)
     beside = rows_beside(from_c, from_d)
-    for (k, i), spot in corner_spots()[0].items():
-        firsts = beside(from_rows[k, i])
-        lasts = beside(from_rows[k, planes - PLANES[k] + i])
+    for (k, distance), (at, reach) in corner_spots()[0].items():
+        firsts = beside(from_rows[k, distance - 1], reach)
+        lasts = beside(from_rows[k, planes - distance], reach)
         for half, (first, last) in enumerate(zip(firsts, lasts)):
-            start = spot.start + half * ROWS[k]
-            span = slice(start, start + ROWS[k])
+            span = slice(at + half * reach, at + (half + 1) * reach)
             to_a[span, :] = jnp.where(is_odd, first, last)
             to_b[span, :] = jnp.where(is_odd, last, first)
 
 
-def fine_before(
-    own, from_c, from_d, middle_a, middle_b, corner_a, corner_b,
-    own_coarse, to_len, cells, v2_kept, source_kept, quarter_kept, weight_kept, step_kept,
-    v2, source, quarter, weight, step, shift, v1, work, coarse_q,
+def inner_planes(planes):
+    return [range(HALO + i, HALO + planes - i) for i in (1, 2, 3)]
+
+
+def fine_inner(
+    own, from_c, from_d, to_a,
+    source, quarter, shift, weight, step, v1, v2, rest,
 ):
+    del to_a
     planes, rows = own.shape[1], own.shape[2]
-    ext_planes, ext_rows = planes + 2 * HALO, rows + 2 * WIDE
-    lane = Lane(ext_rows, 1)
+    lane = Lane(rows + 2 * WIDE, 1)
+    beside = rows_beside(from_c, from_d)
 
     def put(k, p, r, value):
         if k < 3:
@@ -314,70 +336,124 @@
         else:
             shift[p, r, :] = value
 
-    beside = rows_beside(from_c, from_d)
     for (k, p), spot in row_spots(planes)[0].items():
-        low, high = beside(spot)
-        put(k, HALO + p, slice(WIDE - ROWS[k], WIDE), low)
-        put(k, HALO + p, slice(WIDE, WIDE + rows), own[k, p])
-        put(k, HALO + p, slice(WIDE + rows, WIDE + rows + ROWS[k]), high)
+        low, high = beside(spot, ROWS[k])
+        put(k, p, slice(WIDE - ROWS[k], WIDE), low)
+        put(k, p, slice(WIDE, WIDE + rows), own[k, p])
+        put(k, p, slice(WIDE + rows, WIDE + rows + ROWS[k]), high)
+
+    weighed, swept, left = inner_planes(planes)
+    bounds = (HALO, HALO + planes)
+    source_at, quarter_at = From(source, HALO), From(quarter, HALO)
+    for p, w in stiffness_sum(quarter_at, weighed, bounds, lane):
+        q, s, i = quarter_at[p], shift[p - HALO], p - weighed[0]
+        total = w + s
+        weight[i] = total + 8.0 * q
+        st = step_of(s, total + (4.0 * COUPLING) * q)
+        step[i] = st
+        for k in range(3):
+            v1[k, i] = st * source_at[k, p]
+    weight_at, step_at = From(weight, weighed[0]), From(step, weighed[0])
+
+    def put_v2(k, p, value):
+        v2[k, p - swept[0]] = value
+
+    v1_at, v2_at = From(v1, weighed[0]), From(v2, swept[0])
+    sweep(
+        lambda k, p: v1_at[k, p], quarter_at, weight_at, step_at, source_at,
+        swept, (weighed[0], weighed[-1] + 1), lane, put_v2,
+    )
+    for p, _, r in defects(
+        lambda k, p: v2_at[k, p], quarter_at, weight_at, source_at,
+        left, (swept[0], swept[-1] + 1), lane,
+    ):
+        for k in range(3):
+            rest[k, p - left[0]] = r[k]
+
+
+def fine_before(
+    source_in, quarter_in, shift_in, weight_in, step_in, v1_in, v2_in, rest_in,
+    middle_b, middle_a, corner_b, corner_a,
+    own_coarse, to_len, cells, v2_kept, source_kept, quarter_kept, weight_kept, step_kept,
+    v2_out, source_out, quarter_out, weight_out, step_out, shift_out, v1_out, work, coarse_q,
+):
+    planes, ext_rows = quarter_in.shape[0], quarter_in.shape[1]
+    ext_planes, rows = planes + 2 * HALO, ext_rows - 2 * WIDE
+    lane = Lane(ext_rows, 1)
+
+    def put(k, p, r, value):
+        if k < 3:
+            source_out[k, p, r, :] = value
+        elif k == 3:
+            quarter_out[p, r, :] = 0.25 * value
+        else:
+            shift_out[p, r, :] = value
+
     is_odd = odd("len")
+    def put_both(k, distance, start, low, high):
+        r = slice(start, start + low.shape[0])
+        put(k, HALO - distance, r, low)
+        put(k, HALO + planes - 1 + distance, r, high)
+
+    def sides(a, b):
+        return jnp.where(is_odd, a, b), jnp.where(is_odd, b, a)
+
+    spots = middle_spots(rows)[0]
+    for k, count in enumerate(PLANES):
+        for distance in range(1, count + 1):
+            low = sides(*[x[spots[k, count - distance], :] for x in (middle_a, middle_b)])[0]
+            high = sides(*[x[spots[k, distance - 1], :] for x in (middle_a, middle_b)])[1]
+            put_both(k, distance, WIDE, low, high)
+    for (k, distance), (at, reach) in corner_spots()[0].items():
+        for half, start in enumerate((WIDE - reach, WIDE + rows)):
+            span = slice(at + half * reach, at + (half + 1) * reach)
+            put_both(k, distance, start, *sides(corner_a[span, :], corner_b[span, :]))
+
+    weighed, swept, left = inner_planes(planes)
+    here = range(HALO, HALO + planes)
+    source, quarter, shift = [
+        Either(x, here, y)
+        for x, y in ((source_in, source_out), (quarter_in, quarter_out), (shift_in, shift_out))
+    ]
+    weight, step, v1 = [
+        Either(x, weighed, y)
+        for x, y in ((weight_in, weight_out), (step_in, step_out), (v1_in, v1_out))
+    ]
+    v2 = Either(v2_in, swept, v2_out)
     kept = slice(WIDE - HALO, WIDE + rows + HALO)
-    corners = corner_spots()[0]
-    for (k, i), spot in middle_spots(rows)[0].items():
-        reach, corner = ROWS[k], corners[k, i].start
-        for start, a, b in (
-            (WIDE - reach, corner_a[corner : corner + reach, :], corner_b[corner : corner + reach, :]),
-            (WIDE, middle_a[spot, :], middle_b[spot, :]),
-            (
-                WIDE + rows,
-                corner_a[corner + reach : corner + 2 * reach, :],
-                corner_b[corner + reach : corner + 2 * reach, :],
-            ),
-        ):
-            r = slice(start, start + a.shape[0])
-            put(k, HALO - PLANES[k] + i, r, jnp.where(is_odd, a, b))
-            put(k, HALO + planes + i, r, jnp.where(is_odd, b, a))
 
     bounds = (0, ext_planes)
-    for p, w in stiffness_sum(quarter, range(1, ext_planes - 1), bounds, lane):
+    others = [p for p in range(1, ext_planes - 1) if p not in weighed]
+    for p, w in stiffness_sum(quarter, others, bounds, lane):
         q, s = quarter[p], shift[p]
         total = w + s
-        weight[p] = total + 8.0 * q
+        weight_out[p] = total + 8.0 * q
         st = step_of(s, total + (4.0 * COUPLING) * q)
-        step[p] = st
-        for k in range(3):
-            v1[k, p] = st * source[k, p]
-        if 2 <= p < ext_planes - 2:
-            quarter_kept[p - 2] = q[kept]
-        if 3 <= p < ext_planes - 3:
-            weight_kept[p - 3] = weight[p, kept, :]
-            step_kept[p - 3] = st[kept]
-            for k in range(3):
-                source_kept[k, p - 3] = source[k, p, kept, :]
+        step_out[p] = st
+        for k in range(3):
+            v1_out[k, p] = st * source[k, p]
 
     def put_v2(k, p, value):
-        v2[k, p] = value
-        v2_kept[k, p - 2] = value[kept]
+        v2_out[k, p] = value
 
     sweep(
         lambda k, p: v1[k, p], quarter, weight, step, source,
-        range(2, ext_planes - 2), bounds, lane, put_v2,
+        [p for p in range(2, ext_planes - 2) if p not in swept], bounds, lane, put_v2,
     )
 
-    held = {}
     half = rows // 2 + 2 * HALO
     first_row = WIDE - 2 * HALO
     coarse_planes = planes // 2
+    rest = {p: [rest_in[k, p - left[0]] for k in range(3)] for p in left}
     for p, _, r in defects(
         lambda k, p: v2[k, p], quarter, weight, source,
-        range(HALO, HALO + planes), bounds, lane,
+        [p for p in here if p not in left], bounds, lane,
     ):
-        if p % 2 == 0:
-            held = r
-            continue
-        i = (p - HALO) // 2
-        for k in range(3):
-            work[k, i] = held[k] + r[k]
+        rest[p] = r
+    for i in range(coarse_planes):
+        p = HALO + 2 * i
+        for k in range(3):
+            work[k, i] = rest[p][k] + rest[p + 1][k]
     for i in range(coarse_planes):
         work[4, i] = shift[HALO + 2 * i] + shift[HALO + 2 * i + 1]
     reach = coarse_planes + 2
@@ -426,6 +502,15 @@
                 + work[f, i, pl.ds(HALO + 1, rows // 4, stride=2), :]
             )
 
+    for p in range(2, ext_planes - 2):
+        quarter_kept[p - 2] = quarter[p][kept]
+        for k in range(3):
+            v2_kept[k, p - 2] = v2[k, p][kept]
+    for p in range(3, ext_planes - 3):
+        weight_kept[p - 3], step_kept[p - 3] = weight[p][kept], step[p][kept]
+        for k in range(3):
+            source_kept[k, p - 3] = source[k, p][kept]
+
 
 def middle_before(
     own, cells, from_a, from_b,
@@ -477,16 +562,6 @@
     )
     held = {}
     half = rows // 2
-    ids = lane_ids((half, LANES))
-    mine = (ids & 3) == lax.broadcasted_iota(jnp.int32, (half, LANES), 0)
-    lines = 5 * (planes // 2)
-    slots = to_all.shape[0] // lines
-
-    def send(row, value):
-        packed = jnp.sum(jnp.where(mine, value, 0.0), axis=0, keepdims=True)
-        for s in range(slots):
-            to_all[s * lines + row : s * lines + row + 1, :] = packed
-
     for p, _, r in defects(
         lambda k, p: v2[k, p], quarter, weight, source,
         range(HALO, HALO + planes), bounds, lane,
@@ -500,18 +575,31 @@
     for i in range(planes // 2):
         for k in range(3):
             work[k, i] = lane.pair(work[k, i])
-    for i in range(planes // 2):
-        for k in range(3):
-            send(
-                k * (planes // 2) + i,
-                0.125
-                * (
-                    work[k, i, pl.ds(HALO, half, stride=2), :]
-                    + work[k, i, pl.ds(HALO + 1, half, stride=2), :]
-                ),
+    depth = planes // 2
+    ids = lane_ids((depth * half, LANES))
+    row = lax.broadcasted_iota(jnp.int32, ids.shape, 0)
+    mine = ids // ROW == row % half
+    lines = []
+    for k in range(5):
+        parts = [
+            cells[k - 3, i]
+            if k >= 3
+            else 0.125
+            * (
+                work[k, i, pl.ds(HALO, half, stride=2), :]
+                + work[k, i, pl.ds(HALO + 1, half, stride=2), :]
             )
-        for k in range(2):
-            send((3 + k) * (planes // 2) + i, cells[k, i])
+            for i in range(depth)
+        ]
+        x = pick(jnp.concatenate(parts, axis=0), (ids % ROW) * (LANES // ROW))
+        x = jnp.where(mine, x, 0.0)
+        x = x + turn(x, -1, 0)
+        x = x + turn(x, -2, 0)
+        lines += [x[i * half : i * half + 1] for i in range(depth)]
+    block = jnp.concatenate(lines * 4, axis=0)
+    count = block.shape[0]
+    for at in range(0, to_all.shape[0], count):
+        to_all[at : at + count, :] = block
 
 
 def coarse_and_after(
@@ -568,8 +656,7 @@
     line_at = brick - bricks_before(brick) + 8
     half_shape = (rows1 // 2, LANES)
     ids, row = lane_ids(half_shape), lax.broadcasted_iota(jnp.int32, half_shape, 0)
-    mine = (ids & 3) == ((row + 2) & 3)
-    pieces = []
+    lanes = ROW * ((row + 2) % 4) + ids // (LANES // ROW)
     for k in range(3):
         for i in range(planes1 // 2):
             low, own, high = [
@@ -578,14 +665,7 @@
                 )
                 for at in (-1, 0, 1)
             ]
-            piece = jnp.where(row < 2, low, jnp.where(row < 6, own, high))
-            pieces.append(jnp.where(mine, piece, 0.0))
-    for by in (1, 2):
-        first = (ids & by) == 0
-        pieces = [x + swap_lanes(x, by, first) for x in pieces]
-    for k in range(3):
-        for i in range(planes1 // 2):
-            piece = pieces[k * (planes1 // 2) + i]
+            piece = pick(jnp.where(row < 2, low, jnp.where(row < 6, own, high)), lanes)
             for half in range(2):
                 x_mid[k, i, pl.ds(half, rows1 // 2, stride=2), :] = piece
             both = x_mid[k, i]
@@ -680,29 +760,44 @@
         name="pack_rows",
         in_specs=[pl.BlockSpec(memory_space=pltpu.HBM)] * 4,
     )(*here)
-    from_c, from_d = swap(to_c, "brick", 0), swap(to_d, "brick", 1)
-    middle_a, middle_b = swap(to_a, "len", 0), swap(to_b, "len", 1)
+    from_c = swap(to_c, "brick", 0)
+    middle_b = swap(to_b, "len", 1)
+    from_d = swap(to_d, "brick", 1)
+    middle_a = swap(to_a, "len", 0)
     to_a, to_b = call(
         functools.partial(pack_corners, planes),
         [corner, corner],
         name="pack_corners",
-        in_specs=[pl.BlockSpec(memory_space=pltpu.VMEM)] * 2
-        + [pl.BlockSpec(memory_space=pl.ANY)] * 2,
-    )(from_c, from_d, middle_a, middle_b)
-    corner_a, corner_b = swap(to_a, "len", 0), swap(to_b, "len", 1)
+        in_specs=[pl.BlockSpec(memory_space=x) for x in (pltpu.VMEM, pl.ANY) * 2],
+    )(from_c, middle_b, from_d, middle_a)
+    corner_b = swap(to_b, "len", 1)
+    corner_a = swap(to_a, "len", 0)
 
     field, cell = (3, ext, ext_rows, LANES), (ext, ext_rows, LANES)
     line = (rows + 2 * HALO, LANES)
+    block = (planes, ext_rows, LANES)
+    weighed, swept, left = [(len(x), ext_rows, LANES) for x in inner_planes(planes)]
+    inner = call(
+        fine_inner,
+        [(3,) + block, block, block, weighed, weighed]
+        + [(3,) + weighed, (3,) + swept, (3,) + left],
+        name="fine_inner",
+        in_specs=[pl.BlockSpec(memory_space=pltpu.VMEM)] * 3
+        + [pl.BlockSpec(memory_space=pl.ANY)],
+        cost_estimate=pl.CostEstimate(flops=10**7, bytes_accessed=4 * 10**6, transcendentals=0),
+    )(own, from_c, from_d, to_a)
     own, to_len, cells, *fine = call(
         fine_before,
         [(5, half, mid_rows, LANES), (5, half // 2, mid_rows, LANES)]
         + [(2, half // 2, half_rows // 2, LANES)]
         + [(3, ext - 4) + line, (3, ext - 6) + line, (ext - 4,) + line]
         + [(ext - 6,) + line] * 2,
-        [field, field, cell, cell, cell, cell, field, (5, half + 2, ext_rows, LANES), (half + 2, mid_rows + 16, LANES)],
+        [field, field, cell, cell, cell, cell, field]
+        + [(5, half + 2, ext_rows, LANES), (half + 2, mid_rows + 16, LANES)],
         name="fine_before",
-    )(own, from_c, from_d, middle_a, middle_b, corner_a, corner_b)
-    from_a, from_b = swap(to_len, "len", 0), swap(to_len, "len", 1)
+    )(*inner, middle_b, middle_a, corner_b, corner_a)
+    from_b = swap(to_len, "len", 1)
+    from_a = swap(to_len, "len", 0)
 
     field1, cell1 = (3, mid, mid_rows, LANES), (mid, mid_rows, LANES)
     depth = half // 2

time: 47.8 us -> 46.1 us (0.964)
  waiting for transfers between devices: 9.11 us -> 5.8 us
  starting transfers between devices: 14 us -> 16.2 us
  Pallas kernels: 9.49 us -> 8.97 us
    ppermute x8, waiting for transfers between devices: 9.11 us -> 5.8 us  [swap(): return lax.ppermute(x, axis, pairs)]
    ppermute x8, starting transfers between devices: 14 us -> 16.2 us  [swap(): return lax.ppermute(x, axis, pairs)]
    pallas_call x0 -> x1, Pallas kernels: none -> 0.74 us  [body(): call(fine_inner, [(3,) + block, block, block, weighed, weighed] + [(3,) +...]
    pallas_call x1, Pallas kernels: 2.4 us -> 1.73 us  [body(): call(fine_before, [(5, half, mid_rows, LANES), (5, half // 2, mid_rows, L...]
    pallas_call x1, Pallas kernels: 5.12 us -> 4.47 us  [body(): call(functools.partial(coarse_and_after, first_brick), [forces.shape], [(...]
  transfers between devices with their start and end apart: 8 -> 8, of which waited for: 4 -> 4; matrix products, arithmetic and copies ran while one was open for 0% -> 0% of each run, Pallas kernels for 0% -> 2%
where the time goes in v4:
time: 46.1 us; the launch traced here: 45.9 us
  starting transfers between devices  16.2 us (35%)
  blocking collectives  14.8 us (32%)
  Pallas kernels  8.97 us (19%)
  waiting for transfers between devices  5.8 us (13%)
    ppermute x8, starting transfers between devices, swap(): return lax.ppermute(x, axis, pairs)  16.2 us
    all_to_all x1, blocking collectives, body(): table = lax.all_to_all(to_all, BOTH, 0, 0, tiled=True).reshape(-1, LANES)  14.8 us
    ppermute x8, waiting for transfers between devices, swap(): return lax.ppermute(x, axis, pairs)  5.8 us
    pallas_call x1, Pallas kernels, body(): call(functools.partial(coarse_and_after, first_brick), [forces.shape], [(...  4.47 us
    pallas_call x1, Pallas kernels, body(): call(fine_before, [(5, half, mid_rows, LANES), (5, half // 2, mid_rows, L...  1.73 us
    pallas_call x1, Pallas kernels, body(): call(pack_rows, [(5,) + block, side, side, middle_side, middle_side], [bl...  1.14 us
  transfers between devices with their start and end apart: 8, of which 4 were waited for; matrix products, arithmetic and copies ran while one was open for 0% of the time, Pallas kernels for 2%

profile of v4, /device:TPU:0, one launch (start us, length us, event | category | flops | bytes accessed | tf_op | source)
XLA Modules:
  0.0 45.9 jit_solution(6909888189843178858)
XLA Ops:
  0.0 1.1 %pack_rows.1 = (f32[5,8,16,128]{3,2,1,0:T(8,128)S(1)}, f32[408,128]{1,0:T(8,128)S(1)}, f32[408,128]{1,0:T(8,128)S(1)}, f32[256,128]{1,0:T(8,128)S(1)}, f32[256,128]{1,0:T(8,128)S(1)}) custom-call(f32[3,8,16,128]{3,2,1,0:T(8,128)} %forces.1, f32[8,16,128]{2,1,0:T(8,128)} %modulus.1, s32[8,16,128]{2,1,0:T(8,128)} %occupancy.1, s32[8,16,128]{2,1,0:T(8,128)} %bonded.1), custom_call_target="tpu_custom_call" | custom-call | tf_op jit(solution)/shard_map/pack_rows/pallas_call | solution.py:755
  1.1 3.0 %collective-permute-start = (f32[408,128]{1,0:T(8,128)S(1)}, f32[408,128]{1,0:T(8,128)S(1)}, u32[]{:S(2)}, u32[]{:S(2)}) collective-permute-start(f32[408,128]{1,0:T(8,128)S(1)} %get-tuple-element.35), channel_id=1, source_target_pairs={{0,1},{1,0},{2,3},{3,2},{4,5},{5,4},{6,7},{7,6},{8,9},{9,8},{10,11... | collective-permute-start | bytes 626696 | tf_op jit(solution)/shard_map/ppermute | solution.py:739
  4.2 0.7 %collective-permute-start.1 = (f32[408,128]{1,0:T(8,128)S(1)}, f32[408,128]{1,0:T(8,128)S(1)}, u32[]{:S(2)}, u32[]{:S(2)}) collective-permute-start(f32[408,128]{1,0:T(8,128)S(1)} %get-tuple-element.36), channel_id=1, source_target_pairs={{1,2},{2,1},{3,4},{4,3},{5,6},{6,5},{9,10},{10,9},{11,12},{12,11},... | collective-permute-start | bytes 626696 | tf_op jit(solution)/shard_map/ppermute | solution.py:739
  4.8 0.7 %collective-permute-start.2 = (f32[256,128]{1,0:T(8,128)S(1)}, f32[256,128]{1,0:T(8,128)S(1)}, u32[]{:S(2)}, u32[]{:S(2)}) collective-permute-start(f32[256,128]{1,0:T(8,128)S(1)} %get-tuple-element.37), channel_id=1, source_target_pairs={{8,16},{16,8},{9,17},{17,9},{10,18},{18,10},{11,19},{19,11},{12,20... | collective-permute-start | bytes 393224 | tf_op jit(solution)/shard_map/ppermute | solution.py:739
  5.5 2.9 %collective-permute-start.3 = (f32[256,128]{1,0:T(8,128)S(1)}, f32[256,128]{1,0:T(8,128)S(1)}, u32[]{:S(2)}, u32[]{:S(2)}) collective-permute-start(f32[256,128]{1,0:T(8,128)S(1)} %get-tuple-element.38), channel_id=1, source_target_pairs={{0,8},{8,0},{16,24},{24,16},{1,9},{9,1},{17,25},{25,17},{2,10},{10... | collective-permute-start | bytes 393224 | tf_op jit(solution)/shard_map/ppermute | solution.py:739
  8.4 0.0 collective-permute-done.2.middle_b
  8.4 1.0 %collective-permute-done.3.middle_a = f32[256,128]{1,0:T(8,128)S(1)} collective-permute-done((f32[256,128]{1,0:T(8,128)S(1)}, f32[256,128]{1,0:T(8,128)S(1)}, u32[]{:S(2)}, u32[]{:S(2)}) %collective-permute-start.3) | collective-permute-done | bytes 131104 | tf_op jit(solution)/shard_map/ppermute | solution.py:739
  9.4 3.7 %collective-permute-done.from_c = f32[408,128]{1,0:T(8,128)S(1)} collective-permute-done((f32[408,128]{1,0:T(8,128)S(1)}, f32[408,128]{1,0:T(8,128)S(1)}, u32[]{:S(2)}, u32[]{:S(2)}) %collective-permute-start) | collective-permute-done | bytes 208928 | tf_op jit(solution)/shard_map/ppermute | solution.py:739
  13.1 0.0 collective-permute-done.1.from_d
  13.1 0.1 pack_corners.1
  13.1 0.7 %collective-permute-start.4 = (f32[258,128]{1,0:T(8,128)S(1)}, f32[258,128]{1,0:T(8,128)S(1)}, u32[]{:S(2)}, u32[]{:S(2)}) collective-permute-start(f32[258,128]{1,0:T(8,128)S(1)} %get-tuple-element.48), channel_id=1, source_target_pairs={{8,16},{16,8},{9,17},{17,9},{10,18},{18,10},{11,19},{19,11},{12,20... | collective-permute-start | bytes 396296 | tf_op jit(solution)/shard_map/ppermute | solution.py:739
  13.8 2.9 %collective-permute-start.5 = (f32[258,128]{1,0:T(8,128)S(1)}, f32[258,128]{1,0:T(8,128)S(1)}, u32[]{:S(2)}, u32[]{:S(2)}) collective-permute-start(f32[258,128]{1,0:T(8,128)S(1)} %get-tuple-element.39.to_a), channel_id=1, source_target_pairs={{0,8},{8,0},{16,24},{24,16},{1,9},{9,1},{17,25},{25,17},{2,10},{10... | collective-permute-start | bytes 396296 | tf_op jit(solution)/shard_map/ppermute | solution.py:739
  16.7 0.7 %fine_inner.1 = (f32[3,8,40,128]{3,2,1,0:T(8,128)S(1)}, f32[8,40,128]{2,1,0:T(8,128)S(1)}, f32[8,40,128]{2,1,0:T(8,128)S(1)}, f32[6,40,128]{2,1,0:T(8,128)S(1)},...) custom-call(f32[5,8,16,128]{3,2,1,0:T(8,128)S(1)} %get-tuple-element, ...), custom_call_target="tpu_custom_call" | custom-call | flops 10000000 | bytes 4000000 | tf_op jit(solution)/shard_map/fine_inner/pallas_call | solution.py:780
  17.5 0.0 collective-permute-done.4.corner_b
  17.5 0.2 collective-permute-done.5.corner_a
  17.7 1.7 %fine_before.1 = (f32[5,4,16,128]{3,2,1,0:T(8,128)S(1)}, f32[5,2,16,128]{3,2,1,0:T(8,128)S(1)}, f32[2,2,4,128]{3,2,1,0:T(4,128)S(1)}, f32[3,12,24,128]{3,2,1,0:T...) custom-call(f32[3,8,40,128]{3,2,1,0:T(8,128)S(1)} %get-tuple-element, ...), custom_call_target="tpu_custom_call" | custom-call | tf_op jit(solution)/shard_map/fine_before/pallas_call | solution.py:789
  19.4 0.7 %collective-permute-start.7 = (f32[5,2,16,128]{3,2,1,0:T(8,128)S(1)}, f32[5,2,16,128]{3,2,1,0:T(8,128)S(1)}, u32[]{:S(2)}, u32[]{:S(2)}) collective-permute-start(f32[5,2,16,128]{3,2,1,0:T(8,128)S(1)} %get-tuple-element.51), channel_id=1, source_target_pairs={{8,16},{16,8},{9,17},{17,9},{10,18},{18,10},{11,19},{19,11},{12,20... | collective-permute-start | bytes 245768 | tf_op jit(solution)/shard_map/ppermute | solution.py:739
  20.1 4.7 %collective-permute-start.6 = (f32[5,2,16,128]{3,2,1,0:T(8,128)S(1)}, f32[5,2,16,128]{3,2,1,0:T(8,128)S(1)}, u32[]{:S(2)}, u32[]{:S(2)}) collective-permute-start(f32[5,2,16,128]{3,2,1,0:T(8,128)S(1)} %get-tuple-element.51), channel_id=1, source_target_pairs={{0,8},{8,0},{16,24},{24,16},{1,9},{9,1},{17,25},{25,17},{2,10},{10... | collective-permute-start | bytes 245768 | tf_op jit(solution)/shard_map/ppermute | solution.py:739
  24.8 0.0 collective-permute-done.7.from_b
  24.8 0.9 %collective-permute-done.6.from_a = f32[5,2,16,128]{3,2,1,0:T(8,128)S(1)} collective-permute-done((f32[5,2,16,128]{3,2,1,0:T(8,128)S(1)}, f32[5,2,16,128]{3,2,1,0:T(8,128)S(1)}, u32[]{:S(2)}, u32[]{:S(2)}) %collective-permute-start.6) | collective-permute-done | bytes 81952 | tf_op jit(solution)/shard_map/ppermute | solution.py:739
  25.7 0.9 %middle_before.1 = (f32[320,128]{1,0:T(8,128)S(1)}, f32[3,12,16,128]{3,2,1,0:T(8,128)S(1)}, f32[3,12,16,128]{3,2,1,0:T(8,128)S(1)}, f32[12,16,128]{2,1,0:T(8,128...) custom-call(f32[5,4,16,128]{3,2,1,0:T(8,128)S(1)} %get-tuple-element.49.own, ...), custom_call_target="tpu_custom_call" | custom-call | tf_op jit(solution)/shard_map/middle_before/pallas_call | solution.py:805
  26.6 14.8 %all_to_all.5 = f32[160,2,128]{2,1,0:T(2,128)S(1)} all-to-all(f32[160,2,128]{2,1,0:T(2,128)S(1)} %bitcast.3), channel_id=1, replica_groups=mesh['len'=4,'brick'=8] {'len','brick'}, dimensions={0} | all-to-all | bytes 327680 | tf_op jit(solution)/shard_map/all_to_all | solution.py:813
  41.4 4.5 %coarse_and_after.1 = f32[3,8,16,128]{3,2,1,0:T(8,128)} custom-call(f32[320,128]{1,0:T(8,128)S(1)} %bitcast.2, f32[3,12,16,128]{3,2,1,0:T(8,128)S(1)} %get-tuple-element.53.v2_mid, f32[3,12,16,128]{3,2,1,0:T(8,128)S(1)} %get-tuple-element.54.source_mid, f32[12,16,128]{2,1,0:T(8,128)S(1)} %get-tuple-element.55.quarter_mid, ...), custom_call_target="tpu_custom_call" | custom-call | tf_op jit(solution)/shard_map/coarse_and_after/pallas_call | solution.py:825
Async XLA Ops:
  1.1 11.9 %collective-permute-start = (f32[408,128]{1,0:T(8,128)S(1)}, f32[408,128]{1,0:T(8,128)S(1)}, u32[]{:S(2)}, u32[]{:S(2)}) collective-permute-start(f32[408,128]{1,0:T(8,128)S(1)} %get-tuple-element.35), channel_id=1, source_target_pairs={{0,1},{1,0},{2,3},{3,2},{4,5},{5,4},{6,7},{7,6},{8,9},{9,8},{10,11... | collective-permute-start | bytes 626696 | tf_op jit(solution)/shard_map/ppermute | solution.py:739
  4.2 8.9 %collective-permute-start.1 = (f32[408,128]{1,0:T(8,128)S(1)}, f32[408,128]{1,0:T(8,128)S(1)}, u32[]{:S(2)}, u32[]{:S(2)}) collective-permute-start(f32[408,128]{1,0:T(8,128)S(1)} %get-tuple-element.36), channel_id=1, source_target_pairs={{1,2},{2,1},{3,4},{4,3},{5,6},{6,5},{9,10},{10,9},{11,12},{12,11},... | collective-permute-start | bytes 626696 | tf_op jit(solution)/shard_map/ppermute | solution.py:739
  4.8 3.6 %collective-permute-start.2 = (f32[256,128]{1,0:T(8,128)S(1)}, f32[256,128]{1,0:T(8,128)S(1)}, u32[]{:S(2)}, u32[]{:S(2)}) collective-permute-start(f32[256,128]{1,0:T(8,128)S(1)} %get-tuple-element.37), channel_id=1, source_target_pairs={{8,16},{16,8},{9,17},{17,9},{10,18},{18,10},{11,19},{19,11},{12,20... | collective-permute-start | bytes 393224 | tf_op jit(solution)/shard_map/ppermute | solution.py:739
  5.5 3.9 %collective-permute-start.3 = (f32[256,128]{1,0:T(8,128)S(1)}, f32[256,128]{1,0:T(8,128)S(1)}, u32[]{:S(2)}, u32[]{:S(2)}) collective-permute-start(f32[256,128]{1,0:T(8,128)S(1)} %get-tuple-element.38), channel_id=1, source_target_pairs={{0,8},{8,0},{16,24},{24,16},{1,9},{9,1},{17,25},{25,17},{2,10},{10... | collective-permute-start | bytes 393224 | tf_op jit(solution)/shard_map/ppermute | solution.py:739
  13.1 4.3 %collective-permute-start.4 = (f32[258,128]{1,0:T(8,128)S(1)}, f32[258,128]{1,0:T(8,128)S(1)}, u32[]{:S(2)}, u32[]{:S(2)}) collective-permute-start(f32[258,128]{1,0:T(8,128)S(1)} %get-tuple-element.48), channel_id=1, source_target_pairs={{8,16},{16,8},{9,17},{17,9},{10,18},{18,10},{11,19},{19,11},{12,20... | collective-permute-start | bytes 396296 | tf_op jit(solution)/shard_map/ppermute | solution.py:739
  13.8 3.9 %collective-permute-start.5 = (f32[258,128]{1,0:T(8,128)S(1)}, f32[258,128]{1,0:T(8,128)S(1)}, u32[]{:S(2)}, u32[]{:S(2)}) collective-permute-start(f32[258,128]{1,0:T(8,128)S(1)} %get-tuple-element.39.to_a), channel_id=1, source_target_pairs={{0,8},{8,0},{16,24},{24,16},{1,9},{9,1},{17,25},{25,17},{2,10},{10... | collective-permute-start | bytes 396296 | tf_op jit(solution)/shard_map/ppermute | solution.py:739
  19.4 5.3 %collective-permute-start.7 = (f32[5,2,16,128]{3,2,1,0:T(8,128)S(1)}, f32[5,2,16,128]{3,2,1,0:T(8,128)S(1)}, u32[]{:S(2)}, u32[]{:S(2)}) collective-permute-start(f32[5,2,16,128]{3,2,1,0:T(8,128)S(1)} %get-tuple-element.51), channel_id=1, source_target_pairs={{8,16},{16,8},{9,17},{17,9},{10,18},{18,10},{11,19},{19,11},{12,20... | collective-permute-start | bytes 245768 | tf_op jit(solution)/shard_map/ppermute | solution.py:739
  20.1 5.6 %collective-permute-start.6 = (f32[5,2,16,128]{3,2,1,0:T(8,128)S(1)}, f32[5,2,16,128]{3,2,1,0:T(8,128)S(1)}, u32[]{:S(2)}, u32[]{:S(2)}) collective-permute-start(f32[5,2,16,128]{3,2,1,0:T(8,128)S(1)} %get-tuple-element.51), channel_id=1, source_target_pairs={{0,8},{8,0},{16,24},{24,16},{1,9},{9,1},{17,25},{25,17},{2,10},{10... | collective-permute-start | bytes 245768 | tf_op jit(solution)/shard_map/ppermute | solution.py:739

commit v5 on v4

--- a/solution.py
+++ b/solution.py
@@ -45,6 +45,15 @@
     def smooth(self, x):
         return x + self.low * turn(x, self.wide, 1) + self.high * turn(x, -self.wide, 1)
 
+    def beside(self, q):
+        return turn(q, self.wide, 1), turn(q, -self.wide, 1)
+
+    def blend(self, x, y, q, before, after):
+        return (q * x + y) + (
+            self.low * turn(after * x + y, self.wide, 1)
+            + self.high * turn(before * x + y, -self.wide, 1)
+        )
+
     def pair(self, x):
         return x + swap_lanes(x, self.wide, self.first)
 
@@ -101,20 +110,29 @@
 
     def terms(self, q, s):
         total = 24.0 * q + self.full(q) + s
-        return total + 8.0 * q, DAMPING / (total + (4.0 * COUPLING) * q)
-
-    def defects(self, v, q, weight, source):
-        count = q.shape[0]
+        q = [jnp.concatenate([x] * 3, axis=0) for x in (q, turn(q, self.wide, 2), turn(q, -self.wide, 2))]
+        weight = total + 8.0 * q[0][: total.shape[0]]
+        return (q, weight), DAMPING / (total + (4.0 * COUPLING) * q[0][: total.shape[0]])
+
+    def defects(self, v, terms, source):
+        (q3, before, after), weight = terms
+        count = weight.shape[0]
+        q = q3[:count]
         stack = [self.planes(x) for x in v] + [self.planes(q * x) for x in v]
-        both = self.smooth(self.rows(jnp.concatenate(stack, axis=0)))
-        part = [both[i * count : (i + 1) * count] for i in range(6)]
+        both = self.rows(jnp.concatenate(stack, axis=0))
+        x, y = both[: 3 * count], both[3 * count :]
+        sums = (q3 * x + y) + (
+            self.low * turn(after * x + y, self.wide, 2)
+            + self.high * turn(before * x + y, -self.wide, 2)
+        )
         coupled = (4.0 * COUPLING) * q * (v[0] + v[1] + v[2])
         return [
-            source[k] - weight * v[k] + (q * part[k] + part[3 + k]) - coupled for k in range(3)
+            source[k] - weight * v[k] + sums[k * count : (k + 1) * count] - coupled
+            for k in range(3)
         ]
 
-    def sweep(self, v, q, weight, step, source):
-        r = self.defects(v, q, weight, source)
+    def sweep(self, v, terms, step, source):
+        r = self.defects(v, terms, source)
         return [v[k] + step * r[k] for k in range(3)]
 
     def restrict(self, x):
@@ -151,32 +169,40 @@
     return lambda p: get(p) if low <= p < high else None
 
 
-def gathered(field, quarter, planes, bounds, lane):
-    low, high = bounds
-    q_at = remember(within(lambda p: quarter[p], low, high))
-    v_at = [remember(within(lambda p, k=k: field(k, p), low, high)) for k in range(3)]
-    w_at = [
-        remember(within(lambda p, k=k: q_at(p) * v_at[k](p), low, high)) for k in range(3)
+APART = {}
+
+
+def gathered(field, quarter, planes, bounds, lane, beside=None):
+    beside = {} if beside is None else beside
+    q_at = remember(lambda p: quarter[p])
+    v_at = [remember(lambda p, k=k: field(k, p)) for k in range(3)]
+    w_at = [remember(lambda p, k=k: q_at(p) * v_at[k](p)) for k in range(3)]
+    pairs = [
+        [remember(lambda p, x=x: x(p) + x(p + 1)) for x in group] for group in (v_at, w_at)
     ]
     for p in planes:
         q = q_at(p)
+        if p not in beside and beside is not APART:
+            beside[p] = lane.beside(q)
         sums = []
         for k in range(3):
-            x = lane.rows(smooth_planes(v_at[k], p))
-            y = lane.rows(smooth_planes(w_at[k], p))
-            sums.append(q * lane.smooth(x) + lane.smooth(y))
+            x, y = [lane.rows(group[k](p - 1) + group[k](p)) for group in pairs]
+            if beside is APART:
+                sums.append(q * lane.smooth(x) + lane.smooth(y))
+            else:
+                sums.append(lane.blend(x, y, q, *beside[p]))
         yield p, [v_at[k](p) for k in range(3)], q, sums
 
 
-def defects(field, quarter, weight, source, planes, bounds, lane):
-    for p, v, q, sums in gathered(field, quarter, planes, bounds, lane):
+def defects(field, quarter, weight, source, planes, bounds, lane, beside=None):
+    for p, v, q, sums in gathered(field, quarter, planes, bounds, lane, beside):
         coupled = (4.0 * COUPLING) * q * (v[0] + v[1] + v[2])
         e = weight[p]
         yield p, v, [source[k, p] - e * v[k] + sums[k] - coupled for k in range(3)]
 
 
-def sweep(field, quarter, weight, step, source, planes, bounds, lane, put):
-    for p, v, r in defects(field, quarter, weight, source, planes, bounds, lane):
+def sweep(field, quarter, weight, step, source, planes, bounds, lane, put, beside=None):
+    for p, v, r in defects(field, quarter, weight, source, planes, bounds, lane, beside):
         s = step[p]
         for k in range(3):
             put(k, p, v[k] + s * r[k])
@@ -213,6 +239,18 @@
     def __getitem__(self, at):
         p = at[1] if isinstance(at, tuple) else at
         return self.inner[at] if p in self.span else self.outer[at]
+
+
+class Stack:
+    def __init__(self, *parts):
+        self.spots = {p: (ref, i) for ref, planes in parts for i, p in enumerate(planes)}
+
+    def __getitem__(self, at):
+        if isinstance(at, tuple):
+            ref, i = self.spots[at[1]]
+            return ref[at[0], i]
+        ref, i = self.spots[at]
+        return ref[i]
 
 
 def vmem(shape):
@@ -255,25 +293,21 @@
     forces, modulus, occupancy, bonded, own, to_c, to_d, to_a, to_b,
     modulus_here, occupancy_here, bonded_here, arrived,
 ):
-    copies = [
-        pltpu.make_async_copy(source, target, arrived.at[i])
-        for i, (source, target) in enumerate(
-            [
-                (modulus, modulus_here),
-                (occupancy, occupancy_here),
-                (bonded, bonded_here),
-                (forces, own.at[pl.ds(0, 3)]),
-            ]
-        )
-    ]
+    pairs = [(modulus, modulus_here), (occupancy, occupancy_here), (bonded, bonded_here)]
+    pairs += [(forces.at[k], own.at[k]) for k in range(3)]
+    copies = [pltpu.make_async_copy(*pair, arrived.at[i]) for i, pair in enumerate(pairs)]
     for copy in copies:
         copy.start()
-    for copy in copies:
+    planes, rows = own.shape[1], own.shape[2]
+    for copy in copies[:2]:
         copy.wait()
-    planes, rows = own.shape[1], own.shape[2]
     for p in range(planes):
         own[3, p] = modulus_here[p] * occupancy_here[p].astype(F32)
+    copies[2].wait()
+    for p in range(planes):
         own[4, p] = MASS_TERM + PENALTY * bonded_here[p].astype(F32)
+    for copy in copies[3:]:
+        copy.wait()
     is_odd = odd("brick")
     spots, _ = row_spots(planes)
     for (k, p), spot in spots.items():
@@ -319,9 +353,40 @@
     return [range(HALO + i, HALO + planes - i) for i in (1, 2, 3)]
 
 
+def kept_planes(planes):
+    weighed, swept, _ = inner_planes(planes)
+    own = range(HALO, HALO + planes)
+    end = planes + 2 * HALO
+    wide, close = range(2, end - 2), range(3, end - 3)
+    pairs = ((swept, wide), (own, close), (own, wide), (weighed, close), (weighed, close))
+    return [(inner, [p for p in every if p not in inner]) for inner, every in pairs]
+
+
+def keep(kept_rows, targets, arrays, numbers):
+    for k in range(2):
+        for i, p in enumerate(numbers[k]):
+            for c in range(3):
+                targets[k][c, i] = arrays[k][c, p][kept_rows]
+    for k in range(2, 5):
+        for i, p in enumerate(numbers[k]):
+            targets[k][i] = arrays[k][p][kept_rows]
+
+
+def halves(x, rows):
+    count = (rows.stop - rows.start) // 2
+    return x[pl.ds(rows.start, count, stride=2), :] + x[pl.ds(rows.start + 1, count, stride=2), :]
+
+
+def coarse_weight(lane, quarter_at, i, rows):
+    sides, here, others = [
+        smooth_planes(lambda j, at=at: quarter_at(j)[pl.ds(at, rows), :], i) for at in (7, 8, 9)
+    ]
+    return 24.0 * quarter_at(i)[pl.ds(8, rows), :] + lane.smooth(sides + 2.0 * here + others)
+
+
 def fine_inner(
     own, from_c, from_d, to_a,
-    source, quarter, shift, weight, step, v1, v2, rest,
+    source, quarter, shift, weight, step, v1, v2, rest, coarse_q, shift1, sums, cells, *more,
 ):
     del to_a
     planes, rows = own.shape[1], own.shape[2]
@@ -358,25 +423,58 @@
     def put_v2(k, p, value):
         v2[k, p - swept[0]] = value
 
-    v1_at, v2_at = From(v1, weighed[0]), From(v2, swept[0])
+    v1_at, v2_at, near = From(v1, weighed[0]), From(v2, swept[0]), APART
     sweep(
         lambda k, p: v1_at[k, p], quarter_at, weight_at, step_at, source_at,
-        swept, (weighed[0], weighed[-1] + 1), lane, put_v2,
+        swept, (weighed[0], weighed[-1] + 1), lane, put_v2, near,
     )
     for p, _, r in defects(
         lambda k, p: v2_at[k, p], quarter_at, weight_at, source_at,
-        left, (swept[0], swept[-1] + 1), lane,
+        left, (swept[0], swept[-1] + 1), lane, near,
     ):
         for k in range(3):
             rest[k, p - left[0]] = r[k]
 
+    *kept, work = more
+    half = rows // 2 + 2 * HALO
+    outer = slice(WIDE - 2 * HALO, WIDE + rows + 2 * HALO)
+    beyond = slice(outer.start - 2, outer.stop + 2)
+    count = planes // 2
+    for i in range(count):
+        work[0, i] = quarter[2 * i] + quarter[2 * i + 1]
+        work[1, i] = shift[2 * i] + shift[2 * i + 1]
+    for f in range(2):
+        for i in range(count):
+            work[f, i] = lane.pair(work[f, i])
+    for i in range(count):
+        coarse_q[i, pl.ds(7, half + 2), :] = (0.25 * 0.125) * halves(work.at[0, i], beyond)
+        shift1[i] = 0.125 * halves(work.at[1, i], outer)
+    lane1 = Lane(half, 2)
+    for i in range(1, count - 1):
+        s = shift1[i]
+        w = coarse_weight(lane1, lambda j: coarse_q.at[j], i, half)
+        sums[i - 1] = jnp.where(s > 0.0, w + s, 0.0)
+
+    inner = slice(HALO, HALO + rows // 2)
+    for i in range(count // 2):
+        pair = [coarse_q[2 * i + j, pl.ds(8, half), :] for j in range(2)]
+        work[0, i, pl.ds(0, half), :] = lane1.pair(pair[0] + pair[1])
+        work[1, i, pl.ds(0, half), :] = lane1.pair(shift1[2 * i] + shift1[2 * i + 1])
+        for f, scale in enumerate((0.25 * 0.125, 0.125)):
+            cells[f, i] = scale * halves(work.at[f, i], inner)
+    keep(
+        slice(WIDE - HALO, WIDE + rows + HALO), kept,
+        (v2_at, source_at, quarter_at, weight_at, step_at),
+        [x for x, _ in kept_planes(planes)],
+    )
+
 
 def fine_before(
     source_in, quarter_in, shift_in, weight_in, step_in, v1_in, v2_in, rest_in,
-    middle_b, middle_a, corner_b, corner_a,
-    own_coarse, to_len, cells, v2_kept, source_kept, quarter_kept, weight_kept, step_kept,
-    v2_out, source_out, quarter_out, weight_out, step_out, shift_out, v1_out, work, coarse_q,
+    coarse_q_in, shift1, sums_in, middle_b, middle_a, corner_a, corner_b,
+    own_coarse, to_len, *more,
 ):
+    *kept, v2_out, source_out, quarter_out, weight_out, step_out, shift_out, v1_out, work, coarse_q = more
     planes, ext_rows = quarter_in.shape[0], quarter_in.shape[1]
     ext_planes, rows = planes + 2 * HALO, ext_rows - 2 * WIDE
     lane = Lane(ext_rows, 1)
@@ -420,9 +518,8 @@
         for x, y in ((weight_in, weight_out), (step_in, step_out), (v1_in, v1_out))
     ]
     v2 = Either(v2_in, swept, v2_out)
-    kept = slice(WIDE - HALO, WIDE + rows + HALO)
-
-    bounds = (0, ext_planes)
+
+    bounds, near = (0, ext_planes), APART
     others = [p for p in range(1, ext_planes - 1) if p not in weighed]
     for p, w in stiffness_sum(quarter, others, bounds, lane):
         q, s = quarter[p], shift[p]
@@ -438,82 +535,64 @@
 
     sweep(
         lambda k, p: v1[k, p], quarter, weight, step, source,
-        [p for p in range(2, ext_planes - 2) if p not in swept], bounds, lane, put_v2,
+        [p for p in range(2, ext_planes - 2) if p not in swept], bounds, lane, put_v2, near,
     )
 
     half = rows // 2 + 2 * HALO
-    first_row = WIDE - 2 * HALO
+    outer = slice(WIDE - 2 * HALO, WIDE + rows + 2 * HALO)
+    beyond = slice(outer.start - 2, outer.stop + 2)
     coarse_planes = planes // 2
     rest = {p: [rest_in[k, p - left[0]] for k in range(3)] for p in left}
     for p, _, r in defects(
         lambda k, p: v2[k, p], quarter, weight, source,
-        [p for p in here if p not in left], bounds, lane,
+        [p for p in here if p not in left], bounds, lane, near,
     ):
         rest[p] = r
     for i in range(coarse_planes):
         p = HALO + 2 * i
         for k in range(3):
             work[k, i] = rest[p][k] + rest[p + 1][k]
-    for i in range(coarse_planes):
-        work[4, i] = shift[HALO + 2 * i] + shift[HALO + 2 * i + 1]
-    reach = coarse_planes + 2
-    for j in range(reach):
-        work[3, j] = quarter[2 * j + 2] + quarter[2 * j + 3]
-    for k in range(5):
-        for i in range(reach if k == 3 else coarse_planes):
+    for j, p in enumerate((HALO - 2, HALO + planes)):
+        work[3, j] = quarter[p] + quarter[p + 1]
+    for k in range(4):
+        for i in range(2 if k == 3 else coarse_planes):
             work[k, i] = lane.pair(work[k, i])
-
-    def halved(k, i, start, count):
-        return (
-            work[k, i, pl.ds(start, count, stride=2), :]
-            + work[k, i, pl.ds(start + 1, count, stride=2), :]
-        )
-
     for i in range(coarse_planes):
         for k in range(3):
-            own_coarse[k, i] = 0.125 * halved(k, i, first_row, half)
-
-    for j in range(reach):
-        coarse_q[j, pl.ds(7, half + 2), :] = (0.25 * 0.125) * halved(3, j, first_row - 2, half + 2)
+            own_coarse[k, i] = 0.125 * halves(work.at[k, i], outer)
+
+    for j in range(2):
+        coarse_q[j, pl.ds(7, half + 2), :] = (0.25 * 0.125) * halves(work.at[3, j], beyond)
+
+    def quarter1(i):
+        if i < 0:
+            return coarse_q.at[0]
+        return coarse_q.at[1] if i == coarse_planes else coarse_q_in.at[i]
+
     lane1 = Lane(half, 2)
-    shift1, q1 = [], []
     for i in range(coarse_planes):
-        s = 0.125 * halved(4, i, first_row, half)
-        sides = smooth_planes(lambda j: coarse_q[j, pl.ds(7, half), :], i + 1)
-        here = smooth_planes(lambda j: coarse_q[j, pl.ds(8, half), :], i + 1)
-        others = smooth_planes(lambda j: coarse_q[j, pl.ds(9, half), :], i + 1)
-        q = coarse_q[i + 1, pl.ds(8, half), :]
-        w = 24.0 * q + lane1.smooth(sides + 2.0 * here + others)
-        own_coarse[3, i] = q
-        own_coarse[4, i] = jnp.where(s > 0.0, w + s, 0.0)
-        shift1.append(s)
-        q1.append(q)
+        own_coarse[3, i] = coarse_q_in[i, pl.ds(8, half), :]
+        if 0 < i < coarse_planes - 1:
+            own_coarse[4, i] = sums_in[i - 1]
+        else:
+            s = shift1[i]
+            w = coarse_weight(lane1, quarter1, i, half)
+            own_coarse[4, i] = jnp.where(s > 0.0, w + s, 0.0)
 
     even = (lane_ids((half, LANES)) & 1) == 0
     for k in range(5):
         for i in range(coarse_planes // 2):
             to_len[k, i] = jnp.where(even, own_coarse[k, 2 * i], own_coarse[k, 2 * i + 1])
 
-    for i in range(coarse_planes // 2):
-        for f, (values, scale) in enumerate(((q1, 0.25 * 0.125), (shift1, 0.125))):
-            work[f, i, pl.ds(0, half), :] = lane1.pair(values[2 * i] + values[2 * i + 1])
-            cells[f, i] = scale * (
-                work[f, i, pl.ds(HALO, rows // 4, stride=2), :]
-                + work[f, i, pl.ds(HALO + 1, rows // 4, stride=2), :]
-            )
-
-    for p in range(2, ext_planes - 2):
-        quarter_kept[p - 2] = quarter[p][kept]
-        for k in range(3):
-            v2_kept[k, p - 2] = v2[k, p][kept]
-    for p in range(3, ext_planes - 3):
-        weight_kept[p - 3], step_kept[p - 3] = weight[p][kept], step[p][kept]
-        for k in range(3):
-            source_kept[k, p - 3] = source[k, p][kept]
+    keep(
+        slice(WIDE - HALO, WIDE + rows + HALO), kept,
+        (v2, source, quarter, weight, step),
+        [x for _, x in kept_planes(planes)],
+    )
 
 
 def middle_before(
-    own, cells, from_a, from_b,
+    own, cells, from_b, from_a,
     to_all, v2, source, quarter, weight, step,
     v1, work,
 ):
@@ -555,16 +634,16 @@
     def put_v2(k, p, value):
         v2[k, p] = value
 
-    bounds = (0, ext_planes)
+    bounds, near = (0, ext_planes), {}
     sweep(
         lambda k, p: v1[k, p], quarter, weight, step, source,
-        range(1, ext_planes - 1), bounds, lane, put_v2,
+        range(1, ext_planes - 1), bounds, lane, put_v2, near,
     )
     held = {}
     half = rows // 2
     for p, _, r in defects(
         lambda k, p: v2[k, p], quarter, weight, source,
-        range(HALO, HALO + planes), bounds, lane,
+        range(HALO, HALO + planes), bounds, lane, near,
     ):
         if p % 2 == 0:
             held = r
@@ -604,11 +683,10 @@
 
 def coarse_and_after(
     bricks_before,
-    table, v2_mid, source_mid, quarter_mid, weight_mid, step_mid,
-    v2_fine, source_fine, quarter_fine, weight_fine, step_fine,
-    out,
-    wide2, u_mid, x_mid, u_fine, x_fine,
+    table, v2_mid, source_mid, quarter_mid, weight_mid, step_mid, *more,
 ):
+    kept_inner, kept_outer = more[:5], more[5:10]
+    out, wide2, u_mid, x_mid, u_fine, x_fine = more[10:]
     brick = lax.axis_index("brick")
     slab = lax.axis_index("len")
     bricks, planes2 = wide2.shape[2] - 16, wide2.shape[1] - 4
@@ -627,32 +705,34 @@
     lane2, lane3 = Packed(bricks, 1), Packed(bricks, 2)
     b2, q2, s2 = [field(k) for k in range(3)], field(3), field(4)
     e2, x2 = lane2.terms(q2, s2)
-    u2 = lane2.sweep([x2 * b for b in b2], q2, e2, x2, b2)
-
-    rest = lane2.defects(u2, q2, e2, b2)
+    u2 = lane2.sweep([x2 * b for b in b2], e2, x2, b2)
+
+    rest = lane2.defects(u2, e2, b2)
     joint = lane2.restrict(jnp.concatenate(rest + [0.25 * q2, s2], axis=0))
     count = planes2 // 2
     *b3, q3, s3 = [joint[i * count : (i + 1) * count] for i in range(5)]
     e3, x3 = lane3.terms(q3, s3)
     u3 = [x3 * b for b in b3]
     for _ in range(3):
-        u3 = lane3.sweep(u3, q3, e3, x3, b3)
+        u3 = lane3.sweep(u3, e3, x3, b3)
 
     u2 = [u2[k] + twice_planes(u3[k]) for k in range(3)]
     for _ in range(2):
-        u2 = lane2.sweep(u2, q2, e2, x2, b2)
+        u2 = lane2.sweep(u2, e2, x2, b2)
     wide2[...] = jnp.zeros_like(wide2)
     for k in range(3):
         wide2[k, pl.ds(2, planes2), pl.ds(8, bricks), :] = u2[k]
 
-    v2_fine, quarter_fine = From(v2_fine, 2), From(quarter_fine, 2)
-    source_fine, weight_fine, step_fine = [
-        From(x, 3) for x in (source_fine, weight_fine, step_fine)
+    v2_fine, source_fine, quarter_fine, weight_fine, step_fine = [
+        Stack((inner, numbers[0]), (outer, numbers[1]))
+        for inner, outer, numbers in zip(
+            kept_inner, kept_outer, kept_planes(x_fine.shape[1] - 2 * HALO)
+        )
     ]
     planes1 = v2_mid.shape[1]
     rows1 = v2_mid.shape[2]
     lane1 = Lane(rows1, 2)
-    bounds1 = (0, planes1)
+    bounds1, beside1 = (0, planes1), {}
     line_at = brick - bricks_before(brick) + 8
     half_shape = (rows1 // 2, LANES)
     ids, row = lane_ids(half_shape), lax.broadcasted_iota(jnp.int32, half_shape, 0)
@@ -678,7 +758,7 @@
 
     sweep(
         lambda k, p: u_mid[k, p], quarter_mid, weight_mid, step_mid, source_mid,
-        range(2, planes1 - 2), bounds1, lane1, put_mid,
+        range(2, planes1 - 2), bounds1, lane1, put_mid, beside1,
     )
 
     def put_mid_last(k, p, value):
@@ -686,12 +766,12 @@
 
     sweep(
         lambda k, p: x_mid[k, p], quarter_mid, weight_mid, step_mid, source_mid,
-        range(3, planes1 - 3), bounds1, lane1, put_mid_last,
+        range(3, planes1 - 3), bounds1, lane1, put_mid_last, beside1,
     )
 
     planes0, rows0 = x_fine.shape[1], x_fine.shape[2]
     lane0 = Lane(rows0, 1)
-    bounds0 = (0, planes0)
+    bounds0, beside0 = (0, planes0), {}
     half_rows = rows0 // 2
     for k in range(3):
         for i in range(3, planes1 - 3):
@@ -708,7 +788,7 @@
 
     sweep(
         lambda k, p: u_fine[k, p], quarter_fine, weight_fine, step_fine, source_fine,
-        range(3, planes0 - 3), bounds0, lane0, put_fine,
+        range(3, planes0 - 3), bounds0, lane0, put_fine, beside0,
     )
 
     def put_out(k, p, value):
@@ -716,7 +796,7 @@
 
     sweep(
         lambda k, p: x_fine[k, p], quarter_fine, weight_fine, step_fine, source_fine,
-        range(HALO, planes0 - HALO), bounds0, lane0, put_out,
+        range(HALO, planes0 - HALO), bounds0, lane0, put_out, beside0,
     )
 
 
@@ -756,7 +836,7 @@
         pack_rows,
         [(5,) + block, side, side, middle_side, middle_side],
         [block, pltpu.VMEM(block, jnp.int32), pltpu.VMEM(block, jnp.int32)]
-        + [pltpu.SemaphoreType.DMA((4,))],
+        + [pltpu.SemaphoreType.DMA((6,))],
         name="pack_rows",
         in_specs=[pl.BlockSpec(memory_space=pltpu.HBM)] * 4,
     )(*here)
@@ -770,34 +850,44 @@
         name="pack_corners",
         in_specs=[pl.BlockSpec(memory_space=x) for x in (pltpu.VMEM, pl.ANY) * 2],
     )(from_c, middle_b, from_d, middle_a)
+    corner_a = swap(to_a, "len", 0)
     corner_b = swap(to_b, "len", 1)
-    corner_a = swap(to_a, "len", 0)
 
     field, cell = (3, ext, ext_rows, LANES), (ext, ext_rows, LANES)
     line = (rows + 2 * HALO, LANES)
     block = (planes, ext_rows, LANES)
     weighed, swept, left = [(len(x), ext_rows, LANES) for x in inner_planes(planes)]
+    kept_inner, kept_outer = [
+        [
+            ((3,) if k < 2 else ()) + (len(numbers[part]),) + line
+            for k, numbers in enumerate(kept_planes(planes))
+        ]
+        for part in range(2)
+    ]
+    coarse = (half, mid_rows + 16, LANES)
     inner = call(
         fine_inner,
         [(3,) + block, block, block, weighed, weighed]
-        + [(3,) + weighed, (3,) + swept, (3,) + left],
+        + [(3,) + weighed, (3,) + swept, (3,) + left]
+        + [coarse, (half, mid_rows, LANES), (half - 2, mid_rows, LANES)]
+        + [(2, half // 2, half_rows // 2, LANES)]
+        + kept_inner,
+        [(2, half, ext_rows, LANES)],
         name="fine_inner",
         in_specs=[pl.BlockSpec(memory_space=pltpu.VMEM)] * 3
         + [pl.BlockSpec(memory_space=pl.ANY)],
         cost_estimate=pl.CostEstimate(flops=10**7, bytes_accessed=4 * 10**6, transcendentals=0),
     )(own, from_c, from_d, to_a)
-    own, to_len, cells, *fine = call(
+    inner, cells, kept_inner = inner[:11], inner[11], inner[12:]
+    own, to_len, *kept_outer = call(
         fine_before,
-        [(5, half, mid_rows, LANES), (5, half // 2, mid_rows, LANES)]
-        + [(2, half // 2, half_rows // 2, LANES)]
-        + [(3, ext - 4) + line, (3, ext - 6) + line, (ext - 4,) + line]
-        + [(ext - 6,) + line] * 2,
+        [(5, half, mid_rows, LANES), (5, half // 2, mid_rows, LANES)] + kept_outer,
         [field, field, cell, cell, cell, cell, field]
-        + [(5, half + 2, ext_rows, LANES), (half + 2, mid_rows + 16, LANES)],
+        + [(4, half, ext_rows, LANES), (2,) + coarse[1:]],
         name="fine_before",
-    )(*inner, middle_b, middle_a, corner_b, corner_a)
+    )(*inner, middle_b, middle_a, corner_a, corner_b)
+    from_a = swap(to_len, "len", 0)
     from_b = swap(to_len, "len", 1)
-    from_a = swap(to_len, "len", 0)
 
     field1, cell1 = (3, mid, mid_rows, LANES), (mid, mid_rows, LANES)
     depth = half // 2
@@ -807,7 +897,7 @@
         [(slabs * bricks * lines, LANES)] + [field1, field1, cell1, cell1, cell1],
         [field1, (3, depth, mid_rows, LANES)],
         name="middle_before",
-    )(own, cells, from_a, from_b)
+    )(own, cells, from_b, from_a)
 
     to_all = to_all.reshape(-1, 2, LANES)
     table = lax.all_to_all(to_all, BOTH, 0, 0, tiled=True).reshape(-1, LANES)
@@ -828,7 +918,7 @@
         [(3, planes2 + 4, window + 16, LANES), field1, field1]
         + [(3, ext, rows + 2 * HALO, LANES)] * 2,
         name="coarse_and_after",
-    )(table, *middle, *fine)
+    )(table, *middle, *kept_inner, *kept_outer)
     return out
 
 

time: 46.1 us -> 45.6 us (0.989)
  transfers between devices with their start and end apart: 8 -> 8, of which waited for: 4 -> 3; matrix products, arithmetic and copies ran while one was open for 0% -> 0% of each run, Pallas kernels for 2% -> 2%
where the time goes in v5:
time: 45.6 us; the launch traced here: 45.3 us
  starting transfers between devices  16.3 us (36%)
  blocking collectives  14.8 us (32%)
  Pallas kernels  8.58 us (19%)
  waiting for transfers between devices  5.57 us (12%)
    ppermute x8, starting transfers between devices, swap(): return lax.ppermute(x, axis, pairs)  16.3 us
    all_to_all x1, blocking collectives, body(): table = lax.all_to_all(to_all, BOTH, 0, 0, tiled=True).reshape(-1, LANES)  14.8 us
    ppermute x8, waiting for transfers between devices, swap(): return lax.ppermute(x, axis, pairs)  5.57 us
    pallas_call x1, Pallas kernels, body(): call(functools.partial(coarse_and_after, first_brick), [forces.shape], [(...  4.18 us
    pallas_call x1, Pallas kernels, body(): call(fine_before, [(5, half, mid_rows, LANES), (5, half // 2, mid_rows, L...  1.54 us
    pallas_call x1, Pallas kernels, body(): call(pack_rows, [(5,) + block, side, side, middle_side, middle_side], [bl...  1.12 us
    pallas_call x1, Pallas kernels, body(): call(fine_inner, [(3,) + block, block, block, weighed, weighed] + [(3,) +...  0.94 us
  transfers between devices with their start and end apart: 8, of which 3 were waited for; matrix products, arithmetic and copies ran while one was open for 0% of the time, Pallas kernels for 2%

profile of v5, /device:TPU:0, one launch (start us, length us, event | category | flops | bytes accessed | tf_op | source)
XLA Modules:
  0.0 45.3 jit_solution(2958157080195574522)
XLA Ops:
  0.0 1.1 %pack_rows.1 = (f32[5,8,16,128]{3,2,1,0:T(8,128)S(1)}, f32[408,128]{1,0:T(8,128)S(1)}, f32[408,128]{1,0:T(8,128)S(1)}, f32[256,128]{1,0:T(8,128)S(1)}, f32[256,128]{1,0:T(8,128)S(1)}) custom-call(f32[3,8,16,128]{3,2,1,0:T(8,128)} %forces.1, f32[8,16,128]{2,1,0:T(8,128)} %modulus.1, s32[8,16,128]{2,1,0:T(8,128)} %occupancy.1, s32[8,16,128]{2,1,0:T(8,128)} %bonded.1), custom_call_target="tpu_custom_call" | custom-call | tf_op jit(solution)/shard_map/pack_rows/pallas_call | solution.py:835
  1.1 3.0 %collective-permute-start = (f32[408,128]{1,0:T(8,128)S(1)}, f32[408,128]{1,0:T(8,128)S(1)}, u32[]{:S(2)}, u32[]{:S(2)}) collective-permute-start(f32[408,128]{1,0:T(8,128)S(1)} %get-tuple-element.43), channel_id=1, source_target_pairs={{0,1},{1,0},{2,3},{3,2},{4,5},{5,4},{6,7},{7,6},{8,9},{9,8},{10,11... | collective-permute-start | bytes 626696 | tf_op jit(solution)/shard_map/ppermute | solution.py:819
  4.2 0.7 %collective-permute-start.1 = (f32[408,128]{1,0:T(8,128)S(1)}, f32[408,128]{1,0:T(8,128)S(1)}, u32[]{:S(2)}, u32[]{:S(2)}) collective-permute-start(f32[408,128]{1,0:T(8,128)S(1)} %get-tuple-element.44), channel_id=1, source_target_pairs={{1,2},{2,1},{3,4},{4,3},{5,6},{6,5},{9,10},{10,9},{11,12},{12,11},... | collective-permute-start | bytes 626696 | tf_op jit(solution)/shard_map/ppermute | solution.py:819
  4.8 0.7 %collective-permute-start.2 = (f32[256,128]{1,0:T(8,128)S(1)}, f32[256,128]{1,0:T(8,128)S(1)}, u32[]{:S(2)}, u32[]{:S(2)}) collective-permute-start(f32[256,128]{1,0:T(8,128)S(1)} %get-tuple-element.45), channel_id=1, source_target_pairs={{8,16},{16,8},{9,17},{17,9},{10,18},{18,10},{11,19},{19,11},{12,20... | collective-permute-start | bytes 393224 | tf_op jit(solution)/shard_map/ppermute | solution.py:819
  5.5 2.9 %collective-permute-start.3 = (f32[256,128]{1,0:T(8,128)S(1)}, f32[256,128]{1,0:T(8,128)S(1)}, u32[]{:S(2)}, u32[]{:S(2)}) collective-permute-start(f32[256,128]{1,0:T(8,128)S(1)} %get-tuple-element.46), channel_id=1, source_target_pairs={{0,8},{8,0},{16,24},{24,16},{1,9},{9,1},{17,25},{25,17},{2,10},{10... | collective-permute-start | bytes 393224 | tf_op jit(solution)/shard_map/ppermute | solution.py:819
  8.4 0.0 collective-permute-done.2.middle_b
  8.4 1.0 %collective-permute-done.3.middle_a = f32[256,128]{1,0:T(8,128)S(1)} collective-permute-done((f32[256,128]{1,0:T(8,128)S(1)}, f32[256,128]{1,0:T(8,128)S(1)}, u32[]{:S(2)}, u32[]{:S(2)}) %collective-permute-start.3) | collective-permute-done | bytes 131104 | tf_op jit(solution)/shard_map/ppermute | solution.py:819
  9.4 3.7 %collective-permute-done.from_c = f32[408,128]{1,0:T(8,128)S(1)} collective-permute-done((f32[408,128]{1,0:T(8,128)S(1)}, f32[408,128]{1,0:T(8,128)S(1)}, u32[]{:S(2)}, u32[]{:S(2)}) %collective-permute-start) | collective-permute-done | bytes 208928 | tf_op jit(solution)/shard_map/ppermute | solution.py:819
  13.1 0.0 collective-permute-done.1.from_d
  13.1 0.1 pack_corners.1
  13.1 0.1 collective-permute-start.4
  13.2 0.7 %collective-permute-start.5 = (f32[258,128]{1,0:T(8,128)S(1)}, f32[258,128]{1,0:T(8,128)S(1)}, u32[]{:S(2)}, u32[]{:S(2)}) collective-permute-start(f32[258,128]{1,0:T(8,128)S(1)} %get-tuple-element.59), channel_id=1, source_target_pairs={{8,16},{16,8},{9,17},{17,9},{10,18},{18,10},{11,19},{19,11},{12,20... | collective-permute-start | bytes 396296 | tf_op jit(solution)/shard_map/ppermute | solution.py:819
  13.9 0.9 %fine_inner.1 = (f32[3,8,40,128]{3,2,1,0:T(8,128)S(1)}, f32[8,40,128]{2,1,0:T(8,128)S(1)}, f32[8,40,128]{2,1,0:T(8,128)S(1)}, f32[6,40,128]{2,1,0:T(8,128)S(1)},...) custom-call(f32[5,8,16,128]{3,2,1,0:T(8,128)S(1)} %get-tuple-element, ...), custom_call_target="tpu_custom_call" | custom-call | flops 10000000 | bytes 4000000 | tf_op jit(solution)/shard_map/fine_inner/pallas_call | solution.py:868
  14.8 0.0 collective-permute-done.4.corner_a
  14.8 0.0 collective-permute-done.5.corner_b
  14.8 1.5 %fine_before.1 = (f32[5,4,16,128]{3,2,1,0:T(8,128)S(1)}, f32[5,2,16,128]{3,2,1,0:T(8,128)S(1)}, f32[3,8,24,128]{3,2,1,0:T(8,128)S(1)}, f32[3,2,24,128]{3,2,1,0:T...) custom-call(f32[3,8,40,128]{3,2,1,0:T(8,128)S(1)} %get-tuple-element.48.source_in, ...), custom_call_target="tpu_custom_call" | custom-call | tf_op jit(solution)/shard_map/fine_before/pallas_call | solution.py:882
  16.4 0.7 %collective-permute-start.6 = (f32[5,2,16,128]{3,2,1,0:T(8,128)S(1)}, f32[5,2,16,128]{3,2,1,0:T(8,128)S(1)}, u32[]{:S(2)}, u32[]{:S(2)}) collective-permute-start(f32[5,2,16,128]{3,2,1,0:T(8,128)S(1)} %get-tuple-element.62), channel_id=1, source_target_pairs={{8,16},{16,8},{9,17},{17,9},{10,18},{18,10},{11,19},{19,11},{12,20... | collective-permute-start | bytes 245768 | tf_op jit(solution)/shard_map/ppermute | solution.py:819
  17.1 7.6 %collective-permute-start.7 = (f32[5,2,16,128]{3,2,1,0:T(8,128)S(1)}, f32[5,2,16,128]{3,2,1,0:T(8,128)S(1)}, u32[]{:S(2)}, u32[]{:S(2)}) collective-permute-start(f32[5,2,16,128]{3,2,1,0:T(8,128)S(1)} %get-tuple-element.62), channel_id=1, source_target_pairs={{0,8},{8,0},{16,24},{24,16},{1,9},{9,1},{17,25},{25,17},{2,10},{10... | collective-permute-start | bytes 245768 | tf_op jit(solution)/shard_map/ppermute | solution.py:819
  24.6 0.0 collective-permute-done.6.from_b
  24.6 0.9 %collective-permute-done.7.from_a = f32[5,2,16,128]{3,2,1,0:T(8,128)S(1)} collective-permute-done((f32[5,2,16,128]{3,2,1,0:T(8,128)S(1)}, f32[5,2,16,128]{3,2,1,0:T(8,128)S(1)}, u32[]{:S(2)}, u32[]{:S(2)}) %collective-permute-start.7) | collective-permute-done | bytes 81952 | tf_op jit(solution)/shard_map/ppermute | solution.py:819
  25.6 0.7 %middle_before.1 = (f32[320,128]{1,0:T(8,128)S(1)}, f32[3,12,16,128]{3,2,1,0:T(8,128)S(1)}, f32[3,12,16,128]{3,2,1,0:T(8,128)S(1)}, f32[12,16,128]{2,1,0:T(8,128...) custom-call(f32[5,4,16,128]{3,2,1,0:T(8,128)S(1)} %get-tuple-element.60.own, ...), custom_call_target="tpu_custom_call" | custom-call | tf_op jit(solution)/shard_map/middle_before/pallas_call | solution.py:895
  26.3 14.8 %all_to_all.5 = f32[160,2,128]{2,1,0:T(2,128)S(1)} all-to-all(f32[160,2,128]{2,1,0:T(2,128)S(1)} %bitcast.3), channel_id=1, replica_groups=mesh['len'=4,'brick'=8] {'len','brick'}, dimensions={0} | all-to-all | bytes 327680 | tf_op jit(solution)/shard_map/all_to_all | solution.py:903
  41.2 4.2 %coarse_and_after.1 = f32[3,8,16,128]{3,2,1,0:T(8,128)} custom-call(f32[320,128]{1,0:T(8,128)S(1)} %bitcast.2, f32[3,12,16,128]{3,2,1,0:T(8,128)S(1)} %get-tuple-element.64.v2_mid, f32[3,12,16,128]{3,2,1,0:T(8,128)S(1)} %get-tuple-element.65.source_mid, f32[12,16,128]{2,1,0:T(8,128)S(1)} %get-tuple-element.66.quarter_mid, ...), custom_call_target="tpu_custom_call" | custom-call | tf_op jit(solution)/shard_map/coarse_and_after/pallas_call | solution.py:915
Async XLA Ops:
  1.1 11.9 %collective-permute-start = (f32[408,128]{1,0:T(8,128)S(1)}, f32[408,128]{1,0:T(8,128)S(1)}, u32[]{:S(2)}, u32[]{:S(2)}) collective-permute-start(f32[408,128]{1,0:T(8,128)S(1)} %get-tuple-element.43), channel_id=1, source_target_pairs={{0,1},{1,0},{2,3},{3,2},{4,5},{5,4},{6,7},{7,6},{8,9},{9,8},{10,11... | collective-permute-start | bytes 626696 | tf_op jit(solution)/shard_map/ppermute | solution.py:819
  4.2 8.9 %collective-permute-start.1 = (f32[408,128]{1,0:T(8,128)S(1)}, f32[408,128]{1,0:T(8,128)S(1)}, u32[]{:S(2)}, u32[]{:S(2)}) collective-permute-start(f32[408,128]{1,0:T(8,128)S(1)} %get-tuple-element.44), channel_id=1, source_target_pairs={{1,2},{2,1},{3,4},{4,3},{5,6},{6,5},{9,10},{10,9},{11,12},{12,11},... | collective-permute-start | bytes 626696 | tf_op jit(solution)/shard_map/ppermute | solution.py:819
  4.8 3.6 %collective-permute-start.2 = (f32[256,128]{1,0:T(8,128)S(1)}, f32[256,128]{1,0:T(8,128)S(1)}, u32[]{:S(2)}, u32[]{:S(2)}) collective-permute-start(f32[256,128]{1,0:T(8,128)S(1)} %get-tuple-element.45), channel_id=1, source_target_pairs={{8,16},{16,8},{9,17},{17,9},{10,18},{18,10},{11,19},{19,11},{12,20... | collective-permute-start | bytes 393224 | tf_op jit(solution)/shard_map/ppermute | solution.py:819
  5.5 3.9 %collective-permute-start.3 = (f32[256,128]{1,0:T(8,128)S(1)}, f32[256,128]{1,0:T(8,128)S(1)}, u32[]{:S(2)}, u32[]{:S(2)}) collective-permute-start(f32[256,128]{1,0:T(8,128)S(1)} %get-tuple-element.46), channel_id=1, source_target_pairs={{0,8},{8,0},{16,24},{24,16},{1,9},{9,1},{17,25},{25,17},{2,10},{10... | collective-permute-start | bytes 393224 | tf_op jit(solution)/shard_map/ppermute | solution.py:819
  13.1 1.7 %collective-permute-start.4 = (f32[258,128]{1,0:T(8,128)S(1)}, f32[258,128]{1,0:T(8,128)S(1)}, u32[]{:S(2)}, u32[]{:S(2)}) collective-permute-start(f32[258,128]{1,0:T(8,128)S(1)} %get-tuple-element.47.to_a), channel_id=1, source_target_pairs={{0,8},{8,0},{16,24},{24,16},{1,9},{9,1},{17,25},{25,17},{2,10},{10... | collective-permute-start | bytes 396296 | tf_op jit(solution)/shard_map/ppermute | solution.py:819
  13.2 1.6 %collective-permute-start.5 = (f32[258,128]{1,0:T(8,128)S(1)}, f32[258,128]{1,0:T(8,128)S(1)}, u32[]{:S(2)}, u32[]{:S(2)}) collective-permute-start(f32[258,128]{1,0:T(8,128)S(1)} %get-tuple-element.59), channel_id=1, source_target_pairs={{8,16},{16,8},{9,17},{17,9},{10,18},{18,10},{11,19},{19,11},{12,20... | collective-permute-start | bytes 396296 | tf_op jit(solution)/shard_map/ppermute | solution.py:819
  16.4 8.3 %collective-permute-start.6 = (f32[5,2,16,128]{3,2,1,0:T(8,128)S(1)}, f32[5,2,16,128]{3,2,1,0:T(8,128)S(1)}, u32[]{:S(2)}, u32[]{:S(2)}) collective-permute-start(f32[5,2,16,128]{3,2,1,0:T(8,128)S(1)} %get-tuple-element.62), channel_id=1, source_target_pairs={{8,16},{16,8},{9,17},{17,9},{10,18},{18,10},{11,19},{19,11},{12,20... | collective-permute-start | bytes 245768 | tf_op jit(solution)/shard_map/ppermute | solution.py:819
  17.1 8.5 %collective-permute-start.7 = (f32[5,2,16,128]{3,2,1,0:T(8,128)S(1)}, f32[5,2,16,128]{3,2,1,0:T(8,128)S(1)}, u32[]{:S(2)}, u32[]{:S(2)}) collective-permute-start(f32[5,2,16,128]{3,2,1,0:T(8,128)S(1)} %get-tuple-element.62), channel_id=1, source_target_pairs={{0,8},{8,0},{16,24},{24,16},{1,9},{9,1},{17,25},{25,17},{2,10},{10... | collective-permute-start | bytes 245768 | tf_op jit(solution)/shard_map/ppermute | solution.py:819

commit v6 on v5

--- a/solution.py
+++ b/solution.py
@@ -208,6 +208,34 @@
             put(k, p, v[k] + s * r[k])
 
 
+def sweep_rows(field, quarter, weight, step, source, planes, rows, lane, put):
+    near = [slice(rows.start + by, rows.stop + by) for by in (-1, 0, 1)]
+    q_at = remember(lambda p: [quarter.cut(p, r) for r in near])
+    v_at = [remember(lambda p, k=k: [field(k, p, r) for r in near]) for k in range(3)]
+
+    def over_rows(x):
+        return (x[0] + x[2]) + (x[1] + x[1])
+
+    rows_v = [remember(lambda p, k=k: over_rows(v_at[k](p))) for k in range(3)]
+    rows_w = [
+        remember(lambda p, k=k: over_rows([q * v for q, v in zip(q_at(p), v_at[k](p))]))
+        for k in range(3)
+    ]
+    pairs = [
+        [remember(lambda p, x=x: x(p) + x(p + 1)) for x in group] for group in (rows_v, rows_w)
+    ]
+    for p in planes:
+        q = q_at(p)[1]
+        beside = lane.beside(q)
+        v = [x(p)[1] for x in v_at]
+        coupled = (4.0 * COUPLING) * q * (v[0] + v[1] + v[2])
+        e, s = weight.cut(p, rows), step.cut(p, rows)
+        for k in range(3):
+            x, y = [group[k](p - 1) + group[k](p) for group in pairs]
+            sums = lane.blend(x, y, q, *beside)
+            put(k, p, v[k] + s * (source.cut((k, p), rows) - e * v[k] + sums - coupled))
+
+
 def stiffness_sum(quarter, planes, bounds, lane):
     q_at = remember(within(lambda p: quarter[p], *bounds))
     for p in planes:
@@ -251,6 +279,13 @@
             return ref[at[0], i]
         ref, i = self.spots[at]
         return ref[i]
+
+    def cut(self, at, rows):
+        if isinstance(at, tuple):
+            ref, i = self.spots[at[1]]
+            return ref[at[0], i, rows, :]
+        ref, i = self.spots[at]
+        return ref[i, rows, :]
 
 
 def vmem(shape):
@@ -471,7 +506,7 @@
 
 def fine_before(
     source_in, quarter_in, shift_in, weight_in, step_in, v1_in, v2_in, rest_in,
-    coarse_q_in, shift1, sums_in, middle_b, middle_a, corner_a, corner_b,
+    coarse_q_in, shift1, sums_in, middle_b, middle_a, corner_b, corner_a,
     own_coarse, to_len, *more,
 ):
     *kept, v2_out, source_out, quarter_out, weight_out, step_out, shift_out, v1_out, work, coarse_q = more
@@ -530,8 +565,12 @@
         for k in range(3):
             v1_out[k, p] = st * source[k, p]
 
+    numbers = [x for _, x in kept_planes(planes)]
+    kept_rows = slice(WIDE - HALO, WIDE + rows + HALO)
+
     def put_v2(k, p, value):
         v2_out[k, p] = value
+        kept[0][k, numbers[0].index(p)] = value[kept_rows]
 
     sweep(
         lambda k, p: v1[k, p], quarter, weight, step, source,
@@ -584,11 +623,7 @@
         for i in range(coarse_planes // 2):
             to_len[k, i] = jnp.where(even, own_coarse[k, 2 * i], own_coarse[k, 2 * i + 1])
 
-    keep(
-        slice(WIDE - HALO, WIDE + rows + HALO), kept,
-        (v2, source, quarter, weight, step),
-        [x for _, x in kept_planes(planes)],
-    )
+    keep(kept_rows, kept, (v2, source, quarter, weight, step), [[]] + numbers[1:])
 
 
 def middle_before(
@@ -792,11 +827,12 @@
     )
 
     def put_out(k, p, value):
-        out[k, p - HALO] = value[HALO : rows0 - HALO]
-
-    sweep(
-        lambda k, p: x_fine[k, p], quarter_fine, weight_fine, step_fine, source_fine,
-        range(HALO, planes0 - HALO), bounds0, lane0, put_out, beside0,
+        out[k, p - HALO] = value
+
+    own_rows = slice(HALO, rows0 - HALO)
+    sweep_rows(
+        lambda k, p, r: x_fine[k, p, r, :], quarter_fine, weight_fine, step_fine, source_fine,
+        range(HALO, planes0 - HALO), own_rows, Lane(rows0 - 2 * HALO, 1), put_out,
     )
 
 
@@ -877,7 +913,7 @@
         in_specs=[pl.BlockSpec(memory_space=pltpu.VMEM)] * 3
         + [pl.BlockSpec(memory_space=pl.ANY)],
         cost_estimate=pl.CostEstimate(flops=10**7, bytes_accessed=4 * 10**6, transcendentals=0),
-    )(own, from_c, from_d, to_a)
+    )(own, from_c, from_d, to_b)
     inner, cells, kept_inner = inner[:11], inner[11], inner[12:]
     own, to_len, *kept_outer = call(
         fine_before,
@@ -885,7 +921,7 @@
         [field, field, cell, cell, cell, cell, field]
         + [(4, half, ext_rows, LANES), (2,) + coarse[1:]],
         name="fine_before",
-    )(*inner, middle_b, middle_a, corner_a, corner_b)
+    )(*inner, middle_b, middle_a, corner_b, corner_a)
     from_a = swap(to_len, "len", 0)
     from_b = swap(to_len, "len", 1)
 

time: 45.6 us -> 45.4 us (level)
  no operation moved by 1% of the time
where the time goes in v6:
time: 45.4 us; the launch traced here: 45.1 us
  starting transfers between devices  16.2 us (36%)
  blocking collectives  14.8 us (33%)
  Pallas kernels  8.43 us (19%)
  waiting for transfers between devices  5.61 us (12%)
    ppermute x8, starting transfers between devices, swap(): return lax.ppermute(x, axis, pairs)  16.2 us
    all_to_all x1, blocking collectives, body(): table = lax.all_to_all(to_all, BOTH, 0, 0, tiled=True).reshape(-1, LANES)  14.8 us
    ppermute x8, waiting for transfers between devices, swap(): return lax.ppermute(x, axis, pairs)  5.61 us
    pallas_call x1, Pallas kernels, body(): call(functools.partial(coarse_and_after, first_brick), [forces.shape], [(...  4.06 us
    pallas_call x1, Pallas kernels, body(): call(fine_before, [(5, half, mid_rows, LANES), (5, half // 2, mid_rows, L...  1.52 us
    pallas_call x1, Pallas kernels, body(): call(pack_rows, [(5,) + block, side, side, middle_side, middle_side], [bl...  1.12 us
    pallas_call x1, Pallas kernels, body(): call(fine_inner, [(3,) + block, block, block, weighed, weighed] + [(3,) +...  0.94 us
  transfers between devices with their start and end apart: 8, of which 3 were waited for; matrix products, arithmetic and copies ran while one was open for 0% of the time, Pallas kernels for 2%

profile of v6, /device:TPU:0, one launch (start us, length us, event | category | flops | bytes accessed | tf_op | source)
XLA Modules:
  0.0 45.1 jit_solution(12824234128608505801)
XLA Ops:
  0.0 1.1 %pack_rows.1 = (f32[5,8,16,128]{3,2,1,0:T(8,128)S(1)}, f32[408,128]{1,0:T(8,128)S(1)}, f32[408,128]{1,0:T(8,128)S(1)}, f32[256,128]{1,0:T(8,128)S(1)}, f32[256,128]{1,0:T(8,128)S(1)}) custom-call(f32[3,8,16,128]{3,2,1,0:T(8,128)} %forces.1, f32[8,16,128]{2,1,0:T(8,128)} %modulus.1, s32[8,16,128]{2,1,0:T(8,128)} %occupancy.1, s32[8,16,128]{2,1,0:T(8,128)} %bonded.1), custom_call_target="tpu_custom_call" | custom-call | tf_op jit(solution)/shard_map/pack_rows/pallas_call | solution.py:871
  1.1 3.0 %collective-permute-start = (f32[408,128]{1,0:T(8,128)S(1)}, f32[408,128]{1,0:T(8,128)S(1)}, u32[]{:S(2)}, u32[]{:S(2)}) collective-permute-start(f32[408,128]{1,0:T(8,128)S(1)} %get-tuple-element.43), channel_id=1, source_target_pairs={{0,1},{1,0},{2,3},{3,2},{4,5},{5,4},{6,7},{7,6},{8,9},{9,8},{10,11... | collective-permute-start | bytes 626696 | tf_op jit(solution)/shard_map/ppermute | solution.py:855
  4.2 0.7 %collective-permute-start.1 = (f32[408,128]{1,0:T(8,128)S(1)}, f32[408,128]{1,0:T(8,128)S(1)}, u32[]{:S(2)}, u32[]{:S(2)}) collective-permute-start(f32[408,128]{1,0:T(8,128)S(1)} %get-tuple-element.44), channel_id=1, source_target_pairs={{1,2},{2,1},{3,4},{4,3},{5,6},{6,5},{9,10},{10,9},{11,12},{12,11},... | collective-permute-start | bytes 626696 | tf_op jit(solution)/shard_map/ppermute | solution.py:855
  4.8 0.7 %collective-permute-start.2 = (f32[256,128]{1,0:T(8,128)S(1)}, f32[256,128]{1,0:T(8,128)S(1)}, u32[]{:S(2)}, u32[]{:S(2)}) collective-permute-start(f32[256,128]{1,0:T(8,128)S(1)} %get-tuple-element.45), channel_id=1, source_target_pairs={{8,16},{16,8},{9,17},{17,9},{10,18},{18,10},{11,19},{19,11},{12,20... | collective-permute-start | bytes 393224 | tf_op jit(solution)/shard_map/ppermute | solution.py:855
  5.5 2.9 %collective-permute-start.3 = (f32[256,128]{1,0:T(8,128)S(1)}, f32[256,128]{1,0:T(8,128)S(1)}, u32[]{:S(2)}, u32[]{:S(2)}) collective-permute-start(f32[256,128]{1,0:T(8,128)S(1)} %get-tuple-element.46), channel_id=1, source_target_pairs={{0,8},{8,0},{16,24},{24,16},{1,9},{9,1},{17,25},{25,17},{2,10},{10... | collective-permute-start | bytes 393224 | tf_op jit(solution)/shard_map/ppermute | solution.py:855
  8.4 0.0 collective-permute-done.2.middle_b
  8.4 1.0 %collective-permute-done.3.middle_a = f32[256,128]{1,0:T(8,128)S(1)} collective-permute-done((f32[256,128]{1,0:T(8,128)S(1)}, f32[256,128]{1,0:T(8,128)S(1)}, u32[]{:S(2)}, u32[]{:S(2)}) %collective-permute-start.3) | collective-permute-done | bytes 131104 | tf_op jit(solution)/shard_map/ppermute | solution.py:855
  9.4 3.7 %collective-permute-done.from_c = f32[408,128]{1,0:T(8,128)S(1)} collective-permute-done((f32[408,128]{1,0:T(8,128)S(1)}, f32[408,128]{1,0:T(8,128)S(1)}, u32[]{:S(2)}, u32[]{:S(2)}) %collective-permute-start) | collective-permute-done | bytes 208928 | tf_op jit(solution)/shard_map/ppermute | solution.py:855
  13.1 0.0 collective-permute-done.1.from_d
  13.1 0.1 pack_corners.1
  13.1 0.7 %collective-permute-start.4 = (f32[258,128]{1,0:T(8,128)S(1)}, f32[258,128]{1,0:T(8,128)S(1)}, u32[]{:S(2)}, u32[]{:S(2)}) collective-permute-start(f32[258,128]{1,0:T(8,128)S(1)} %get-tuple-element.47.to_a), channel_id=1, source_target_pairs={{8,16},{16,8},{9,17},{17,9},{10,18},{18,10},{11,19},{19,11},{12,20... | collective-permute-start | bytes 396296 | tf_op jit(solution)/shard_map/ppermute | solution.py:855
  13.8 2.9 %collective-permute-start.5 = (f32[258,128]{1,0:T(8,128)S(1)}, f32[258,128]{1,0:T(8,128)S(1)}, u32[]{:S(2)}, u32[]{:S(2)}) collective-permute-start(f32[258,128]{1,0:T(8,128)S(1)} %get-tuple-element.59), channel_id=1, source_target_pairs={{0,8},{8,0},{16,24},{24,16},{1,9},{9,1},{17,25},{25,17},{2,10},{10... | collective-permute-start | bytes 396296 | tf_op jit(solution)/shard_map/ppermute | solution.py:855
  16.7 0.9 %fine_inner.1 = (f32[3,8,40,128]{3,2,1,0:T(8,128)S(1)}, f32[8,40,128]{2,1,0:T(8,128)S(1)}, f32[8,40,128]{2,1,0:T(8,128)S(1)}, f32[6,40,128]{2,1,0:T(8,128)S(1)},...) custom-call(f32[5,8,16,128]{3,2,1,0:T(8,128)S(1)} %get-tuple-element, ...), custom_call_target="tpu_custom_call" | custom-call | flops 10000000 | bytes 4000000 | tf_op jit(solution)/shard_map/fine_inner/pallas_call | solution.py:904
  17.6 0.0 collective-permute-done.4.corner_b
  17.7 0.0 collective-permute-done.5.corner_a
  17.7 1.5 %fine_before.1 = (f32[5,4,16,128]{3,2,1,0:T(8,128)S(1)}, f32[5,2,16,128]{3,2,1,0:T(8,128)S(1)}, f32[3,8,24,128]{3,2,1,0:T(8,128)S(1)}, f32[3,2,24,128]{3,2,1,0:T...) custom-call(f32[3,8,40,128]{3,2,1,0:T(8,128)S(1)} %get-tuple-element.48.source_in, ...), custom_call_target="tpu_custom_call" | custom-call | tf_op jit(solution)/shard_map/fine_before/pallas_call | solution.py:918
  19.2 0.7 %collective-permute-start.6 = (f32[5,2,16,128]{3,2,1,0:T(8,128)S(1)}, f32[5,2,16,128]{3,2,1,0:T(8,128)S(1)}, u32[]{:S(2)}, u32[]{:S(2)}) collective-permute-start(f32[5,2,16,128]{3,2,1,0:T(8,128)S(1)} %get-tuple-element.62), channel_id=1, source_target_pairs={{8,16},{16,8},{9,17},{17,9},{10,18},{18,10},{11,19},{19,11},{12,20... | collective-permute-start | bytes 245768 | tf_op jit(solution)/shard_map/ppermute | solution.py:855
  19.9 4.7 %collective-permute-start.7 = (f32[5,2,16,128]{3,2,1,0:T(8,128)S(1)}, f32[5,2,16,128]{3,2,1,0:T(8,128)S(1)}, u32[]{:S(2)}, u32[]{:S(2)}) collective-permute-start(f32[5,2,16,128]{3,2,1,0:T(8,128)S(1)} %get-tuple-element.62), channel_id=1, source_target_pairs={{0,8},{8,0},{16,24},{24,16},{1,9},{9,1},{17,25},{25,17},{2,10},{10... | collective-permute-start | bytes 245768 | tf_op jit(solution)/shard_map/ppermute | solution.py:855
  24.6 0.0 collective-permute-done.6.from_b
  24.6 0.9 %collective-permute-done.7.from_a = f32[5,2,16,128]{3,2,1,0:T(8,128)S(1)} collective-permute-done((f32[5,2,16,128]{3,2,1,0:T(8,128)S(1)}, f32[5,2,16,128]{3,2,1,0:T(8,128)S(1)}, u32[]{:S(2)}, u32[]{:S(2)}) %collective-permute-start.7) | collective-permute-done | bytes 81952 | tf_op jit(solution)/shard_map/ppermute | solution.py:855
  25.5 0.7 %middle_before.1 = (f32[320,128]{1,0:T(8,128)S(1)}, f32[3,12,16,128]{3,2,1,0:T(8,128)S(1)}, f32[3,12,16,128]{3,2,1,0:T(8,128)S(1)}, f32[12,16,128]{2,1,0:T(8,128...) custom-call(f32[5,4,16,128]{3,2,1,0:T(8,128)S(1)} %get-tuple-element.60.own, ...), custom_call_target="tpu_custom_call" | custom-call | tf_op jit(solution)/shard_map/middle_before/pallas_call | solution.py:931
  26.2 14.8 %all_to_all.5 = f32[160,2,128]{2,1,0:T(2,128)S(1)} all-to-all(f32[160,2,128]{2,1,0:T(2,128)S(1)} %bitcast.3), channel_id=1, replica_groups=mesh['len'=4,'brick'=8] {'len','brick'}, dimensions={0} | all-to-all | bytes 327680 | tf_op jit(solution)/shard_map/all_to_all | solution.py:939
  41.1 4.1 %coarse_and_after.1 = f32[3,8,16,128]{3,2,1,0:T(8,128)} custom-call(f32[320,128]{1,0:T(8,128)S(1)} %bitcast.2, f32[3,12,16,128]{3,2,1,0:T(8,128)S(1)} %get-tuple-element.64.v2_mid, f32[3,12,16,128]{3,2,1,0:T(8,128)S(1)} %get-tuple-element.65.source_mid, f32[12,16,128]{2,1,0:T(8,128)S(1)} %get-tuple-element.66.quarter_mid, ...), custom_call_target="tpu_custom_call" | custom-call | tf_op jit(solution)/shard_map/coarse_and_after/pallas_call | solution.py:951
Async XLA Ops:
  1.1 11.9 %collective-permute-start = (f32[408,128]{1,0:T(8,128)S(1)}, f32[408,128]{1,0:T(8,128)S(1)}, u32[]{:S(2)}, u32[]{:S(2)}) collective-permute-start(f32[408,128]{1,0:T(8,128)S(1)} %get-tuple-element.43), channel_id=1, source_target_pairs={{0,1},{1,0},{2,3},{3,2},{4,5},{5,4},{6,7},{7,6},{8,9},{9,8},{10,11... | collective-permute-start | bytes 626696 | tf_op jit(solution)/shard_map/ppermute | solution.py:855
  4.2 8.9 %collective-permute-start.1 = (f32[408,128]{1,0:T(8,128)S(1)}, f32[408,128]{1,0:T(8,128)S(1)}, u32[]{:S(2)}, u32[]{:S(2)}) collective-permute-start(f32[408,128]{1,0:T(8,128)S(1)} %get-tuple-element.44), channel_id=1, source_target_pairs={{1,2},{2,1},{3,4},{4,3},{5,6},{6,5},{9,10},{10,9},{11,12},{12,11},... | collective-permute-start | bytes 626696 | tf_op jit(solution)/shard_map/ppermute | solution.py:855
  4.8 3.6 %collective-permute-start.2 = (f32[256,128]{1,0:T(8,128)S(1)}, f32[256,128]{1,0:T(8,128)S(1)}, u32[]{:S(2)}, u32[]{:S(2)}) collective-permute-start(f32[256,128]{1,0:T(8,128)S(1)} %get-tuple-element.45), channel_id=1, source_target_pairs={{8,16},{16,8},{9,17},{17,9},{10,18},{18,10},{11,19},{19,11},{12,20... | collective-permute-start | bytes 393224 | tf_op jit(solution)/shard_map/ppermute | solution.py:855
  5.5 3.9 %collective-permute-start.3 = (f32[256,128]{1,0:T(8,128)S(1)}, f32[256,128]{1,0:T(8,128)S(1)}, u32[]{:S(2)}, u32[]{:S(2)}) collective-permute-start(f32[256,128]{1,0:T(8,128)S(1)} %get-tuple-element.46), channel_id=1, source_target_pairs={{0,8},{8,0},{16,24},{24,16},{1,9},{9,1},{17,25},{25,17},{2,10},{10... | collective-permute-start | bytes 393224 | tf_op jit(solution)/shard_map/ppermute | solution.py:855
  13.1 4.5 %collective-permute-start.4 = (f32[258,128]{1,0:T(8,128)S(1)}, f32[258,128]{1,0:T(8,128)S(1)}, u32[]{:S(2)}, u32[]{:S(2)}) collective-permute-start(f32[258,128]{1,0:T(8,128)S(1)} %get-tuple-element.47.to_a), channel_id=1, source_target_pairs={{8,16},{16,8},{9,17},{17,9},{10,18},{18,10},{11,19},{19,11},{12,20... | collective-permute-start | bytes 396296 | tf_op jit(solution)/shard_map/ppermute | solution.py:855
  13.8 3.9 %collective-permute-start.5 = (f32[258,128]{1,0:T(8,128)S(1)}, f32[258,128]{1,0:T(8,128)S(1)}, u32[]{:S(2)}, u32[]{:S(2)}) collective-permute-start(f32[258,128]{1,0:T(8,128)S(1)} %get-tuple-element.59), channel_id=1, source_target_pairs={{0,8},{8,0},{16,24},{24,16},{1,9},{9,1},{17,25},{25,17},{2,10},{10... | collective-permute-start | bytes 396296 | tf_op jit(solution)/shard_map/ppermute | solution.py:855
  19.2 5.3 %collective-permute-start.6 = (f32[5,2,16,128]{3,2,1,0:T(8,128)S(1)}, f32[5,2,16,128]{3,2,1,0:T(8,128)S(1)}, u32[]{:S(2)}, u32[]{:S(2)}) collective-permute-start(f32[5,2,16,128]{3,2,1,0:T(8,128)S(1)} %get-tuple-element.62), channel_id=1, source_target_pairs={{8,16},{16,8},{9,17},{17,9},{10,18},{18,10},{11,19},{19,11},{12,20... | collective-permute-start | bytes 245768 | tf_op jit(solution)/shard_map/ppermute | solution.py:855
  19.9 5.6 %collective-permute-start.7 = (f32[5,2,16,128]{3,2,1,0:T(8,128)S(1)}, f32[5,2,16,128]{3,2,1,0:T(8,128)S(1)}, u32[]{:S(2)}, u32[]{:S(2)}) collective-permute-start(f32[5,2,16,128]{3,2,1,0:T(8,128)S(1)} %get-tuple-element.62), channel_id=1, source_target_pairs={{0,8},{8,0},{16,24},{24,16},{1,9},{9,1},{17,25},{25,17},{2,10},{10... | collective-permute-start | bytes 245768 | tf_op jit(solution)/shard_map/ppermute | solution.py:855

commit v7 on v6

--- a/solution.py
+++ b/solution.py
@@ -208,7 +208,7 @@
             put(k, p, v[k] + s * r[k])
 
 
-def sweep_rows(field, quarter, weight, step, source, planes, rows, lane, put):
+def defects_rows(field, quarter, weight, source, planes, rows, lane, apart=False):
     near = [slice(rows.start + by, rows.stop + by) for by in (-1, 0, 1)]
     q_at = remember(lambda p: [quarter.cut(p, r) for r in near])
     v_at = [remember(lambda p, k=k: [field(k, p, r) for r in near]) for k in range(3)]
@@ -226,14 +226,14 @@
     ]
     for p in planes:
         q = q_at(p)[1]
-        beside = lane.beside(q)
+        beside = None if apart else lane.beside(q)
         v = [x(p)[1] for x in v_at]
         coupled = (4.0 * COUPLING) * q * (v[0] + v[1] + v[2])
-        e, s = weight.cut(p, rows), step.cut(p, rows)
+        e = weight.cut(p, rows)
         for k in range(3):
             x, y = [group[k](p - 1) + group[k](p) for group in pairs]
-            sums = lane.blend(x, y, q, *beside)
-            put(k, p, v[k] + s * (source.cut((k, p), rows) - e * v[k] + sums - coupled))
+            sums = q * lane.smooth(x) + lane.smooth(y) if apart else lane.blend(x, y, q, *beside)
+            yield k, p, v[k], source.cut((k, p), rows) - e * v[k] + sums - coupled
 
 
 def stiffness_sum(quarter, planes, bounds, lane):
@@ -248,25 +248,6 @@
 
 def odd(axis):
     return lax.rem(lax.axis_index(axis), 2) == 1
-
-
-class From:
-    def __init__(self, ref, first):
-        self.ref, self.first = ref, first
-
-    def __getitem__(self, at):
-        if isinstance(at, tuple):
-            return self.ref[at[0], at[1] - self.first]
-        return self.ref[at - self.first]
-
-
-class Either:
-    def __init__(self, inner, span, outer):
-        self.inner, self.span, self.outer = From(inner, span[0]), span, outer
-
-    def __getitem__(self, at):
-        p = at[1] if isinstance(at, tuple) else at
-        return self.inner[at] if p in self.span else self.outer[at]
 
 
 class Stack:
@@ -444,7 +425,8 @@
 
     weighed, swept, left = inner_planes(planes)
     bounds = (HALO, HALO + planes)
-    source_at, quarter_at = From(source, HALO), From(quarter, HALO)
+    own_planes = range(HALO, HALO + planes)
+    source_at, quarter_at = Stack((source, own_planes)), Stack((quarter, own_planes))
     for p, w in stiffness_sum(quarter_at, weighed, bounds, lane):
         q, s, i = quarter_at[p], shift[p - HALO], p - weighed[0]
         total = w + s
@@ -453,26 +435,26 @@
         step[i] = st
         for k in range(3):
             v1[k, i] = st * source_at[k, p]
-    weight_at, step_at = From(weight, weighed[0]), From(step, weighed[0])
+    weight_at, step_at = Stack((weight, weighed)), Stack((step, weighed))
 
     def put_v2(k, p, value):
         v2[k, p - swept[0]] = value
 
-    v1_at, v2_at, near = From(v1, weighed[0]), From(v2, swept[0]), APART
+    v1_at, v2_at, near = Stack((v1, weighed)), Stack((v2, swept)), APART
     sweep(
         lambda k, p: v1_at[k, p], quarter_at, weight_at, step_at, source_at,
         swept, (weighed[0], weighed[-1] + 1), lane, put_v2, near,
     )
-    for p, _, r in defects(
-        lambda k, p: v2_at[k, p], quarter_at, weight_at, source_at,
-        left, (swept[0], swept[-1] + 1), lane, near,
+    outer = slice(WIDE - 2 * HALO, WIDE + rows + 2 * HALO)
+    lane_outer = Lane(outer.stop - outer.start, 1)
+    for k, p, _, r in defects_rows(
+        lambda k, p, r: v2_at.cut((k, p), r), quarter_at, weight_at, source_at,
+        left, outer, lane_outer, apart=True,
     ):
-        for k in range(3):
-            rest[k, p - left[0]] = r[k]
+        rest[k, p - left[0]] = r
 
     *kept, work = more
     half = rows // 2 + 2 * HALO
-    outer = slice(WIDE - 2 * HALO, WIDE + rows + 2 * HALO)
     beyond = slice(outer.start - 2, outer.stop + 2)
     count = planes // 2
     for i in range(count):
@@ -544,15 +526,19 @@
 
     weighed, swept, left = inner_planes(planes)
     here = range(HALO, HALO + planes)
-    source, quarter, shift = [
-        Either(x, here, y)
-        for x, y in ((source_in, source_out), (quarter_in, quarter_out), (shift_in, shift_out))
+    every = range(ext_planes)
+    source, quarter, shift, weight, step, v1, v2 = [
+        Stack((outer, every), (inner, numbers))
+        for inner, numbers, outer in (
+            (source_in, here, source_out),
+            (quarter_in, here, quarter_out),
+            (shift_in, here, shift_out),
+            (weight_in, weighed, weight_out),
+            (step_in, weighed, step_out),
+            (v1_in, weighed, v1_out),
+            (v2_in, swept, v2_out),
+        )
     ]
-    weight, step, v1 = [
-        Either(x, weighed, y)
-        for x, y in ((weight_in, weight_out), (step_in, step_out), (v1_in, v1_out))
-    ]
-    v2 = Either(v2_in, swept, v2_out)
 
     bounds, near = (0, ext_planes), APART
     others = [p for p in range(1, ext_planes - 1) if p not in weighed]
@@ -581,24 +567,28 @@
     outer = slice(WIDE - 2 * HALO, WIDE + rows + 2 * HALO)
     beyond = slice(outer.start - 2, outer.stop + 2)
     coarse_planes = planes // 2
-    rest = {p: [rest_in[k, p - left[0]] for k in range(3)] for p in left}
-    for p, _, r in defects(
-        lambda k, p: v2[k, p], quarter, weight, source,
-        [p for p in here if p not in left], bounds, lane, near,
+    rest = {(k, p): rest_in[k, p - left[0]] for p in left for k in range(3)}
+    height = outer.stop - outer.start
+    lane_outer = Lane(height, 1)
+    for k, p, _, r in defects_rows(
+        lambda k, p, r: v2.cut((k, p), r), quarter, weight, source,
+        [p for p in here if p not in left], outer, lane_outer, apart=True,
     ):
-        rest[p] = r
+        rest[k, p] = r
     for i in range(coarse_planes):
         p = HALO + 2 * i
         for k in range(3):
-            work[k, i] = rest[p][k] + rest[p + 1][k]
+            work[k, i, pl.ds(0, height), :] = rest[k, p] + rest[k, p + 1]
     for j, p in enumerate((HALO - 2, HALO + planes)):
         work[3, j] = quarter[p] + quarter[p + 1]
-    for k in range(4):
-        for i in range(2 if k == 3 else coarse_planes):
-            work[k, i] = lane.pair(work[k, i])
     for i in range(coarse_planes):
         for k in range(3):
-            own_coarse[k, i] = 0.125 * halves(work.at[k, i], outer)
+            work[k, i, pl.ds(0, height), :] = lane_outer.pair(work[k, i, pl.ds(0, height), :])
+    for j in range(2):
+        work[3, j] = lane.pair(work[3, j])
+    for i in range(coarse_planes):
+        for k in range(3):
+            own_coarse[k, i] = 0.125 * halves(work.at[k, i], slice(0, height))
 
     for j in range(2):
         coarse_q[j, pl.ds(7, half + 2), :] = (0.25 * 0.125) * halves(work.at[3, j], beyond)
@@ -826,14 +816,12 @@
         range(3, planes0 - 3), bounds0, lane0, put_fine, beside0,
     )
 
-    def put_out(k, p, value):
-        out[k, p - HALO] = value
-
     own_rows = slice(HALO, rows0 - HALO)
-    sweep_rows(
-        lambda k, p, r: x_fine[k, p, r, :], quarter_fine, weight_fine, step_fine, source_fine,
-        range(HALO, planes0 - HALO), own_rows, Lane(rows0 - 2 * HALO, 1), put_out,
-    )
+    for k, p, v, r in defects_rows(
+        lambda k, p, r: x_fine[k, p, r, :], quarter_fine, weight_fine, source_fine,
+        range(HALO, planes0 - HALO), own_rows, Lane(rows0 - 2 * HALO, 1),
+    ):
+        out[k, p - HALO] = v + step_fine.cut(p, own_rows) * r
 
 
 def call(kernel, outs, scratch=(), name=None, **more):
@@ -904,7 +892,7 @@
     inner = call(
         fine_inner,
         [(3,) + block, block, block, weighed, weighed]
-        + [(3,) + weighed, (3,) + swept, (3,) + left]
+        + [(3,) + weighed, (3,) + swept, (3, left[0], 2 * mid_rows, LANES)]
         + [coarse, (half, mid_rows, LANES), (half - 2, mid_rows, LANES)]
         + [(2, half // 2, half_rows // 2, LANES)]
         + kept_inner,

time: 45.4 us -> 45.4 us (level)
  no operation moved by 1% of the time
where the time goes in v7:
time: 45.4 us; the launch traced here: 45.1 us
  starting transfers between devices  16.2 us (36%)
  blocking collectives  14.8 us (33%)
  Pallas kernels  8.43 us (19%)
  waiting for transfers between devices  5.59 us (12%)
    ppermute x8, starting transfers between devices, swap(): return lax.ppermute(x, axis, pairs)  16.2 us
    all_to_all x1, blocking collectives, body(): table = lax.all_to_all(to_all, BOTH, 0, 0, tiled=True).reshape(-1, LANES)  14.8 us
    ppermute x8, waiting for transfers between devices, swap(): return lax.ppermute(x, axis, pairs)  5.59 us
    pallas_call x1, Pallas kernels, body(): call(functools.partial(coarse_and_after, first_brick), [forces.shape], [(...  4.07 us
    pallas_call x1, Pallas kernels, body(): call(fine_before, [(5, half, mid_rows, LANES), (5, half // 2, mid_rows, L...  1.5 us
    pallas_call x1, Pallas kernels, body(): call(pack_rows, [(5,) + block, side, side, middle_side, middle_side], [bl...  1.12 us
    pallas_call x1, Pallas kernels, body(): call(fine_inner, [(3,) + block, block, block, weighed, weighed] + [(3,) +...  0.95 us
  transfers between devices with their start and end apart: 8, of which 3 were waited for; matrix products, arithmetic and copies ran while one was open for 0% of the time, Pallas kernels for 2%

profile of v7, /device:TPU:0, one launch (start us, length us, event | category | flops | bytes accessed | tf_op | source)
XLA Modules:
  0.0 45.1 jit_solution(4319455102393657233)
XLA Ops:
  0.0 1.1 %pack_rows.1 = (f32[5,8,16,128]{3,2,1,0:T(8,128)S(1)}, f32[408,128]{1,0:T(8,128)S(1)}, f32[408,128]{1,0:T(8,128)S(1)}, f32[256,128]{1,0:T(8,128)S(1)}, f32[256,128]{1,0:T(8,128)S(1)}) custom-call(f32[3,8,16,128]{3,2,1,0:T(8,128)} %forces.1, f32[8,16,128]{2,1,0:T(8,128)} %modulus.1, s32[8,16,128]{2,1,0:T(8,128)} %occupancy.1, s32[8,16,128]{2,1,0:T(8,128)} %bonded.1), custom_call_target="tpu_custom_call" | custom-call | tf_op jit(solution)/shard_map/pack_rows/pallas_call | solution.py:859
  1.1 3.0 %collective-permute-start = (f32[408,128]{1,0:T(8,128)S(1)}, f32[408,128]{1,0:T(8,128)S(1)}, u32[]{:S(2)}, u32[]{:S(2)}) collective-permute-start(f32[408,128]{1,0:T(8,128)S(1)} %get-tuple-element.43), channel_id=1, source_target_pairs={{0,1},{1,0},{2,3},{3,2},{4,5},{5,4},{6,7},{7,6},{8,9},{9,8},{10,11... | collective-permute-start | bytes 626696 | tf_op jit(solution)/shard_map/ppermute | solution.py:843
  4.2 0.7 %collective-permute-start.1 = (f32[408,128]{1,0:T(8,128)S(1)}, f32[408,128]{1,0:T(8,128)S(1)}, u32[]{:S(2)}, u32[]{:S(2)}) collective-permute-start(f32[408,128]{1,0:T(8,128)S(1)} %get-tuple-element.44), channel_id=1, source_target_pairs={{1,2},{2,1},{3,4},{4,3},{5,6},{6,5},{9,10},{10,9},{11,12},{12,11},... | collective-permute-start | bytes 626696 | tf_op jit(solution)/shard_map/ppermute | solution.py:843
  4.8 0.7 %collective-permute-start.2 = (f32[256,128]{1,0:T(8,128)S(1)}, f32[256,128]{1,0:T(8,128)S(1)}, u32[]{:S(2)}, u32[]{:S(2)}) collective-permute-start(f32[256,128]{1,0:T(8,128)S(1)} %get-tuple-element.45), channel_id=1, source_target_pairs={{8,16},{16,8},{9,17},{17,9},{10,18},{18,10},{11,19},{19,11},{12,20... | collective-permute-start | bytes 393224 | tf_op jit(solution)/shard_map/ppermute | solution.py:843
  5.5 2.9 %collective-permute-start.3 = (f32[256,128]{1,0:T(8,128)S(1)}, f32[256,128]{1,0:T(8,128)S(1)}, u32[]{:S(2)}, u32[]{:S(2)}) collective-permute-start(f32[256,128]{1,0:T(8,128)S(1)} %get-tuple-element.46), channel_id=1, source_target_pairs={{0,8},{8,0},{16,24},{24,16},{1,9},{9,1},{17,25},{25,17},{2,10},{10... | collective-permute-start | bytes 393224 | tf_op jit(solution)/shard_map/ppermute | solution.py:843
  8.4 0.0 collective-permute-done.2.middle_b
  8.4 1.0 %collective-permute-done.3.middle_a = f32[256,128]{1,0:T(8,128)S(1)} collective-permute-done((f32[256,128]{1,0:T(8,128)S(1)}, f32[256,128]{1,0:T(8,128)S(1)}, u32[]{:S(2)}, u32[]{:S(2)}) %collective-permute-start.3) | collective-permute-done | bytes 131104 | tf_op jit(solution)/shard_map/ppermute | solution.py:843
  9.4 3.7 %collective-permute-done.from_c = f32[408,128]{1,0:T(8,128)S(1)} collective-permute-done((f32[408,128]{1,0:T(8,128)S(1)}, f32[408,128]{1,0:T(8,128)S(1)}, u32[]{:S(2)}, u32[]{:S(2)}) %collective-permute-start) | collective-permute-done | bytes 208928 | tf_op jit(solution)/shard_map/ppermute | solution.py:843
  13.1 0.0 collective-permute-done.1.from_d
  13.1 0.1 pack_corners.1
  13.1 0.7 %collective-permute-start.4 = (f32[258,128]{1,0:T(8,128)S(1)}, f32[258,128]{1,0:T(8,128)S(1)}, u32[]{:S(2)}, u32[]{:S(2)}) collective-permute-start(f32[258,128]{1,0:T(8,128)S(1)} %get-tuple-element.47.to_a), channel_id=1, source_target_pairs={{8,16},{16,8},{9,17},{17,9},{10,18},{18,10},{11,19},{19,11},{12,20... | collective-permute-start | bytes 396296 | tf_op jit(solution)/shard_map/ppermute | solution.py:843
  13.8 2.9 %collective-permute-start.5 = (f32[258,128]{1,0:T(8,128)S(1)}, f32[258,128]{1,0:T(8,128)S(1)}, u32[]{:S(2)}, u32[]{:S(2)}) collective-permute-start(f32[258,128]{1,0:T(8,128)S(1)} %get-tuple-element.59), channel_id=1, source_target_pairs={{0,8},{8,0},{16,24},{24,16},{1,9},{9,1},{17,25},{25,17},{2,10},{10... | collective-permute-start | bytes 396296 | tf_op jit(solution)/shard_map/ppermute | solution.py:843
  16.7 1.0 %fine_inner.1 = (f32[3,8,40,128]{3,2,1,0:T(8,128)S(1)}, f32[8,40,128]{2,1,0:T(8,128)S(1)}, f32[8,40,128]{2,1,0:T(8,128)S(1)}, f32[6,40,128]{2,1,0:T(8,128)S(1)},...) custom-call(f32[5,8,16,128]{3,2,1,0:T(8,128)S(1)} %get-tuple-element, ...), custom_call_target="tpu_custom_call" | custom-call | flops 10000000 | bytes 4000000 | tf_op jit(solution)/shard_map/fine_inner/pallas_call | solution.py:892
  17.7 0.0 collective-permute-done.4.corner_b
  17.7 0.0 collective-permute-done.5.corner_a
  17.7 1.5 %fine_before.1 = (f32[5,4,16,128]{3,2,1,0:T(8,128)S(1)}, f32[5,2,16,128]{3,2,1,0:T(8,128)S(1)}, f32[3,8,24,128]{3,2,1,0:T(8,128)S(1)}, f32[3,2,24,128]{3,2,1,0:T...) custom-call(f32[3,8,40,128]{3,2,1,0:T(8,128)S(1)} %get-tuple-element.48.source_in, ...), custom_call_target="tpu_custom_call" | custom-call | tf_op jit(solution)/shard_map/fine_before/pallas_call | solution.py:906
  19.2 0.7 %collective-permute-start.6 = (f32[5,2,16,128]{3,2,1,0:T(8,128)S(1)}, f32[5,2,16,128]{3,2,1,0:T(8,128)S(1)}, u32[]{:S(2)}, u32[]{:S(2)}) collective-permute-start(f32[5,2,16,128]{3,2,1,0:T(8,128)S(1)} %get-tuple-element.62), channel_id=1, source_target_pairs={{8,16},{16,8},{9,17},{17,9},{10,18},{18,10},{11,19},{19,11},{12,20... | collective-permute-start | bytes 245768 | tf_op jit(solution)/shard_map/ppermute | solution.py:843
  19.9 4.7 %collective-permute-start.7 = (f32[5,2,16,128]{3,2,1,0:T(8,128)S(1)}, f32[5,2,16,128]{3,2,1,0:T(8,128)S(1)}, u32[]{:S(2)}, u32[]{:S(2)}) collective-permute-start(f32[5,2,16,128]{3,2,1,0:T(8,128)S(1)} %get-tuple-element.62), channel_id=1, source_target_pairs={{0,8},{8,0},{16,24},{24,16},{1,9},{9,1},{17,25},{25,17},{2,10},{10... | collective-permute-start | bytes 245768 | tf_op jit(solution)/shard_map/ppermute | solution.py:843
  24.5 0.0 collective-permute-done.6.from_b
  24.5 0.9 %collective-permute-done.7.from_a = f32[5,2,16,128]{3,2,1,0:T(8,128)S(1)} collective-permute-done((f32[5,2,16,128]{3,2,1,0:T(8,128)S(1)}, f32[5,2,16,128]{3,2,1,0:T(8,128)S(1)}, u32[]{:S(2)}, u32[]{:S(2)}) %collective-permute-start.7) | collective-permute-done | bytes 81952 | tf_op jit(solution)/shard_map/ppermute | solution.py:843
  25.5 0.7 %middle_before.1 = (f32[320,128]{1,0:T(8,128)S(1)}, f32[3,12,16,128]{3,2,1,0:T(8,128)S(1)}, f32[3,12,16,128]{3,2,1,0:T(8,128)S(1)}, f32[12,16,128]{2,1,0:T(8,128...) custom-call(f32[5,4,16,128]{3,2,1,0:T(8,128)S(1)} %get-tuple-element.60.own, ...), custom_call_target="tpu_custom_call" | custom-call | tf_op jit(solution)/shard_map/middle_before/pallas_call | solution.py:919
  26.2 14.8 %all_to_all.5 = f32[160,2,128]{2,1,0:T(2,128)S(1)} all-to-all(f32[160,2,128]{2,1,0:T(2,128)S(1)} %bitcast.3), channel_id=1, replica_groups=mesh['len'=4,'brick'=8] {'len','brick'}, dimensions={0} | all-to-all | bytes 327680 | tf_op jit(solution)/shard_map/all_to_all | solution.py:927
  41.1 4.1 %coarse_and_after.1 = f32[3,8,16,128]{3,2,1,0:T(8,128)} custom-call(f32[320,128]{1,0:T(8,128)S(1)} %bitcast.2, f32[3,12,16,128]{3,2,1,0:T(8,128)S(1)} %get-tuple-element.64.v2_mid, f32[3,12,16,128]{3,2,1,0:T(8,128)S(1)} %get-tuple-element.65.source_mid, f32[12,16,128]{2,1,0:T(8,128)S(1)} %get-tuple-element.66.quarter_mid, ...), custom_call_target="tpu_custom_call" | custom-call | tf_op jit(solution)/shard_map/coarse_and_after/pallas_call | solution.py:939
Async XLA Ops:
  1.1 11.9 %collective-permute-start = (f32[408,128]{1,0:T(8,128)S(1)}, f32[408,128]{1,0:T(8,128)S(1)}, u32[]{:S(2)}, u32[]{:S(2)}) collective-permute-start(f32[408,128]{1,0:T(8,128)S(1)} %get-tuple-element.43), channel_id=1, source_target_pairs={{0,1},{1,0},{2,3},{3,2},{4,5},{5,4},{6,7},{7,6},{8,9},{9,8},{10,11... | collective-permute-start | bytes 626696 | tf_op jit(solution)/shard_map/ppermute | solution.py:843
  4.2 8.9 %collective-permute-start.1 = (f32[408,128]{1,0:T(8,128)S(1)}, f32[408,128]{1,0:T(8,128)S(1)}, u32[]{:S(2)}, u32[]{:S(2)}) collective-permute-start(f32[408,128]{1,0:T(8,128)S(1)} %get-tuple-element.44), channel_id=1, source_target_pairs={{1,2},{2,1},{3,4},{4,3},{5,6},{6,5},{9,10},{10,9},{11,12},{12,11},... | collective-permute-start | bytes 626696 | tf_op jit(solution)/shard_map/ppermute | solution.py:843
  4.8 3.6 %collective-permute-start.2 = (f32[256,128]{1,0:T(8,128)S(1)}, f32[256,128]{1,0:T(8,128)S(1)}, u32[]{:S(2)}, u32[]{:S(2)}) collective-permute-start(f32[256,128]{1,0:T(8,128)S(1)} %get-tuple-element.45), channel_id=1, source_target_pairs={{8,16},{16,8},{9,17},{17,9},{10,18},{18,10},{11,19},{19,11},{12,20... | collective-permute-start | bytes 393224 | tf_op jit(solution)/shard_map/ppermute | solution.py:843
  5.5 3.9 %collective-permute-start.3 = (f32[256,128]{1,0:T(8,128)S(1)}, f32[256,128]{1,0:T(8,128)S(1)}, u32[]{:S(2)}, u32[]{:S(2)}) collective-permute-start(f32[256,128]{1,0:T(8,128)S(1)} %get-tuple-element.46), channel_id=1, source_target_pairs={{0,8},{8,0},{16,24},{24,16},{1,9},{9,1},{17,25},{25,17},{2,10},{10... | collective-permute-start | bytes 393224 | tf_op jit(solution)/shard_map/ppermute | solution.py:843
  13.1 4.6 %collective-permute-start.4 = (f32[258,128]{1,0:T(8,128)S(1)}, f32[258,128]{1,0:T(8,128)S(1)}, u32[]{:S(2)}, u32[]{:S(2)}) collective-permute-start(f32[258,128]{1,0:T(8,128)S(1)} %get-tuple-element.47.to_a), channel_id=1, source_target_pairs={{8,16},{16,8},{9,17},{17,9},{10,18},{18,10},{11,19},{19,11},{12,20... | collective-permute-start | bytes 396296 | tf_op jit(solution)/shard_map/ppermute | solution.py:843
  13.8 3.9 %collective-permute-start.5 = (f32[258,128]{1,0:T(8,128)S(1)}, f32[258,128]{1,0:T(8,128)S(1)}, u32[]{:S(2)}, u32[]{:S(2)}) collective-permute-start(f32[258,128]{1,0:T(8,128)S(1)} %get-tuple-element.59), channel_id=1, source_target_pairs={{0,8},{8,0},{16,24},{24,16},{1,9},{9,1},{17,25},{25,17},{2,10},{10... | collective-permute-start | bytes 396296 | tf_op jit(solution)/shard_map/ppermute | solution.py:843
  19.2 5.3 %collective-permute-start.6 = (f32[5,2,16,128]{3,2,1,0:T(8,128)S(1)}, f32[5,2,16,128]{3,2,1,0:T(8,128)S(1)}, u32[]{:S(2)}, u32[]{:S(2)}) collective-permute-start(f32[5,2,16,128]{3,2,1,0:T(8,128)S(1)} %get-tuple-element.62), channel_id=1, source_target_pairs={{8,16},{16,8},{9,17},{17,9},{10,18},{18,10},{11,19},{19,11},{12,20... | collective-permute-start | bytes 245768 | tf_op jit(solution)/shard_map/ppermute | solution.py:843
  19.9 5.6 %collective-permute-start.7 = (f32[5,2,16,128]{3,2,1,0:T(8,128)S(1)}, f32[5,2,16,128]{3,2,1,0:T(8,128)S(1)}, u32[]{:S(2)}, u32[]{:S(2)}) collective-permute-start(f32[5,2,16,128]{3,2,1,0:T(8,128)S(1)} %get-tuple-element.62), channel_id=1, source_target_pairs={{0,8},{8,0},{16,24},{24,16},{1,9},{9,1},{17,25},{25,17},{2,10},{10... | collective-permute-start | bytes 245768 | tf_op jit(solution)/shard_map/ppermute | solution.py:843

commit v8 on v6

--- a/solution.py
+++ b/solution.py
@@ -208,7 +208,7 @@
             put(k, p, v[k] + s * r[k])
 
 
-def sweep_rows(field, quarter, weight, step, source, planes, rows, lane, put):
+def sweep_rows(field, quarter, weight, step, source, planes, rows, lane, put, beside_at):
     near = [slice(rows.start + by, rows.stop + by) for by in (-1, 0, 1)]
     q_at = remember(lambda p: [quarter.cut(p, r) for r in near])
     v_at = [remember(lambda p, k=k: [field(k, p, r) for r in near]) for k in range(3)]
@@ -226,7 +226,7 @@
     ]
     for p in planes:
         q = q_at(p)[1]
-        beside = lane.beside(q)
+        beside = beside_at(p)
         v = [x(p)[1] for x in v_at]
         coupled = (4.0 * COUPLING) * q * (v[0] + v[1] + v[2])
         e, s = weight.cut(p, rows), step.cut(p, rows)
@@ -470,7 +470,7 @@
         for k in range(3):
             rest[k, p - left[0]] = r[k]
 
-    *kept, work = more
+    *kept, q_before, q_after, work = more
     half = rows // 2 + 2 * HALO
     outer = slice(WIDE - 2 * HALO, WIDE + rows + 2 * HALO)
     beyond = slice(outer.start - 2, outer.stop + 2)
@@ -489,6 +489,11 @@
         s = shift1[i]
         w = coarse_weight(lane1, lambda j: coarse_q.at[j], i, half)
         sums[i - 1] = jnp.where(s > 0.0, w + s, 0.0)
+
+    for i in range(planes):
+        rolled = lane.beside(quarter[i])
+        for target, x in zip((q_before, q_after), rolled):
+            target[i] = x[WIDE - HALO : WIDE + rows + HALO]
 
     inner = slice(HALO, HALO + rows // 2)
     for i in range(count // 2):
@@ -721,7 +726,7 @@
     table, v2_mid, source_mid, quarter_mid, weight_mid, step_mid, *more,
 ):
     kept_inner, kept_outer = more[:5], more[5:10]
-    out, wide2, u_mid, x_mid, u_fine, x_fine = more[10:]
+    q_before, q_after, out, wide2, u_mid, x_mid, u_fine, x_fine = more[10:]
     brick = lax.axis_index("brick")
     slab = lax.axis_index("len")
     bricks, planes2 = wide2.shape[2] - 16, wide2.shape[1] - 4
@@ -806,7 +811,10 @@
 
     planes0, rows0 = x_fine.shape[1], x_fine.shape[2]
     lane0 = Lane(rows0, 1)
-    bounds0, beside0 = (0, planes0), {}
+    bounds0 = (0, planes0)
+    beside0 = {
+        i + HALO: (q_before[i], q_after[i]) for i in range(planes0 - 2 * HALO)
+    }
     half_rows = rows0 // 2
     for k in range(3):
         for i in range(3, planes1 - 3):
@@ -833,6 +841,7 @@
     sweep_rows(
         lambda k, p, r: x_fine[k, p, r, :], quarter_fine, weight_fine, step_fine, source_fine,
         range(HALO, planes0 - HALO), own_rows, Lane(rows0 - 2 * HALO, 1), put_out,
+        lambda p: (q_before[p - HALO, own_rows, :], q_after[p - HALO, own_rows, :]),
     )
 
 
@@ -907,14 +916,15 @@
         + [(3,) + weighed, (3,) + swept, (3,) + left]
         + [coarse, (half, mid_rows, LANES), (half - 2, mid_rows, LANES)]
         + [(2, half // 2, half_rows // 2, LANES)]
-        + kept_inner,
+        + kept_inner
+        + [(planes,) + line] * 2,
         [(2, half, ext_rows, LANES)],
         name="fine_inner",
         in_specs=[pl.BlockSpec(memory_space=pltpu.VMEM)] * 3
         + [pl.BlockSpec(memory_space=pl.ANY)],
         cost_estimate=pl.CostEstimate(flops=10**7, bytes_accessed=4 * 10**6, transcendentals=0),
     )(own, from_c, from_d, to_b)
-    inner, cells, kept_inner = inner[:11], inner[11], inner[12:]
+    inner, cells, kept_inner, rolled = inner[:11], inner[11], inner[12:17], inner[17:]
     own, to_len, *kept_outer = call(
         fine_before,
         [(5, half, mid_rows, LANES), (5, half // 2, mid_rows, LANES)] + kept_outer,
@@ -954,7 +964,7 @@
         [(3, planes2 + 4, window + 16, LANES), field1, field1]
         + [(3, ext, rows + 2 * HALO, LANES)] * 2,
         name="coarse_and_after",
-    )(table, *middle, *kept_inner, *kept_outer)
+    )(table, *middle, *kept_inner, *kept_outer, *rolled)
     return out
 
 

time: 45.4 us -> 45.4 us (level)
  no operation moved by 1% of the time
where the time goes in v8:
time: 45.4 us; the launch traced here: 45.2 us
  starting transfers between devices  16.2 us (36%)
  blocking collectives  14.8 us (33%)
  Pallas kernels  8.51 us (19%)
  waiting for transfers between devices  5.58 us (12%)
    ppermute x8, starting transfers between devices, swap(): return lax.ppermute(x, axis, pairs)  16.2 us
    all_to_all x1, blocking collectives, body(): table = lax.all_to_all(to_all, BOTH, 0, 0, tiled=True).reshape(-1, LANES)  14.8 us
    ppermute x8, waiting for transfers between devices, swap(): return lax.ppermute(x, axis, pairs)  5.58 us
    pallas_call x1, Pallas kernels, body(): call(functools.partial(coarse_and_after, first_brick), [forces.shape], [(...  4.09 us
    pallas_call x1, Pallas kernels, body(): call(fine_before, [(5, half, mid_rows, LANES), (5, half // 2, mid_rows, L...  1.53 us
    pallas_call x1, Pallas kernels, body(): call(pack_rows, [(5,) + block, side, side, middle_side, middle_side], [bl...  1.12 us
    pallas_call x1, Pallas kernels, body(): call(fine_inner, [(3,) + block, block, block, weighed, weighed] + [(3,) +...  0.97 us
  transfers between devices with their start and end apart: 8, of which 3 were waited for; matrix products, arithmetic and copies ran while one was open for 0% of the time, Pallas kernels for 2%

profile of v8, /device:TPU:0, one launch (start us, length us, event | category | flops | bytes accessed | tf_op | source)
XLA Modules:
  0.0 45.2 jit_solution(15467364614557315)
XLA Ops:
  0.0 1.1 %pack_rows.1 = (f32[5,8,16,128]{3,2,1,0:T(8,128)S(1)}, f32[408,128]{1,0:T(8,128)S(1)}, f32[408,128]{1,0:T(8,128)S(1)}, f32[256,128]{1,0:T(8,128)S(1)}, f32[256,128]{1,0:T(8,128)S(1)}) custom-call(f32[3,8,16,128]{3,2,1,0:T(8,128)} %forces.1, f32[8,16,128]{2,1,0:T(8,128)} %modulus.1, s32[8,16,128]{2,1,0:T(8,128)} %occupancy.1, s32[8,16,128]{2,1,0:T(8,128)} %bonded.1), custom_call_target="tpu_custom_call" | custom-call | tf_op jit(solution)/shard_map/pack_rows/pallas_call | solution.py:880
  1.1 3.0 %collective-permute-start = (f32[408,128]{1,0:T(8,128)S(1)}, f32[408,128]{1,0:T(8,128)S(1)}, u32[]{:S(2)}, u32[]{:S(2)}) collective-permute-start(f32[408,128]{1,0:T(8,128)S(1)} %get-tuple-element.45), channel_id=1, source_target_pairs={{0,1},{1,0},{2,3},{3,2},{4,5},{5,4},{6,7},{7,6},{8,9},{9,8},{10,11... | collective-permute-start | bytes 626696 | tf_op jit(solution)/shard_map/ppermute | solution.py:864
  4.2 0.7 %collective-permute-start.1 = (f32[408,128]{1,0:T(8,128)S(1)}, f32[408,128]{1,0:T(8,128)S(1)}, u32[]{:S(2)}, u32[]{:S(2)}) collective-permute-start(f32[408,128]{1,0:T(8,128)S(1)} %get-tuple-element.46), channel_id=1, source_target_pairs={{1,2},{2,1},{3,4},{4,3},{5,6},{6,5},{9,10},{10,9},{11,12},{12,11},... | collective-permute-start | bytes 626696 | tf_op jit(solution)/shard_map/ppermute | solution.py:864
  4.8 0.7 %collective-permute-start.2 = (f32[256,128]{1,0:T(8,128)S(1)}, f32[256,128]{1,0:T(8,128)S(1)}, u32[]{:S(2)}, u32[]{:S(2)}) collective-permute-start(f32[256,128]{1,0:T(8,128)S(1)} %get-tuple-element.47), channel_id=1, source_target_pairs={{8,16},{16,8},{9,17},{17,9},{10,18},{18,10},{11,19},{19,11},{12,20... | collective-permute-start | bytes 393224 | tf_op jit(solution)/shard_map/ppermute | solution.py:864
  5.5 2.9 %collective-permute-start.3 = (f32[256,128]{1,0:T(8,128)S(1)}, f32[256,128]{1,0:T(8,128)S(1)}, u32[]{:S(2)}, u32[]{:S(2)}) collective-permute-start(f32[256,128]{1,0:T(8,128)S(1)} %get-tuple-element.48), channel_id=1, source_target_pairs={{0,8},{8,0},{16,24},{24,16},{1,9},{9,1},{17,25},{25,17},{2,10},{10... | collective-permute-start | bytes 393224 | tf_op jit(solution)/shard_map/ppermute | solution.py:864
  8.4 0.0 collective-permute-done.2.middle_b
  8.4 1.0 %collective-permute-done.3.middle_a = f32[256,128]{1,0:T(8,128)S(1)} collective-permute-done((f32[256,128]{1,0:T(8,128)S(1)}, f32[256,128]{1,0:T(8,128)S(1)}, u32[]{:S(2)}, u32[]{:S(2)}) %collective-permute-start.3) | collective-permute-done | bytes 131104 | tf_op jit(solution)/shard_map/ppermute | solution.py:864
  9.4 3.7 %collective-permute-done.from_c = f32[408,128]{1,0:T(8,128)S(1)} collective-permute-done((f32[408,128]{1,0:T(8,128)S(1)}, f32[408,128]{1,0:T(8,128)S(1)}, u32[]{:S(2)}, u32[]{:S(2)}) %collective-permute-start) | collective-permute-done | bytes 208928 | tf_op jit(solution)/shard_map/ppermute | solution.py:864
  13.1 0.0 collective-permute-done.1.from_d
  13.1 0.1 pack_corners.1
  13.1 0.7 %collective-permute-start.4 = (f32[258,128]{1,0:T(8,128)S(1)}, f32[258,128]{1,0:T(8,128)S(1)}, u32[]{:S(2)}, u32[]{:S(2)}) collective-permute-start(f32[258,128]{1,0:T(8,128)S(1)} %get-tuple-element.49.to_a), channel_id=1, source_target_pairs={{8,16},{16,8},{9,17},{17,9},{10,18},{18,10},{11,19},{19,11},{12,20... | collective-permute-start | bytes 396296 | tf_op jit(solution)/shard_map/ppermute | solution.py:864
  13.8 2.9 %collective-permute-start.5 = (f32[258,128]{1,0:T(8,128)S(1)}, f32[258,128]{1,0:T(8,128)S(1)}, u32[]{:S(2)}, u32[]{:S(2)}) collective-permute-start(f32[258,128]{1,0:T(8,128)S(1)} %get-tuple-element.61), channel_id=1, source_target_pairs={{0,8},{8,0},{16,24},{24,16},{1,9},{9,1},{17,25},{25,17},{2,10},{10... | collective-permute-start | bytes 396296 | tf_op jit(solution)/shard_map/ppermute | solution.py:864
  16.7 1.0 %fine_inner.1 = (f32[3,8,40,128]{3,2,1,0:T(8,128)S(1)}, f32[8,40,128]{2,1,0:T(8,128)S(1)}, f32[8,40,128]{2,1,0:T(8,128)S(1)}, f32[6,40,128]{2,1,0:T(8,128)S(1)},...) custom-call(f32[5,8,16,128]{3,2,1,0:T(8,128)S(1)} %get-tuple-element, ...), custom_call_target="tpu_custom_call" | custom-call | flops 10000000 | bytes 4000000 | tf_op jit(solution)/shard_map/fine_inner/pallas_call | solution.py:913
  17.7 0.0 collective-permute-done.4.corner_b
  17.7 0.0 collective-permute-done.5.corner_a
  17.7 1.5 %fine_before.1 = (f32[5,4,16,128]{3,2,1,0:T(8,128)S(1)}, f32[5,2,16,128]{3,2,1,0:T(8,128)S(1)}, f32[3,8,24,128]{3,2,1,0:T(8,128)S(1)}, f32[3,2,24,128]{3,2,1,0:T...) custom-call(f32[3,8,40,128]{3,2,1,0:T(8,128)S(1)} %get-tuple-element.50.source_in, ...), custom_call_target="tpu_custom_call" | custom-call | tf_op jit(solution)/shard_map/fine_before/pallas_call | solution.py:928
  19.2 0.7 %collective-permute-start.6 = (f32[5,2,16,128]{3,2,1,0:T(8,128)S(1)}, f32[5,2,16,128]{3,2,1,0:T(8,128)S(1)}, u32[]{:S(2)}, u32[]{:S(2)}) collective-permute-start(f32[5,2,16,128]{3,2,1,0:T(8,128)S(1)} %get-tuple-element.64), channel_id=1, source_target_pairs={{8,16},{16,8},{9,17},{17,9},{10,18},{18,10},{11,19},{19,11},{12,20... | collective-permute-start | bytes 245768 | tf_op jit(solution)/shard_map/ppermute | solution.py:864
  19.9 4.7 %collective-permute-start.7 = (f32[5,2,16,128]{3,2,1,0:T(8,128)S(1)}, f32[5,2,16,128]{3,2,1,0:T(8,128)S(1)}, u32[]{:S(2)}, u32[]{:S(2)}) collective-permute-start(f32[5,2,16,128]{3,2,1,0:T(8,128)S(1)} %get-tuple-element.64), channel_id=1, source_target_pairs={{0,8},{8,0},{16,24},{24,16},{1,9},{9,1},{17,25},{25,17},{2,10},{10... | collective-permute-start | bytes 245768 | tf_op jit(solution)/shard_map/ppermute | solution.py:864
  24.6 0.0 collective-permute-done.6.from_b
  24.6 0.9 %collective-permute-done.7.from_a = f32[5,2,16,128]{3,2,1,0:T(8,128)S(1)} collective-permute-done((f32[5,2,16,128]{3,2,1,0:T(8,128)S(1)}, f32[5,2,16,128]{3,2,1,0:T(8,128)S(1)}, u32[]{:S(2)}, u32[]{:S(2)}) %collective-permute-start.7) | collective-permute-done | bytes 81952 | tf_op jit(solution)/shard_map/ppermute | solution.py:864
  25.5 0.8 %middle_before.1 = (f32[320,128]{1,0:T(8,128)S(1)}, f32[3,12,16,128]{3,2,1,0:T(8,128)S(1)}, f32[3,12,16,128]{3,2,1,0:T(8,128)S(1)}, f32[12,16,128]{2,1,0:T(8,128...) custom-call(f32[5,4,16,128]{3,2,1,0:T(8,128)S(1)} %get-tuple-element.62.own, ...), custom_call_target="tpu_custom_call" | custom-call | tf_op jit(solution)/shard_map/middle_before/pallas_call | solution.py:941
  26.2 14.8 %all_to_all.5 = f32[160,2,128]{2,1,0:T(2,128)S(1)} all-to-all(f32[160,2,128]{2,1,0:T(2,128)S(1)} %bitcast.3), channel_id=1, replica_groups=mesh['len'=4,'brick'=8] {'len','brick'}, dimensions={0} | all-to-all | bytes 327680 | tf_op jit(solution)/shard_map/all_to_all | solution.py:949
  41.1 4.1 %coarse_and_after.1 = f32[3,8,16,128]{3,2,1,0:T(8,128)} custom-call(f32[320,128]{1,0:T(8,128)S(1)} %bitcast.2, f32[3,12,16,128]{3,2,1,0:T(8,128)S(1)} %get-tuple-element.66.v2_mid, f32[3,12,16,128]{3,2,1,0:T(8,128)S(1)} %get-tuple-element.67.source_mid, f32[12,16,128]{2,1,0:T(8,128)S(1)} %get-tuple-element.68.quarter_mid, ...), custom_call_target="tpu_custom_call" | custom-call | tf_op jit(solution)/shard_map/coarse_and_after/pallas_call | solution.py:961
Async XLA Ops:
  1.1 11.9 %collective-permute-start = (f32[408,128]{1,0:T(8,128)S(1)}, f32[408,128]{1,0:T(8,128)S(1)}, u32[]{:S(2)}, u32[]{:S(2)}) collective-permute-start(f32[408,128]{1,0:T(8,128)S(1)} %get-tuple-element.45), channel_id=1, source_target_pairs={{0,1},{1,0},{2,3},{3,2},{4,5},{5,4},{6,7},{7,6},{8,9},{9,8},{10,11... | collective-permute-start | bytes 626696 | tf_op jit(solution)/shard_map/ppermute | solution.py:864
  4.2 8.9 %collective-permute-start.1 = (f32[408,128]{1,0:T(8,128)S(1)}, f32[408,128]{1,0:T(8,128)S(1)}, u32[]{:S(2)}, u32[]{:S(2)}) collective-permute-start(f32[408,128]{1,0:T(8,128)S(1)} %get-tuple-element.46), channel_id=1, source_target_pairs={{1,2},{2,1},{3,4},{4,3},{5,6},{6,5},{9,10},{10,9},{11,12},{12,11},... | collective-permute-start | bytes 626696 | tf_op jit(solution)/shard_map/ppermute | solution.py:864
  4.8 3.6 %collective-permute-start.2 = (f32[256,128]{1,0:T(8,128)S(1)}, f32[256,128]{1,0:T(8,128)S(1)}, u32[]{:S(2)}, u32[]{:S(2)}) collective-permute-start(f32[256,128]{1,0:T(8,128)S(1)} %get-tuple-element.47), channel_id=1, source_target_pairs={{8,16},{16,8},{9,17},{17,9},{10,18},{18,10},{11,19},{19,11},{12,20... | collective-permute-start | bytes 393224 | tf_op jit(solution)/shard_map/ppermute | solution.py:864
  5.5 3.9 %collective-permute-start.3 = (f32[256,128]{1,0:T(8,128)S(1)}, f32[256,128]{1,0:T(8,128)S(1)}, u32[]{:S(2)}, u32[]{:S(2)}) collective-permute-start(f32[256,128]{1,0:T(8,128)S(1)} %get-tuple-element.48), channel_id=1, source_target_pairs={{0,8},{8,0},{16,24},{24,16},{1,9},{9,1},{17,25},{25,17},{2,10},{10... | collective-permute-start | bytes 393224 | tf_op jit(solution)/shard_map/ppermute | solution.py:864
  13.1 4.6 %collective-permute-start.4 = (f32[258,128]{1,0:T(8,128)S(1)}, f32[258,128]{1,0:T(8,128)S(1)}, u32[]{:S(2)}, u32[]{:S(2)}) collective-permute-start(f32[258,128]{1,0:T(8,128)S(1)} %get-tuple-element.49.to_a), channel_id=1, source_target_pairs={{8,16},{16,8},{9,17},{17,9},{10,18},{18,10},{11,19},{19,11},{12,20... | collective-permute-start | bytes 396296 | tf_op jit(solution)/shard_map/ppermute | solution.py:864
  13.8 3.9 %collective-permute-start.5 = (f32[258,128]{1,0:T(8,128)S(1)}, f32[258,128]{1,0:T(8,128)S(1)}, u32[]{:S(2)}, u32[]{:S(2)}) collective-permute-start(f32[258,128]{1,0:T(8,128)S(1)} %get-tuple-element.61), channel_id=1, source_target_pairs={{0,8},{8,0},{16,24},{24,16},{1,9},{9,1},{17,25},{25,17},{2,10},{10... | collective-permute-start | bytes 396296 | tf_op jit(solution)/shard_map/ppermute | solution.py:864
  19.2 5.3 %collective-permute-start.6 = (f32[5,2,16,128]{3,2,1,0:T(8,128)S(1)}, f32[5,2,16,128]{3,2,1,0:T(8,128)S(1)}, u32[]{:S(2)}, u32[]{:S(2)}) collective-permute-start(f32[5,2,16,128]{3,2,1,0:T(8,128)S(1)} %get-tuple-element.64), channel_id=1, source_target_pairs={{8,16},{16,8},{9,17},{17,9},{10,18},{18,10},{11,19},{19,11},{12,20... | collective-permute-start | bytes 245768 | tf_op jit(solution)/shard_map/ppermute | solution.py:864
  19.9 5.6 %collective-permute-start.7 = (f32[5,2,16,128]{3,2,1,0:T(8,128)S(1)}, f32[5,2,16,128]{3,2,1,0:T(8,128)S(1)}, u32[]{:S(2)}, u32[]{:S(2)}) collective-permute-start(f32[5,2,16,128]{3,2,1,0:T(8,128)S(1)} %get-tuple-element.64), channel_id=1, source_target_pairs={{0,8},{8,0},{16,24},{24,16},{1,9},{9,1},{17,25},{25,17},{2,10},{10... | collective-permute-start | bytes 245768 | tf_op jit(solution)/shard_map/ppermute | solution.py:864
